TPU v7x, 512 devices: a whole 4x4x16 slice. The times are simulated.
512 devices in a mesh: section: 32 (over z, x_lo), tensor: 16 (over x_hi, y, core).
Axes of the slice: x: 4 (x_hi: 2, x_lo: 2; x = x_hi * 2 + x_lo), y: 4, z: 16, core: 2. Of those that a mesh axis runs over, the one named last changes fastest.
Arguments:
- inputs: bfloat16 [32, 256, 2048], P('section', None, 'tensor'), may hold values from -6 to 6
- out_grads: bfloat16 [32, 256, 2048], P('section', None, 'tensor'), may hold values from -1.5 to 1.5
- parked_store: bfloat16 [32, 2, 256, 2048], P('section', None, None, 'tensor'), may hold values from -6 to 6
- fetch_slot: int32 [32], P('section'), may hold values from 0 to 1
- norm_gain: float32 [32, 2048], P('section'), may hold values from 0.5 to 1.5
- weight_in: bfloat16 [32, 2048, 4096], P('section', None, 'tensor'), may hold values from -0.125 to 0.125
- weight_out: bfloat16 [32, 4096, 2048], P('section', 'tensor'), may hold values from -0.09375 to 0.09375
Outputs:
- arrivals: bfloat16 [32, 256, 2048], P('section', None, 'tensor')
- sent_grads: bfloat16 [32, 256, 2048], P('section', None, 'tensor')
- parked: bfloat16 [32, 256, 2048], P('section', None, 'tensor')
- weight_in_grad: bfloat16 [32, 2048, 4096], P('section', None, 'tensor')
- weight_out_grad: bfloat16 [32, 4096, 2048], P('section', 'tensor')
All inputs are finite; a program needn't handle non-finite values.
Results may differ from a plain program's by a relative error of at most 0.014.
Values may be sent and summed in bfloat16 or wider, within the bound.
No kernel may reach another device: no remote copies, remote signals or barrier semaphores. Data moves between devices by JAX's collectives and lax.ppermute only.
A program may use at most 64 MiB of HBM per device.

v0:
```python
import jax
import jax.numpy as jnp
from jax import lax
from jax.sharding import PartitionSpec as P

EPSILON = 1e-05
GELU_ROOT = 0.7978845608028654
GELU_CUBIC = 0.044715


def from_partner(value, axis, apart):
    mask = 2**apart
    pairs = [(source, source ^ mask) for source in range(lax.axis_size(axis))]
    return lax.ppermute(value, axis, pairs)


def shifted(block, axis, distance):
    devices = range(lax.axis_size(axis))
    route = [(i - distance, i) for i in devices if i - distance in devices]
    return lax.ppermute(block, axis, route)


def gelu_value(values):
    inner = GELU_ROOT * (values + GELU_CUBIC * values * values * values)
    return 0.5 * values * (1.0 + jnp.tanh(inner))


def gelu_slope(values):
    inner = GELU_ROOT * (values + GELU_CUBIC * values * values * values)
    tangent = jnp.tanh(inner)
    return 0.5 * (1.0 + tangent) + 0.5 * values * (1.0 - tangent * tangent) * GELU_ROOT * (
        1.0 + 3.0 * GELU_CUBIC * values * values
    )


def moments_scale(total, squares, full_width):
    center = total / full_width
    scale = lax.rsqrt(squares / full_width - center * center + EPSILON)
    return (center, scale)


def per_device(inputs, out_grads, parked_store, fetch_slot, norm_gain, weight_in, weight_out):
    forward_in = inputs[0]
    grad_out = out_grads[0]
    gain_row = norm_gain[0]
    weight_a = weight_in[0]
    weight_b = weight_out[0]
    shard_cols = forward_in.shape[1]
    full_width = shard_cols * lax.axis_size("tensor")
    offset = lax.axis_index("tensor") * shard_cols
    gain_part = lax.dynamic_slice_in_dim(gain_row, offset, shard_cols, 0)
    returned = lax.dynamic_index_in_dim(parked_store[0], fetch_slot[0], 0, keepdims=False)
    bit_count = lax.axis_size("section").bit_length() - 1
    hop_list = list(range(bit_count))
    parked = forward_in
    for section_bit in hop_list:
        parked = from_partner(parked, "section", section_bit)
    forward_f = forward_in.astype(jnp.float32)
    total, squares = lax.psum(
        (jnp.sum(forward_f, axis=1), jnp.sum(forward_f * forward_f, axis=1)), "tensor"
    )
    center, scale = moments_scale(total, squares, full_width)
    normed_part = ((forward_f - center[:, None]) * scale[:, None] * gain_part[None, :]).astype(
        jnp.bfloat16
    )
    pre = jnp.dot(
        lax.all_gather(normed_part, "tensor", axis=1, tiled=True),
        weight_a,
        preferred_element_type=jnp.float32,
    )
    act = gelu_value(pre).astype(jnp.bfloat16)
    branch_term = jnp.dot(act, weight_b, preferred_element_type=jnp.float32)
    branch = lax.psum_scatter(
        branch_term.astype(jnp.bfloat16), "tensor", scatter_dimension=1, tiled=True
    ).astype(jnp.float32)
    outputs = (forward_in.astype(jnp.float32) + branch).astype(jnp.bfloat16)
    arrivals = shifted(outputs, "section", 1)
    fetched = returned
    for section_bit in hop_list:
        fetched = from_partner(fetched, "section", section_bit)
    back_f = fetched.astype(jnp.float32)
    back_total, back_squares = lax.psum(
        (jnp.sum(back_f, axis=1), jnp.sum(back_f * back_f, axis=1)), "tensor"
    )
    back_center, back_scale = moments_scale(back_total, back_squares, full_width)
    hidden = (back_f - back_center[:, None]) * back_scale[:, None]
    back_part = (hidden * gain_part[None, :]).astype(jnp.bfloat16)
    back_normed = lax.all_gather(back_part, "tensor", axis=1, tiled=True)
    back_pre = jnp.dot(back_normed, weight_a, preferred_element_type=jnp.float32)
    back_act = gelu_value(back_pre).astype(jnp.bfloat16)
    grad_full = lax.all_gather(grad_out, "tensor", axis=1, tiled=True)
    act_grad = lax.dot_general(
        grad_full, weight_b, (((1,), (1,)), ((), ())), preferred_element_type=jnp.float32
    )
    pre_grad = (act_grad * gelu_slope(back_pre)).astype(jnp.bfloat16)
    normed_term = lax.dot_general(
        pre_grad, weight_a, (((1,), (1,)), ((), ())), preferred_element_type=jnp.float32
    )
    normed_grad = lax.psum_scatter(
        normed_term.astype(jnp.bfloat16), "tensor", scatter_dimension=1, tiled=True
    ).astype(jnp.float32)
    scaled_grad = normed_grad * gain_part[None, :]
    plain_sum, moment_sum = lax.psum(
        (jnp.sum(scaled_grad, axis=1), jnp.sum(scaled_grad * hidden, axis=1)), "tensor"
    )
    plain_mean = plain_sum / full_width
    moment_mean = moment_sum / full_width
    input_grad = (
        grad_out.astype(jnp.float32)
        + back_scale[:, None] * (scaled_grad - plain_mean[:, None] - hidden * moment_mean[:, None])
    ).astype(jnp.bfloat16)
    sent_grads = shifted(input_grad, "section", -1)
    grad_a = lax.dot_general(
        back_normed, pre_grad, (((0,), (0,)), ((), ())), preferred_element_type=jnp.float32
    ).astype(jnp.bfloat16)
    grad_b = lax.dot_general(
        back_act, grad_full, (((0,), (0,)), ((), ())), preferred_element_type=jnp.float32
    ).astype(jnp.bfloat16)
    return (arrivals[None], sent_grads[None], parked[None], grad_a[None], grad_b[None])


def solution(mesh):
    return jax.shard_map(
        per_device,
        mesh=mesh,
        in_specs=(
            P("section", None, "tensor"),
            P("section", None, "tensor"),
            P("section", None, None, "tensor"),
            P("section"),
            P("section", None),
            P("section", None, "tensor"),
            P("section", "tensor", None),
        ),
        out_specs=(
            P("section", None, "tensor"),
            P("section", None, "tensor"),
            P("section", None, "tensor"),
            P("section", None, "tensor"),
            P("section", "tensor", None),
        ),
        check_vma=False,
    )
```

profile of v0, /device:TPU:40, one launch (start us, length us, event | category | flops | bytes accessed | tf_op | source)
XLA Modules:
  0.0 511.2 jit_solution(3884165083200587636)
XLA Ops:
  8.0 0.8 dynamic-slice_bitcast_fusion
  8.8 3.4 collective-permute-start.1
  12.2 2.8 collective-permute-done.1
  15.0 2.0 collective-permute-start.2
  17.0 4.1 collective-permute-done.2
  21.1 5.2 %collective-permute-start.3 = (bf16[256,128]{1,0:T(8,128)(2,1)S(1)}, bf16[256,128]{1,0:T(8,128)(2,1)S(1)}, u32[]{:S(2)}, u32[]{:S(2)}) collective-permute-start(bf16[256,128]{1,0:T(8,128)(2,1)S(1)} %collective-permute-done.2), channel_id=1, source_target_pairs={{0,64},{16,80},{32,96},{48,112},{64,0},{80,16},{96,32},{112,48},{1... | collective-permute-start | bytes 196616 | tf_op jit(solution)/shard_map/ppermute | solution.py:14
  26.3 2.2 collective-permute-done.3
  28.5 9.1 %collective-permute-start.4 = (bf16[256,128]{1,0:T(8,128)(2,1)S(1)}, bf16[256,128]{1,0:T(8,128)(2,1)S(1)}, u32[]{:S(2)}, u32[]{:S(2)}) collective-permute-start(bf16[256,128]{1,0:T(8,128)(2,1)S(1)} %collective-permute-done.3), channel_id=1, source_target_pairs={{0,128},{16,144},{32,160},{48,176},{64,192},{80,208},{96,224},{112... | collective-permute-start | bytes 196616 | tf_op jit(solution)/shard_map/ppermute | solution.py:14
  37.6 2.2 collective-permute-done.4
  39.8 14.1 %collective-permute-start.5 = (bf16[256,128]{1,0:T(8,128)(2,1)S(1)}, bf16[256,128]{1,0:T(8,128)(2,1)S(1)}, u32[]{:S(2)}, u32[]{:S(2)}) collective-permute-start(bf16[256,128]{1,0:T(8,128)(2,1)S(1)} %collective-permute-done.4), channel_id=1, source_target_pairs={{0,256},{16,272},{32,288},{48,304},{64,320},{80,336},{96,352},{112... | collective-permute-start | bytes 196616 | tf_op jit(solution)/shard_map/ppermute | solution.py:14
  53.9 0.7 dynamic-slice_bitcast_fusion.1
  54.6 3.0 collective-permute-done.5
  57.7 29.3 %all-reduce.1 = (f32[256]{0:T(256)S(1)}, f32[256]{0:T(256)S(1)}) all-reduce(f32[256]{0:T(256)S(1)} %get-tuple-element.8, f32[256]{0:T(256)S(1)} %get-tuple-element.7), channel_id=1, replica_groups=mesh['section'=32,'tensor'=16] {'tensor'}, use_global_device_ids=true, to_apply=%region_8.9 | all-reduce | flops 512 | bytes 4096 | tf_op jit(solution)/shard_map/psum | solution.py:82
  87.0 0.8 fusion.31
  87.8 0.7 all-gather.9.cloned.1.call-update
  88.6 59.7 %all-gather.7.cloned.1.call-done = bf16[256,2048]{1,0:T(8,128)(2,1)} async-done(((bf16[256,128]{1,0:T(8,128)(2,1)}), bf16[256,2048]{1,0:T(8,128)(2,1)}) %all-gather.7.cloned.1.call-update) | async-done | bytes 1048592 | tf_op jit(solution)/shard_map/all_gather | solution.py:88
  148.3 1.7 fusion.8
  150.0 59.7 %all-gather.9.cloned.1.call-done = bf16[1,256,2048]{2,1,0:T(8,128)(2,1)} async-done(((bf16[1,256,128]{2,1,0:T(8,128)(2,1)}), bf16[1,256,2048]{2,1,0:T(8,128)(2,1)}) %all-gather.9.cloned.1.call-update) | async-done | bytes 1048592 | tf_op jit(solution)/shard_map/all_gather | solution.py:91
  209.7 1.7 fusion.2
  211.4 0.7 copy-done.5
  212.6 1.3 copy.14
  214.0 0.8 copy-done.4
  214.9 91.1 %reduce-scatter.9.cloned.1.call-done = bf16[128,256]{1,0:T(8,128)(2,1)} async-done(((bf16[2048,256]{1,0:T(8,128)(2,1)}), bf16[128,256]{1,0:T(8,128)(2,1)}) %reduce-scatter.9.cloned.1.call-update) | async-done | bytes 65552
  306.0 0.9 copy.15
  307.2 28.3 %all-reduce = (f32[256]{0:T(256)S(1)}, f32[256]{0:T(256)S(1)}, f32[256]{0:T(256)S(1)}, f32[256]{0:T(256)S(1)}) all-reduce(f32[256]{0:T(256)S(1)} %get-tuple-element.10, f32[256]{0:T(256)S(1)} %get-tuple-element.9, f32[256]{0:T(256)S(1)} %get-tuple-element.6, ...), channel_id=1, replica_groups=mesh['section'=32,'tensor'=16] {'tensor'}, use_global_device_ids=true, to_apply=%region_3.4 | all-reduce | flops 1024 | bytes 8192 | tf_op jit(solution)/shard_map/psum | solution.py:59
  335.5 0.9 fusion.36
  336.5 60.9 %all-gather.5.cloned.1.call-done = bf16[256,2048]{1,0:T(8,128)(2,1)} async-done(((bf16[256,128]{1,0:T(8,128)(2,1)}), bf16[256,2048]{1,0:T(8,128)(2,1)}) %all-gather.5.cloned.1.call-update) | async-done | bytes 1048592 | tf_op jit(solution)/shard_map/all_gather | solution.py:67
  397.4 2.5 convolution_convert_fusion.3
  399.9 1.3 copy.12
  401.3 3.2 collective-permute-start.7
  404.5 3.0 collective-permute-done.7
  407.6 2.4 collective-permute-start.8
  409.9 3.8 collective-permute-done.8
  413.7 4.4 collective-permute-start.9
  418.2 2.6 collective-permute-done.9
  420.8 7.6 %collective-permute-start.10 = (bf16[256,128]{1,0:T(8,128)(2,1)S(1)}, bf16[256,128]{1,0:T(8,128)(2,1)S(1)}, u32[]{:S(2)}, u32[]{:S(2)}) collective-permute-start(bf16[256,128]{1,0:T(8,128)(2,1)S(1)} %collective-permute-done.9), channel_id=1, source_target_pairs={{0,128},{16,144},{32,160},{48,176},{64,192},{80,208},{96,224},{112... | collective-permute-start | bytes 196616 | tf_op jit(solution)/shard_map/ppermute | solution.py:14
  428.4 2.4 collective-permute-done.10
  430.8 13.5 %collective-permute-start.11 = (bf16[256,128]{1,0:T(8,128)(2,1)S(1)}, bf16[256,128]{1,0:T(8,128)(2,1)S(1)}, u32[]{:S(2)}, u32[]{:S(2)}) collective-permute-start(bf16[256,128]{1,0:T(8,128)(2,1)S(1)} %collective-permute-done.10), channel_id=1, source_target_pairs={{0,256},{16,272},{32,288},{48,304},{64,320},{80,336},{96,352},{112... | collective-permute-start | bytes 196616 | tf_op jit(solution)/shard_map/ppermute | solution.py:14
  444.3 2.9 collective-permute-done.11
  447.8 2.5 fusion
  450.2 4.1 collective-permute-start.6
  454.4 40.3 %reduce-scatter.7.cloned.1.call-done = bf16[128,256]{1,0:T(8,128)(2,1)} async-done(((bf16[2048,256]{1,0:T(8,128)(2,1)}), bf16[128,256]{1,0:T(8,128)(2,1)}) %reduce-scatter.7.cloned.1.call-update) | async-done | bytes 65552
  494.6 0.9 copy.13
  495.6 2.6 collective-permute-start
  498.2 1.5 fusion.1
  499.7 3.1 collective-permute-done
  502.8 0.6 copy.20
  504.1 0.6 copy.22
  (37 shorter events, 2.6 us)
Async XLA Ops:
  7.2 141.2 %copy-start = (bf16[1,2048,256]{2,1,0:T(8,128)(2,1)S(1)}, bf16[1,2048,256]{2,1,0:T(8,128)(2,1)}, u32[]{:S(2)}) copy-start(bf16[1,2048,256]{2,1,0:T(8,128)(2,1)} %param.12) | copy-start | bytes 3145732
  7.2 141.1 %all-gather.7.cloned.1.call-start = ((), (), s32[]{:S(2)}) async-start(), calls=%async_computation.3 | async-start | bytes 1114112 | tf_op jit(solution)/shard_map/all_gather | solution.py:88
  8.8 6.1 %collective-permute-start.1 = (bf16[256,128]{1,0:T(8,128)(2,1)S(1)}, bf16[256,128]{1,0:T(8,128)(2,1)S(1)}, u32[]{:S(2)}, u32[]{:S(2)}) collective-permute-start(bf16[256,128]{1,0:T(8,128)(2,1)S(1)} %dynamic-slice_bitcast_fusion), channel_id=1, source_target_pairs={{0,16},{16,0},{32,48},{48,32},{64,80},{80,64},{96,112},{112,96},{1... | collective-permute-start | bytes 196616 | tf_op jit(solution)/shard_map/ppermute | solution.py:14
  15.0 6.1 %collective-permute-start.2 = (bf16[256,128]{1,0:T(8,128)(2,1)S(1)}, bf16[256,128]{1,0:T(8,128)(2,1)S(1)}, u32[]{:S(2)}, u32[]{:S(2)}) collective-permute-start(bf16[256,128]{1,0:T(8,128)(2,1)S(1)} %collective-permute-done.1), channel_id=1, source_target_pairs={{0,32},{16,48},{32,0},{48,16},{64,96},{80,112},{96,64},{112,80},{1... | collective-permute-start | bytes 196616 | tf_op jit(solution)/shard_map/ppermute | solution.py:14
  21.1 7.4 %collective-permute-start.3 = (bf16[256,128]{1,0:T(8,128)(2,1)S(1)}, bf16[256,128]{1,0:T(8,128)(2,1)S(1)}, u32[]{:S(2)}, u32[]{:S(2)}) collective-permute-start(bf16[256,128]{1,0:T(8,128)(2,1)S(1)} %collective-permute-done.2), channel_id=1, source_target_pairs={{0,64},{16,80},{32,96},{48,112},{64,0},{80,16},{96,32},{112,48},{1... | collective-permute-start | bytes 196616 | tf_op jit(solution)/shard_map/ppermute | solution.py:14
  28.5 11.3 %collective-permute-start.4 = (bf16[256,128]{1,0:T(8,128)(2,1)S(1)}, bf16[256,128]{1,0:T(8,128)(2,1)S(1)}, u32[]{:S(2)}, u32[]{:S(2)}) collective-permute-start(bf16[256,128]{1,0:T(8,128)(2,1)S(1)} %collective-permute-done.3), channel_id=1, source_target_pairs={{0,128},{16,144},{32,160},{48,176},{64,192},{80,208},{96,224},{112... | collective-permute-start | bytes 196616 | tf_op jit(solution)/shard_map/ppermute | solution.py:14
  39.8 17.7 %collective-permute-start.5 = (bf16[256,128]{1,0:T(8,128)(2,1)S(1)}, bf16[256,128]{1,0:T(8,128)(2,1)S(1)}, u32[]{:S(2)}, u32[]{:S(2)}) collective-permute-start(bf16[256,128]{1,0:T(8,128)(2,1)S(1)} %collective-permute-done.4), channel_id=1, source_target_pairs={{0,256},{16,272},{32,288},{48,304},{64,320},{80,336},{96,352},{112... | collective-permute-start | bytes 196616 | tf_op jit(solution)/shard_map/ppermute | solution.py:14
  87.8 121.9 %all-gather.9.cloned.1.call-start = ((), (), s32[]{:S(2)}) async-start(), calls=%async_computation.4 | async-start | bytes 1114112 | tf_op jit(solution)/shard_map/all_gather | solution.py:91
  88.6 121.1 %copy-start.3 = (bf16[1,256,2048]{2,1,0:T(8,128)(2,1)S(1)}, bf16[1,256,2048]{2,1,0:T(8,128)(2,1)}, u32[]{:S(2)}) copy-start(bf16[1,256,2048]{2,1,0:T(8,128)(2,1)} %param.13) | copy-start | bytes 3145732
  88.6 217.4 %reduce-scatter.9.cloned.1.call-start = ((), (), s32[]{:S(2)}) async-start(), calls=%async_computation.6 | async-start | bytes 1114112
  211.4 0.7 copy-start.5
  213.9 0.8 copy-start.4
  213.9 121.6 %copy-start.6 = (bf16[1,256,128]{2,1,0:T(8,128)(2,1)S(1)}, bf16[1,256,128]{2,1,0:T(8,128)(2,1)}, u32[]{:S(2)}) copy-start(bf16[1,256,128]{2,1,0:T(8,128)(2,1)} %param.8) | copy-start | bytes 196612
  213.9 183.5 %all-gather.5.cloned.1.call-start = ((), (), s32[]{:S(2)}) async-start(), calls=%async_computation.2 | async-start | bytes 1114112 | tf_op jit(solution)/shard_map/all_gather | solution.py:67
  336.4 158.2 %reduce-scatter.7.cloned.1.call-start = ((), (), s32[]{:S(2)}) async-start(), calls=%async_computation.5 | async-start | bytes 1114112
  401.2 46.5 %copy-start.1 = (bf16[256,2048]{1,0:T(8,128)(2,1)S(1)}, bf16[256,2048]{1,0:T(8,128)(2,1)}, u32[]{:S(2)}) copy-start(bf16[256,2048]{1,0:T(8,128)(2,1)} %all-gather.7.cloned.1.call-done) | copy-start | bytes 3145732
  401.3 6.3 %collective-permute-start.7 = (bf16[256,128]{1,0:T(8,128)(2,1)S(1)}, bf16[256,128]{1,0:T(8,128)(2,1)S(1)}, u32[]{:S(2)}, u32[]{:S(2)}) collective-permute-start(bf16[256,128]{1,0:T(8,128)(2,1)S(1)} %bitcast.55), channel_id=1, source_target_pairs={{0,16},{16,0},{32,48},{48,32},{64,80},{80,64},{96,112},{112,96},{1... | collective-permute-start | bytes 196616 | tf_op jit(solution)/shard_map/ppermute | solution.py:14
  407.6 6.1 %collective-permute-start.8 = (bf16[256,128]{1,0:T(8,128)(2,1)S(1)}, bf16[256,128]{1,0:T(8,128)(2,1)S(1)}, u32[]{:S(2)}, u32[]{:S(2)}) collective-permute-start(bf16[256,128]{1,0:T(8,128)(2,1)S(1)} %collective-permute-done.7), channel_id=1, source_target_pairs={{0,32},{16,48},{32,0},{48,16},{64,96},{80,112},{96,64},{112,80},{1... | collective-permute-start | bytes 196616 | tf_op jit(solution)/shard_map/ppermute | solution.py:14
  413.7 7.0 %collective-permute-start.9 = (bf16[256,128]{1,0:T(8,128)(2,1)S(1)}, bf16[256,128]{1,0:T(8,128)(2,1)S(1)}, u32[]{:S(2)}, u32[]{:S(2)}) collective-permute-start(bf16[256,128]{1,0:T(8,128)(2,1)S(1)} %collective-permute-done.8), channel_id=1, source_target_pairs={{0,64},{16,80},{32,96},{48,112},{64,0},{80,16},{96,32},{112,48},{1... | collective-permute-start | bytes 196616 | tf_op jit(solution)/shard_map/ppermute | solution.py:14
  420.8 10.1 %collective-permute-start.10 = (bf16[256,128]{1,0:T(8,128)(2,1)S(1)}, bf16[256,128]{1,0:T(8,128)(2,1)S(1)}, u32[]{:S(2)}, u32[]{:S(2)}) collective-permute-start(bf16[256,128]{1,0:T(8,128)(2,1)S(1)} %collective-permute-done.9), channel_id=1, source_target_pairs={{0,128},{16,144},{32,160},{48,176},{64,192},{80,208},{96,224},{112... | collective-permute-start | bytes 196616 | tf_op jit(solution)/shard_map/ppermute | solution.py:14
  430.8 16.4 %collective-permute-start.11 = (bf16[256,128]{1,0:T(8,128)(2,1)S(1)}, bf16[256,128]{1,0:T(8,128)(2,1)S(1)}, u32[]{:S(2)}, u32[]{:S(2)}) collective-permute-start(bf16[256,128]{1,0:T(8,128)(2,1)S(1)} %collective-permute-done.10), channel_id=1, source_target_pairs={{0,256},{16,272},{32,288},{48,304},{64,320},{80,336},{96,352},{112... | collective-permute-start | bytes 196616 | tf_op jit(solution)/shard_map/ppermute | solution.py:14
  447.2 0.6 copy-start.8
  447.8 2.5 copy-start.7
  447.8 50.5 %copy-start.2 = (bf16[1,256,2048]{2,1,0:T(8,128)(2,1)S(1)}, bf16[1,256,2048]{2,1,0:T(8,128)(2,1)}, u32[]{:S(2)}) copy-start(bf16[1,256,2048]{2,1,0:T(8,128)(2,1)} %all-gather.9.cloned.1.call-done) | copy-start | bytes 3145732
  450.2 49.5 %collective-permute-start.6 = (bf16[256,128]{1,0:T(8,128)(2,1)S(1)}, bf16[256,128]{1,0:T(8,128)(2,1)S(1)}, u32[]{:S(2)}, u32[]{:S(2)}) collective-permute-start(bf16[256,128]{1,0:T(8,128)(2,1)S(1)} %copy-done.7), channel_id=1, source_target_pairs={{16,0},{32,16},{48,32},{64,48},{80,64},{96,80},{112,96},{128,112},... | collective-permute-start | bytes 196616 | tf_op jit(solution)/shard_map/ppermute | solution.py:20
  495.6 8.5 %copy-start.9 = (bf16[256,128]{1,0:T(8,128)(2,1)S(1)}, bf16[256,128]{1,0:T(8,128)(2,1)}, u32[]{:S(2)}) copy-start(bf16[256,128]{1,0:T(8,128)(2,1)} %copy-done.8) | copy-start | bytes 196612
  495.6 7.2 %collective-permute-start = (bf16[256,128]{1,0:T(8,128)(2,1)S(1)}, bf16[256,128]{1,0:T(8,128)(2,1)S(1)}, u32[]{:S(2)}, u32[]{:S(2)}) collective-permute-start(bf16[256,128]{1,0:T(8,128)(2,1)S(1)} %fusion.41), channel_id=1, source_target_pairs={{0,16},{16,32},{32,48},{48,64},{64,80},{80,96},{96,112},{112,128},... | collective-permute-start | bytes 196616 | tf_op jit(solution)/shard_map/ppermute | solution.py:20
Sparse Core Ops, SparseCore 0:
  87.9 60.3 all-gather.6
  151.5 58.1 all-gather.8
  214.9 91.0 reduce-scatter.8
  336.6 60.7 all-gather.4
  403.1 91.4 reduce-scatter.6
where the time goes:
time: 513 us; the launch traced here: 511 us
  waiting for transfers between devices  345 us (67%)
  starting transfers between devices  71.8 us (14%)
  blocking collectives  57.6 us (11%)
  between operations  14.7 us (3%)
  matrix products  10.3 us (2%)
  local copies, waits for them, and re-layouts  9.98 us (2%)
    unnamed x7, waiting for transfers between devices  132 us
    ppermute x10, starting transfers between devices, from_partner(): return lax.ppermute(value, axis, pairs)  64.9 us
    all_gather x1, waiting for transfers between devices, per_device(): lax.all_gather(normed_part, 'tensor', axis=1, tiled=True)  60.9 us
    all_gather x1, waiting for transfers between devices, per_device(): back_normed = lax.all_gather(back_part, 'tensor', axis=1, tiled=True)  59.7 us
    all_gather x1, waiting for transfers between devices, per_device(): grad_full = lax.all_gather(grad_out, 'tensor', axis=1, tiled=True)  59.7 us
    psum x1, blocking collectives, per_device(): lax.psum((jnp.sum(back_f, axis=1), jnp.sum(back_f * back_f, axis=1)), 'te...  29.3 us
    ppermute x10, waiting for transfers between devices, from_partner(): return lax.ppermute(value, axis, pairs)  29 us
    psum x1, blocking collectives, per_device(): lax.psum((jnp.sum(forward_f, axis=1), jnp.sum(forward_f * forward_f, axis...  28.3 us
  transfers between devices with their start and end apart: 17, of which 16 were waited for; matrix products, arithmetic and copies ran while one was open for 1% of the time, Pallas kernels for 0%

commit v1 on v0

v1 whole, which is shorter than its diff:
```python
import functools

import jax
import jax.numpy as jnp
from jax import lax
from jax.experimental import pallas as pl
from jax.experimental.pallas import tpu as pltpu
from jax.sharding import PartitionSpec as P

EPSILON = 1e-05
GELU_ROOT = 0.7978845608028654
GELU_CUBIC = 0.044715

BF = jnp.bfloat16
F32 = jnp.float32
ROWS = 16
VMEM_LIMIT = 48 * 2**20


def vmem(count):
    return [pl.BlockSpec(memory_space=pltpu.VMEM)] * count


def dot(left, right, dims=((1,), (0,))):
    return lax.dot_general(left, right, (dims, ((), ())), preferred_element_type=F32)


def gelu_parts(values):
    inner = GELU_ROOT * (values + GELU_CUBIC * values * values * values)
    return jnp.tanh(inner)


def split_two(values):
    high = values.astype(BF)
    low = (values - high.astype(F32)).astype(BF)
    return high, low


def sums_to_rows(first, second):
    tokens = first.shape[0]
    parts = [part.astype(F32) for value in (first, second) for part in split_two(value)]
    lane = lax.broadcasted_iota(jnp.int32, (tokens, 128), 1)
    wide = jnp.zeros((tokens, 128), F32)
    for index, part in enumerate(parts):
        wide = jnp.where(lane == index, part, wide)
    tall = wide.T
    return jnp.concatenate([tall[:8, :128], tall[:8, 128:]], axis=0).astype(BF)


def resplit(rows_f):
    out = []
    for half in (0, 8):
        for stat in (0, 2):
            total = rows_f[half + stat : half + stat + 1] + rows_f[half + stat + 1 : half + stat + 2]
            out += list(split_two(total))
        out.append(jnp.zeros((4, rows_f.shape[1]), BF))
    return jnp.concatenate([part.astype(F32) for part in out], axis=0).astype(BF)


def both_cores(me, near, far):
    return jnp.concatenate([jnp.where(me == 0, near, far), jnp.where(me == 0, far, near)], axis=1)


def block_kernel(core, near, far, gain, weight_a, weight_b, own, other, normed_out, pre_grad_out, act_out, stats_out, hidden_ref):
    me = core[0]
    chips, _, tokens, _ = near.shape
    width = 2 * chips * 128

    def stats_of(which):
        total = jnp.zeros((tokens, 128), F32)
        squares = jnp.zeros((tokens, 128), F32)
        for chip in range(chips):
            for side in (near, far):
                value = side[chip, which].astype(F32)
                total += value
                squares += value * value
        center = jnp.sum(total, axis=1, keepdims=True) / width
        second = jnp.sum(squares, axis=1, keepdims=True) / width
        return center, lax.rsqrt(second - center * center + EPSILON)

    def chunk(which, chip):
        return both_cores(me, near[chip, which], far[chip, which])

    def cols(chip):
        return slice(chip * 256, chip * 256 + 256)

    def put(chip, rows, value):
        low, high = value[:, :128], value[:, 128:]
        own[chip, rows, :] = jnp.where(me == 0, low, high)
        other[chip, rows, :] = jnp.where(me == 0, high, low)

    center, scale = stats_of(0)
    pre = jnp.zeros((tokens, 256), F32)
    for chip in range(chips):
        normed = ((chunk(0, chip).astype(F32) - center) * scale * gain[:, cols(chip)]).astype(BF)
        pre += dot(normed, weight_a[cols(chip), :])
    act = (0.5 * pre * (1.0 + gelu_parts(pre))).astype(BF)
    for chip in range(chips):
        put(chip, slice(0, tokens), dot(act, weight_b[:, cols(chip)]).astype(BF))

    center, scale = stats_of(2)
    stats_out[...] = jnp.concatenate([jnp.broadcast_to(center, (tokens, 128)), jnp.broadcast_to(scale, (tokens, 128))], axis=1)
    pre = jnp.zeros((tokens, 256), F32)
    act_grad = jnp.zeros((tokens, 256), F32)
    for chip in range(chips):
        hidden = (chunk(2, chip).astype(F32) - center) * scale
        hidden_ref[:, cols(chip)] = hidden
        normed = (hidden * gain[:, cols(chip)]).astype(BF)
        normed_out[:, cols(chip)] = normed
        pre += dot(normed, weight_a[cols(chip), :])
        act_grad += dot(chunk(1, chip), weight_b[:, cols(chip)], ((1,), (1,)))
    tangent = gelu_parts(pre)
    act_out[...] = (0.5 * pre * (1.0 + tangent)).astype(BF)
    slope = 0.5 * (1.0 + tangent) + 0.5 * pre * (1.0 - tangent * tangent) * GELU_ROOT * (
        1.0 + 3.0 * GELU_CUBIC * pre * pre
    )
    pre_grad = (act_grad * slope).astype(BF)
    pre_grad_out[...] = pre_grad
    plain = jnp.zeros((tokens, 256), F32)
    moment = jnp.zeros((tokens, 256), F32)
    for chip in range(chips):
        term = dot(pre_grad, weight_a[cols(chip), :], ((1,), (1,))).astype(BF)
        put(chip, slice(tokens, 2 * tokens), term)
        scaled = term.astype(F32) * gain[:, cols(chip)]
        plain += scaled
        moment += scaled * hidden_ref[:, cols(chip)]
    rows = sums_to_rows(jnp.sum(plain, axis=1, keepdims=True), jnp.sum(moment, axis=1, keepdims=True))
    for chip in range(chips):
        own[chip, 2 * tokens :, :] = rows
        other[chip, 2 * tokens :, :] = rows


def pair_kernel(own, received, total):
    chips, rows, _ = own.shape
    body = rows - ROWS
    for chip in range(chips):
        total[chip, :body, :] = (own[chip, :body, :].astype(F32) + received[chip, :body, :].astype(F32)).astype(BF)
    sums = resplit(own[0, body:, :].astype(F32) + received[0, body:, :].astype(F32))
    for chip in range(chips):
        total[chip, body:, :] = sums


def finish_kernel(parts, forward_in, grad_out, fetched, stats, gain, outputs, input_grad):
    chips, rows, _ = parts.shape
    tokens = forward_in.shape[0]
    width = 2 * chips * 128
    total = jnp.zeros((rows, 128), F32)
    for chip in range(chips):
        total += parts[chip].astype(F32)
    outputs[...] = (forward_in[...].astype(F32) + total[:tokens]).astype(BF)
    scaled = total[tokens : 2 * tokens] * gain[...]
    sums = total[2 * tokens :]
    flat = jnp.concatenate([sums[:8], sums[8:]], axis=1)
    tall = jnp.concatenate([flat, jnp.zeros((120, tokens), F32)], axis=0).T
    plain_mean = (tall[:, 0:1] + tall[:, 1:2]) / width
    moment_mean = (tall[:, 2:3] + tall[:, 3:4]) / width
    center, scale = stats[:, :128], stats[:, 128:]
    hidden = (fetched[...].astype(F32) - center) * scale
    input_grad[...] = (
        grad_out[...].astype(F32) + scale * (scaled - plain_mean - hidden * moment_mean)
    ).astype(BF)


def weights_kernel(core, near, far, normed, pre_grad, act, grad_a, grad_b):
    me = core[0]
    chips = near.shape[0]
    for chip in range(chips):
        cols = slice(chip * 256, chip * 256 + 256)
        grad_a[cols, :] = dot(normed[:, cols], pre_grad[...], ((0,), (0,))).astype(BF)
        chunk = both_cores(me, near[chip, 1], far[chip, 1])
        grad_b[:, cols] = dot(act[...], chunk, ((0,), (0,))).astype(BF)


def call(kernel, out_shapes, operands, specs=None, scratch=(), flops=0, nbytes=0):
    return pl.pallas_call(
        kernel,
        out_shape=out_shapes,
        in_specs=specs or vmem(len(operands)),
        out_specs=tuple(vmem(len(out_shapes))),
        scratch_shapes=list(scratch),
        compiler_params=pltpu.CompilerParams(vmem_limit_bytes=VMEM_LIMIT),
        cost_estimate=pl.CostEstimate(flops=flops, bytes_accessed=nbytes, transcendentals=0),
    )(*operands)


def per_device(inputs, out_grads, parked_store, fetch_slot, norm_gain, weight_in, weight_out):
    forward_in = inputs[0]
    grad_out = out_grads[0]
    weight_a = weight_in[0]
    weight_b = weight_out[0]
    tokens, shard_cols = forward_in.shape
    sections, ranks = lax.axis_size("section"), lax.axis_size("tensor")
    chips = ranks // 2
    width = shard_cols * ranks
    hidden_units = weight_a.shape[1]
    rank = lax.axis_index("tensor")
    core = lax.rem(rank, 2)
    same_core = [[2 * chip + side for chip in range(chips)] for side in range(2)]
    mirror = [(s, sections - 1 - s) for s in range(sections)]
    swap = [(t, t ^ 1) for t in range(ranks)]

    returned = lax.dynamic_index_in_dim(parked_store[0], fetch_slot[0], 0, keepdims=False)
    fetched = lax.ppermute(returned, "section", mirror)
    parked = lax.ppermute(forward_in, "section", mirror)

    mine = jnp.stack([forward_in, grad_out, fetched])
    spread = jnp.broadcast_to(mine[None], (chips,) + mine.shape)
    near = lax.all_to_all(spread, "tensor", 0, 0, tiled=True, axis_index_groups=same_core)
    far = lax.ppermute(near, "tensor", swap)

    shape = jax.ShapeDtypeStruct
    part_rows = 2 * tokens + ROWS
    parts = shape((chips, part_rows, 128), BF)
    own, other, normed, pre_grad, act, stats = call(
        block_kernel,
        (
            parts,
            parts,
            shape((tokens, width), BF),
            shape((tokens, hidden_units), BF),
            shape((tokens, hidden_units), BF),
            shape((tokens, 256), F32),
        ),
        (core.reshape(1), near, far, norm_gain, weight_a, weight_b),
        specs=[pl.BlockSpec(memory_space=pltpu.SMEM)] + vmem(5),
        scratch=(pltpu.VMEM((tokens, width), F32),),
        flops=10 * tokens * width * hidden_units,
        nbytes=10 * 2**20,
    )

    received = lax.ppermute(other, "tensor", swap)
    summed = call(pair_kernel, (parts,), (own, received), nbytes=3 * 2**20)[0]
    collected = lax.all_to_all(summed, "tensor", 0, 0, tiled=True, axis_index_groups=same_core)

    gain_part = lax.dynamic_slice_in_dim(norm_gain, rank * shard_cols, shard_cols, 1)
    piece = shape((tokens, shard_cols), BF)
    outputs, input_grad = call(
        finish_kernel,
        (piece, piece),
        (collected, forward_in, grad_out, fetched, stats, gain_part),
        nbytes=2 * 2**20,
    )
    arrivals = lax.ppermute(outputs, "section", [(s, s + 1) for s in range(sections - 1)])
    sent_grads = lax.ppermute(input_grad, "section", [(s + 1, s) for s in range(sections - 1)])

    grad_a, grad_b = call(
        weights_kernel,
        (shape(weight_a.shape, BF), shape(weight_b.shape, BF)),
        (core.reshape(1), near, far, normed, pre_grad, act),
        specs=[pl.BlockSpec(memory_space=pltpu.SMEM)] + vmem(5),
        flops=4 * tokens * width * hidden_units,
        nbytes=6 * 2**20,
    )
    return (arrivals[None], sent_grads[None], parked[None], grad_a[None], grad_b[None])


def solution(mesh):
    return jax.shard_map(
        per_device,
        mesh=mesh,
        in_specs=(
            P("section", None, "tensor"),
            P("section", None, "tensor"),
            P("section", None, None, "tensor"),
            P("section"),
            P("section", None),
            P("section", None, "tensor"),
            P("section", "tensor", None),
        ),
        out_specs=(
            P("section", None, "tensor"),
            P("section", None, "tensor"),
            P("section", None, "tensor"),
            P("section", None, "tensor"),
            P("section", "tensor", None),
        ),
        check_vma=False,
    )
```

time: 513 us -> 110 us (0.21)
  the two profiles are of different devices: /device:TPU:40 before, /device:TPU:2 now
where the time goes in v1:
time: 110 us; the launch traced here: 109 us
  waiting for transfers between devices  29.2 us (27%)
  blocking collectives  28.6 us (26%)
  starting transfers between devices  27.6 us (25%)
  local copies, waits for them, and re-layouts  12.3 us (11%)
  Pallas kernels  9.17 us (8%)
  between operations  1.51 us (1%)
    all_to_all x1, blocking collectives, per_device(): lax.all_to_all(spread, 'tensor', 0, 0, tiled=True, axis_index_groups=same...  28.6 us
    all_to_all x1, waiting for transfers between devices, per_device(): lax.all_to_all(summed, 'tensor', 0, 0, tiled=True, axis_index_groups=same...  15.7 us
    unnamed x41, local copies, waits for them, and re-layouts  11.9 us
    ppermute x1, starting transfers between devices, per_device(): fetched = lax.ppermute(returned, 'section', mirror)  11.4 us
    pallas_call x4, Pallas kernels, call(): pl.pallas_call(kernel, out_shape=out_shapes, in_specs=specs or vmem(len(o...  9.17 us
    ppermute x1, waiting for transfers between devices, per_device(): fetched = lax.ppermute(returned, 'section', mirror)  6.29 us
    all_to_all x1, starting transfers between devices, per_device(): lax.all_to_all(summed, 'tensor', 0, 0, tiled=True, axis_index_groups=same...  4.5 us
    ppermute x1, starting transfers between devices, per_device(): lax.ppermute(outputs, 'section', [(s, s + 1) for s in range(sections - 1)])  3.52 us
  transfers between devices with their start and end apart: 7, of which 5 were waited for; matrix products, arithmetic and copies ran while one was open for 0% of the time, Pallas kernels for 3%

profile of v1, /device:TPU:2, one launch (start us, length us, event | category | flops | bytes accessed | tf_op | source)
XLA Modules:
  0.0 109.3 jit_solution(1046349409625198720)
XLA Ops:
  0.6 0.0 copy-start
  1.3 0.2 copy-done
  1.6 11.4 %collective-permute-start = (bf16[256,128]{1,0:T(8,128)(2,1)S(1)}, bf16[256,128]{1,0:T(8,128)(2,1)S(1)}, u32[]{:S(2)}, u32[]{:S(2)}) collective-permute-start(bf16[256,128]{1,0:T(8,128)(2,1)S(1)} %dynamic-slice_bitcast_fusion), channel_id=1, source_target_pairs={{0,496},{16,480},{32,464},{48,448},{64,432},{80,416},{96,400},{112... | collective-permute-start | bytes 196616 | tf_op jit(solution)/shard_map/ppermute | solution.py:203
  12.9 6.3 %collective-permute-done.fetched = bf16[256,128]{1,0:T(8,128)(2,1)S(1)} collective-permute-done((bf16[256,128]{1,0:T(8,128)(2,1)S(1)}, bf16[256,128]{1,0:T(8,128)(2,1)S(1)}, u32[]{:S(2)}, u32[]{:S(2)}) %collective-permute-start) | collective-permute-done | bytes 65568 | tf_op jit(solution)/shard_map/ppermute | solution.py:203
  19.2 0.9 pad_maximum_fusion
  20.1 0.3 broadcast_in_dim.21
  20.5 0.0 copy-start.18
  20.5 28.6 %all_to_all.10.near = bf16[8,3,256,128]{3,2,1,0:T(8,128)(2,1)S(1)} all-to-all(bf16[8,3,256,128]{3,2,1,0:T(8,128)(2,1)S(1)} %broadcast_in_dim.21), channel_id=1, replica_groups={{0,2,4,6,8,10,12,14},{1,3,5,7,9,11,13,15},{16,18,20,22,24,26,28,30},{17..., dimensions={0} | all-to-all | bytes 3145728 | tf_op jit(solution)/shard_map/all_to_all | solution.py:208
  49.1 0.0 copy-start.1
  49.1 1.9 %collective-permute-start.1 = (bf16[8,3,256,128]{3,2,1,0:T(8,128)(2,1)S(1)}, bf16[8,3,256,128]{3,2,1,0:T(8,128)(2,1)S(1)}, u32[]{:S(2)}, u32[]{:S(2)}) collective-permute-start(bf16[8,3,256,128]{3,2,1,0:T(8,128)(2,1)S(1)} %all_to_all.10.near), channel_id=1, source_target_pairs={{0,1},{1,0},{2,3},{3,2},{4,5},{5,4},{6,7},{7,6},{8,9},{9,8},{10,11... | collective-permute-start | bytes 4718600 | tf_op jit(solution)/shard_map/ppermute | solution.py:209
  51.0 3.4 %collective-permute-done.1.far = bf16[8,3,256,128]{3,2,1,0:T(8,128)(2,1)S(1)} collective-permute-done((bf16[8,3,256,128]{3,2,1,0:T(8,128)(2,1)S(1)}, bf16[8,3,256,128]{3,2,1,0:T(8,128)(2,1)S(1)}, u32[]{:S(2)}, u32[]{:S(2)}) %collective-permute-start.1) | collective-permute-done | bytes 1572896 | tf_op jit(solution)/shard_map/ppermute | solution.py:209
  54.4 0.0 copy-done.1
  54.4 1.1 %copy-done.3 = bf16[8,3,256,128]{3,2,1,0:T(8,128)(2,1)} copy-done((bf16[8,3,256,128]{3,2,1,0:T(8,128)(2,1)}, bf16[8,3,256,128]{3,2,1,0:T(8,128)(2,1)S(1)}, u32[]{:S(2)}) %copy-start.3) | copy-done | bytes 1572888
  55.6 0.0 copy-done.18
  55.6 1.2 %copy-done.8 = bf16[1,2048,256]{2,1,0:T(8,128)(2,1)S(1)} copy-done((bf16[1,2048,256]{2,1,0:T(8,128)(2,1)S(1)}, bf16[1,2048,256]{2,1,0:T(8,128)(2,1)}, u32[]{:S(2)}) %copy-start.8) | copy-done | bytes 1048600
  56.8 1.2 %copy-done.9 = bf16[1,256,2048]{2,1,0:T(8,128)(2,1)S(1)} copy-done((bf16[1,256,2048]{2,1,0:T(8,128)(2,1)S(1)}, bf16[1,256,2048]{2,1,0:T(8,128)(2,1)}, u32[]{:S(2)}) %copy-start.9) | copy-done | bytes 1048600
  58.0 5.1 %shard_map.110 = (bf16[8,528,128]{2,1,0:T(8,128)(2,1)S(1)}, bf16[8,528,128]{2,1,0:T(8,128)(2,1)S(1)}, bf16[256,2048]{1,0:T(8,128)(2,1)S(1)}, bf16[256,256]{1,0:T...) custom-call(s32[1]{0:T(128)} %bitcast.core, bf16[8,3,256,128]{3,2,1,0:T(8,128)(2,1)} %copy-done.1, ...), custom_call_target="tpu_custom_call" | custom-call | flops 1342177280 | bytes 10485760 | tf_op jit(solution)/shard_map/pallas_call | solution.py:175
  63.1 1.0 copy-done.6
  64.1 0.7 copy-done.12
  64.8 0.7 copy-done.14
  65.4 0.6 copy-done.16
  66.1 2.0 %collective-permute-start.2 = (bf16[8,528,128]{2,1,0:T(8,128)(2,1)S(1)}, bf16[8,528,128]{2,1,0:T(8,128)(2,1)S(1)}, u32[]{:S(2)}, u32[]{:S(2)}) collective-permute-start(bf16[8,528,128]{2,1,0:T(8,128)(2,1)S(1)} %get-tuple-element.16), channel_id=1, source_target_pairs={{0,1},{1,0},{2,3},{3,2},{4,5},{5,4},{6,7},{7,6},{8,9},{9,8},{10,11... | collective-permute-start | bytes 3244040 | tf_op jit(solution)/shard_map/ppermute | solution.py:231
  68.1 2.5 %collective-permute-done.2.received = bf16[8,528,128]{2,1,0:T(8,128)(2,1)S(1)} collective-permute-done((bf16[8,528,128]{2,1,0:T(8,128)(2,1)S(1)}, bf16[8,528,128]{2,1,0:T(8,128)(2,1)S(1)}, u32[]{:S(2)}, u32[]{:S(2)}) %collective-permute-start.2) | collective-permute-done | bytes 1081376 | tf_op jit(solution)/shard_map/ppermute | solution.py:231
  70.7 0.3 shard_map.111
  70.9 0.0 copy-start.5
  71.0 1.0 copy-done.5
  72.0 4.5 %all-to-all-start.1 = ((bf16[8,528,128]{2,1,0:T(8,128)(2,1)}), bf16[8,528,128]{2,1,0:T(8,128)(2,1)}, u32[]{:S(2)}, u32[]{:S(2)}) async-start(bf16[8,528,128]{2,1,0:T(8,128)(2,1)} %copy-done.5), calls=%async_computation.1 | async-start | bytes 2162688 | tf_op jit(solution)/shard_map/all_to_all | solution.py:233
  76.5 0.0 copy-done.11
  76.5 1.9 %collective-permute-start.5 = (bf16[256,128]{1,0:T(8,128)(2,1)S(1)}, bf16[256,128]{1,0:T(8,128)(2,1)S(1)}, u32[]{:S(2)}, u32[]{:S(2)}) collective-permute-start(bf16[256,128]{1,0:T(8,128)(2,1)S(1)} %bitcast.20), channel_id=1, source_target_pairs={{0,496},{16,480},{32,464},{48,448},{64,432},{80,416},{96,400},{112... | collective-permute-start | bytes 196616 | tf_op jit(solution)/shard_map/ppermute | solution.py:204
  78.5 15.7 %all-to-all-done.1.parts = bf16[8,528,128]{2,1,0:T(8,128)(2,1)} async-done(((bf16[8,528,128]{2,1,0:T(8,128)(2,1)}), bf16[8,528,128]{2,1,0:T(8,128)(2,1)}, u32[]{:S(2)}, u32[]{:S(2)}) %all-to-all-start.1) | async-done | bytes 1081376 | tf_op jit(solution)/shard_map/all_to_all | solution.py:233
  94.1 0.0 copy-done.10
  94.1 0.9 copy-done.13
  95.1 1.7 %shard_map.112 = (bf16[256,128]{1,0:T(8,128)(2,1)S(1)}, bf16[256,128]{1,0:T(8,128)(2,1)S(1)}) custom-call(bf16[8,528,128]{2,1,0:T(8,128)(2,1)} %all-to-all-done.1.parts, bf16[256,128]{1,0:T(8,128)(2,1)S(1)} %bitcast.21, bf16[256,128]{1,0:T(8,128)(2,1)S(1)} %bitcast.19, bf16[256,128]{1,0:T(8,128)(2,1)S(1)} %collective-permute-done.fetched, ...), custom_call_target="tpu_custom_call" | custom-call | bytes 2097152 | tf_op jit(solution)/shard_map/pallas_call | solution.py:175
  96.8 3.5 %collective-permute-start.3 = (bf16[256,128]{1,0:T(8,128)(2,1)S(1)}, bf16[256,128]{1,0:T(8,128)(2,1)S(1)}, u32[]{:S(2)}, u32[]{:S(2)}) collective-permute-start(bf16[256,128]{1,0:T(8,128)(2,1)S(1)} %get-tuple-element.18), channel_id=1, source_target_pairs={{0,16},{16,32},{32,48},{48,64},{64,80},{80,96},{96,112},{112,128},... | collective-permute-start | bytes 196616 | tf_op jit(solution)/shard_map/ppermute | solution.py:243
  100.3 2.3 %collective-permute-start.4 = (bf16[256,128]{1,0:T(8,128)(2,1)S(1)}, bf16[256,128]{1,0:T(8,128)(2,1)S(1)}, u32[]{:S(2)}, u32[]{:S(2)}) collective-permute-start(bf16[256,128]{1,0:T(8,128)(2,1)S(1)} %get-tuple-element.19), channel_id=1, source_target_pairs={{16,0},{32,16},{48,32},{64,48},{80,64},{96,80},{112,96},{128,112},... | collective-permute-start | bytes 196616 | tf_op jit(solution)/shard_map/ppermute | solution.py:244
  102.7 0.0 collective-permute-done.5
  102.7 0.0 copy-done.2
  102.7 0.0 copy-done.4
  102.7 0.0 copy-done.15
  102.7 0.0 copy-done.17
  102.7 0.0 copy-start.7
  102.7 1.2 %copy-done.7 = bf16[256,2048]{1,0:T(8,128)(2,1)S(1)} copy-done((bf16[256,2048]{1,0:T(8,128)(2,1)S(1)}, bf16[256,2048]{1,0:T(8,128)(2,1)}, u32[]{:S(2)}) %copy-start.7) | copy-done | bytes 1048600
  103.9 2.1 %shard_map.113 = (bf16[2048,256]{1,0:T(8,128)(2,1)}, bf16[256,2048]{1,0:T(8,128)(2,1)}) custom-call(s32[1]{0:T(128)} %bitcast.core, bf16[8,3,256,128]{3,2,1,0:T(8,128)(2,1)S(1)} %copy-done.2, bf16[8,3,256,128]{3,2,1,0:T(8,128)(2,1)S(1)} %copy-done.4, bf16[256,2048]{1,0:T(8,128)(2,1)S(1)} %copy-done.7, bf16[256,256]{1,0:T(8,128)(2,1)S(1)} %copy-done.15, ...), custom_call_target="tpu_custom_call" | custom-call | flops 536870912 | bytes 6291456 | tf_op jit(solution)/shard_map/pallas_call | solution.py:175
  106.0 0.0 collective-permute-done.3
  106.0 1.4 %collective-permute-done.4 = bf16[256,128]{1,0:T(8,128)(2,1)S(1)} collective-permute-done((bf16[256,128]{1,0:T(8,128)(2,1)S(1)}, bf16[256,128]{1,0:T(8,128)(2,1)S(1)}, u32[]{:S(2)}, u32[]{:S(2)}) %collective-permute-start.4) | collective-permute-done | bytes 65568 | tf_op jit(solution)/shard_map/ppermute | solution.py:244
  107.4 0.6 copy.16
  108.0 0.6 copy.17
  108.7 0.6 copy.18
  (16 shorter events, 0.0 us)
Async XLA Ops:
  0.6 0.9 copy-start
  1.6 17.7 %collective-permute-start = (bf16[256,128]{1,0:T(8,128)(2,1)S(1)}, bf16[256,128]{1,0:T(8,128)(2,1)S(1)}, u32[]{:S(2)}, u32[]{:S(2)}) collective-permute-start(bf16[256,128]{1,0:T(8,128)(2,1)S(1)} %dynamic-slice_bitcast_fusion), channel_id=1, source_target_pairs={{0,496},{16,480},{32,464},{48,448},{64,432},{80,416},{96,400},{112... | collective-permute-start | bytes 196616 | tf_op jit(solution)/shard_map/ppermute | solution.py:203
  20.5 35.1 %copy-start.18 = (f32[1,2048]{1,0:T(1,128)S(1)}, f32[1,2048]{1,0:T(1,128)}, u32[]{:S(2)}) copy-start(f32[1,2048]{1,0:T(1,128)} %gain.1) | copy-start | bytes 24580
  49.1 5.3 %copy-start.1 = (bf16[8,3,256,128]{3,2,1,0:T(8,128)(2,1)}, bf16[8,3,256,128]{3,2,1,0:T(8,128)(2,1)S(1)}, u32[]{:S(2)}) copy-start(bf16[8,3,256,128]{3,2,1,0:T(8,128)(2,1)S(1)} %all_to_all.10.near) | copy-start | bytes 4718596
  49.1 5.3 %collective-permute-start.1 = (bf16[8,3,256,128]{3,2,1,0:T(8,128)(2,1)S(1)}, bf16[8,3,256,128]{3,2,1,0:T(8,128)(2,1)S(1)}, u32[]{:S(2)}, u32[]{:S(2)}) collective-permute-start(bf16[8,3,256,128]{3,2,1,0:T(8,128)(2,1)S(1)} %all_to_all.10.near), channel_id=1, source_target_pairs={{0,1},{1,0},{2,3},{3,2},{4,5},{5,4},{6,7},{7,6},{8,9},{9,8},{10,11... | collective-permute-start | bytes 4718600 | tf_op jit(solution)/shard_map/ppermute | solution.py:209
  54.4 1.1 %copy-start.3 = (bf16[8,3,256,128]{3,2,1,0:T(8,128)(2,1)}, bf16[8,3,256,128]{3,2,1,0:T(8,128)(2,1)S(1)}, u32[]{:S(2)}) copy-start(bf16[8,3,256,128]{3,2,1,0:T(8,128)(2,1)S(1)} %collective-permute-done.1.far) | copy-start | bytes 4718596
  55.6 1.2 %copy-start.8 = (bf16[1,2048,256]{2,1,0:T(8,128)(2,1)S(1)}, bf16[1,2048,256]{2,1,0:T(8,128)(2,1)}, u32[]{:S(2)}) copy-start(bf16[1,2048,256]{2,1,0:T(8,128)(2,1)} %param.12) | copy-start | bytes 3145732
  56.8 1.2 %copy-start.9 = (bf16[1,256,2048]{2,1,0:T(8,128)(2,1)S(1)}, bf16[1,256,2048]{2,1,0:T(8,128)(2,1)}, u32[]{:S(2)}) copy-start(bf16[1,256,2048]{2,1,0:T(8,128)(2,1)} %param.13) | copy-start | bytes 3145732
  63.1 1.0 copy-start.6
  64.1 0.7 copy-start.12
  64.8 0.7 copy-start.14
  65.4 0.7 copy-start.16
  66.1 4.6 %collective-permute-start.2 = (bf16[8,528,128]{2,1,0:T(8,128)(2,1)S(1)}, bf16[8,528,128]{2,1,0:T(8,128)(2,1)S(1)}, u32[]{:S(2)}, u32[]{:S(2)}) collective-permute-start(bf16[8,528,128]{2,1,0:T(8,128)(2,1)S(1)} %get-tuple-element.16), channel_id=1, source_target_pairs={{0,1},{1,0},{2,3},{3,2},{4,5},{5,4},{6,7},{7,6},{8,9},{9,8},{10,11... | collective-permute-start | bytes 3244040 | tf_op jit(solution)/shard_map/ppermute | solution.py:231
  70.7 5.8 %copy-start.11 = (bf16[1,256,128]{2,1,0:T(8,128)(2,1)S(1)}, bf16[1,256,128]{2,1,0:T(8,128)(2,1)}, u32[]{:S(2)}) copy-start(bf16[1,256,128]{2,1,0:T(8,128)(2,1)} %param.7) | copy-start | bytes 196612
  70.7 23.4 %copy-start.10 = (bf16[1,256,128]{2,1,0:T(8,128)(2,1)S(1)}, bf16[1,256,128]{2,1,0:T(8,128)(2,1)}, u32[]{:S(2)}) copy-start(bf16[1,256,128]{2,1,0:T(8,128)(2,1)} %param.8) | copy-start | bytes 196612
  70.9 1.0 copy-start.5
  72.0 30.7 %copy-start.2 = (bf16[8,3,256,128]{3,2,1,0:T(8,128)(2,1)S(1)}, bf16[8,3,256,128]{3,2,1,0:T(8,128)(2,1)}, u32[]{:S(2)}) copy-start(bf16[8,3,256,128]{3,2,1,0:T(8,128)(2,1)} %copy-done.1) | copy-start | bytes 4718596
  72.0 30.7 %copy-start.4 = (bf16[8,3,256,128]{3,2,1,0:T(8,128)(2,1)S(1)}, bf16[8,3,256,128]{3,2,1,0:T(8,128)(2,1)}, u32[]{:S(2)}) copy-start(bf16[8,3,256,128]{3,2,1,0:T(8,128)(2,1)} %copy-done.3) | copy-start | bytes 4718596
  72.0 22.1 %all-to-all-start.1 = ((bf16[8,528,128]{2,1,0:T(8,128)(2,1)}), bf16[8,528,128]{2,1,0:T(8,128)(2,1)}, u32[]{:S(2)}, u32[]{:S(2)}) async-start(bf16[8,528,128]{2,1,0:T(8,128)(2,1)} %copy-done.5), calls=%async_computation.1 | async-start | bytes 2162688 | tf_op jit(solution)/shard_map/all_to_all | solution.py:233
  76.5 26.2 %collective-permute-start.5 = (bf16[256,128]{1,0:T(8,128)(2,1)S(1)}, bf16[256,128]{1,0:T(8,128)(2,1)S(1)}, u32[]{:S(2)}, u32[]{:S(2)}) collective-permute-start(bf16[256,128]{1,0:T(8,128)(2,1)S(1)} %bitcast.20), channel_id=1, source_target_pairs={{0,496},{16,480},{32,464},{48,448},{64,432},{80,416},{96,400},{112... | collective-permute-start | bytes 196616 | tf_op jit(solution)/shard_map/ppermute | solution.py:204
  94.1 1.0 copy-start.13
  95.1 7.6 %copy-start.15 = (bf16[256,256]{1,0:T(8,128)(2,1)S(1)}, bf16[256,256]{1,0:T(8,128)(2,1)}, u32[]{:S(2)}) copy-start(bf16[256,256]{1,0:T(8,128)(2,1)} %copy-done.14) | copy-start | bytes 393220
  95.1 7.6 %copy-start.17 = (bf16[256,256]{1,0:T(8,128)(2,1)S(1)}, bf16[256,256]{1,0:T(8,128)(2,1)}, u32[]{:S(2)}) copy-start(bf16[256,256]{1,0:T(8,128)(2,1)} %copy-done.16) | copy-start | bytes 393220
  96.8 9.2 %collective-permute-start.3 = (bf16[256,128]{1,0:T(8,128)(2,1)S(1)}, bf16[256,128]{1,0:T(8,128)(2,1)S(1)}, u32[]{:S(2)}, u32[]{:S(2)}) collective-permute-start(bf16[256,128]{1,0:T(8,128)(2,1)S(1)} %get-tuple-element.18), channel_id=1, source_target_pairs={{0,16},{16,32},{32,48},{48,64},{64,80},{80,96},{96,112},{112,128},... | collective-permute-start | bytes 196616 | tf_op jit(solution)/shard_map/ppermute | solution.py:243
  100.3 7.1 %collective-permute-start.4 = (bf16[256,128]{1,0:T(8,128)(2,1)S(1)}, bf16[256,128]{1,0:T(8,128)(2,1)S(1)}, u32[]{:S(2)}, u32[]{:S(2)}) collective-permute-start(bf16[256,128]{1,0:T(8,128)(2,1)S(1)} %get-tuple-element.19), channel_id=1, source_target_pairs={{16,0},{32,16},{48,32},{64,48},{80,64},{96,80},{112,96},{128,112},... | collective-permute-start | bytes 196616 | tf_op jit(solution)/shard_map/ppermute | solution.py:244
  102.7 1.2 %copy-start.7 = (bf16[256,2048]{1,0:T(8,128)(2,1)S(1)}, bf16[256,2048]{1,0:T(8,128)(2,1)}, u32[]{:S(2)}) copy-start(bf16[256,2048]{1,0:T(8,128)(2,1)} %copy-done.6) | copy-start | bytes 3145732

commit v2 on v1

v2 whole, which is shorter than its diff:
```python
import functools

import jax
import jax.numpy as jnp
from jax import lax
from jax.experimental import pallas as pl
from jax.experimental.pallas import tpu as pltpu
from jax.sharding import PartitionSpec as P

EPSILON = 1e-05
GELU_ROOT = 0.7978845608028654
GELU_CUBIC = 0.044715

BF = jnp.bfloat16
F32 = jnp.float32
ROWS = 32
VMEM_LIMIT = 16 * 2**20


def hbm(count):
    return [pl.BlockSpec(memory_space=pltpu.HBM)] * count


def vmem(count):
    return [pl.BlockSpec(memory_space=pltpu.VMEM)] * count


def dot(left, right, dims=((1,), (0,))):
    return lax.dot_general(left, right, (dims, ((), ())), preferred_element_type=F32)


def gelu_parts(values):
    inner = GELU_ROOT * (values + GELU_CUBIC * values * values * values)
    return jnp.tanh(inner)


def split_three(values):
    high = values.astype(BF)
    rest = values - high.astype(F32)
    middle = rest.astype(BF)
    return high, middle, (rest - middle.astype(F32)).astype(BF)


def columns_to_rows(columns):
    tokens = columns[0].shape[0]
    lane = lax.broadcasted_iota(jnp.int32, (tokens, 128), 1)
    wide = jnp.zeros((tokens, 128), F32)
    for index, column in enumerate(columns):
        wide = jnp.where(lane == index, column, wide)
    tall = wide.T[:8]
    return jnp.concatenate([stack_parts(tall[:, :128]), stack_parts(tall[:, 128:])], axis=0)


def stack_parts(rows):
    high, middle, low = (part.astype(F32) for part in split_three(rows[:4]))
    return jnp.concatenate([high, middle, low, jnp.zeros_like(high)], axis=0).astype(BF)


def add_parts(rows):
    halves = [rows[at : at + 4] + rows[at + 4 : at + 8] + rows[at + 8 : at + 12] for at in (0, 16)]
    return jnp.concatenate(halves, axis=1)


def both_cores(me, near, far):
    return jnp.concatenate([jnp.where(me == 0, near, far), jnp.where(me == 0, far, near)], axis=1)


def norm_stats(blocks, width):
    total, squares = 0.0, 0.0
    for block in blocks:
        value = block.astype(F32)
        total += value
        squares += value * value
    center = jnp.sum(total, axis=1, keepdims=True) / width
    second = jnp.sum(squares, axis=1, keepdims=True) / width
    return center, lax.rsqrt(second - center * center + EPSILON)


def chip_cols(chip):
    return slice(chip * 256, chip * 256 + 256)


def forward_kernel(core, near, far, gain, weight_a, weight_b, packed):
    me = core[0]
    chips, _, tokens, _ = near.shape
    hidden_units = weight_a.shape[1]
    center, scale = norm_stats([side[chip, 0] for chip in range(chips) for side in (near, far)], 256 * chips)
    pre = jnp.zeros((tokens, hidden_units), F32)
    act_grad = jnp.zeros((tokens, hidden_units), F32)
    for chip in range(chips):
        value = both_cores(me, near[chip, 0], far[chip, 0]).astype(F32)
        normed = ((value - center) * scale * gain[:, chip_cols(chip)]).astype(BF)
        pre += dot(normed, weight_a[chip_cols(chip), :])
        grad = both_cores(me, near[chip, 1], far[chip, 1])
        act_grad += dot(grad, weight_b[:, chip_cols(chip)], ((1,), (1,)))
    packed[:tokens, :hidden_units] = act_grad
    packed[:tokens, hidden_units:] = (0.5 * pre * (1.0 + gelu_parts(pre))).astype(BF).astype(F32)
    parts = [part.astype(F32) for part in split_three(gain[...])]
    gains = jnp.concatenate(parts + [jnp.zeros((13, gain.shape[1]), F32)], axis=0).astype(BF)
    gained = dot(gains, weight_a[...])
    packed[tokens:, :hidden_units] = jnp.broadcast_to(gained[0:1] + gained[1:2] + gained[2:3], (8, hidden_units))


def side_parts(side, act, pre_grad, weight_a, weight_b, parts):
    chips = parts.shape[0]
    tokens = act.shape[0]
    for chip in range(0, chips, 2):
        starts = [pl.multiple_of((chip + step) * 256 + side * 128, 128) for step in range(2)]
        columns = jnp.concatenate([weight_b[:, pl.ds(start, 128)] for start in starts], axis=1)
        branch = dot(act, columns).astype(BF)
        rows = jnp.concatenate([weight_a[pl.ds(start, 128), :] for start in starts], axis=0)
        term = dot(pre_grad, rows, ((1,), (1,))).astype(BF)
        for step in range(2):
            parts[chip + step, :tokens, :] = branch[:, step * 128 : step * 128 + 128]
            parts[chip + step, tokens : 2 * tokens, :] = term[:, step * 128 : step * 128 + 128]


def backward_kernel(core, near, far, packed, gain, weight_a, weight_b, other, normed_out, small):
    me = core[0]
    chips, tokens, _ = near.shape
    hidden_units = weight_a.shape[1]
    width = 256 * chips
    center, scale = norm_stats([side[chip] for chip in range(chips) for side in (near, far)], width)
    pre = jnp.zeros((tokens, hidden_units), F32)
    for chip in range(chips):
        hidden = (both_cores(me, near[chip], far[chip]).astype(F32) - center) * scale
        normed = (hidden * gain[:, chip_cols(chip)]).astype(BF)
        normed_out[:, chip_cols(chip)] = normed
        pre += dot(normed, weight_a[chip_cols(chip), :])
    tangent = gelu_parts(pre)
    slope = 0.5 * (1.0 + tangent) + 0.5 * pre * (1.0 - tangent * tangent) * GELU_ROOT * (
        1.0 + 3.0 * GELU_CUBIC * pre * pre
    )
    pre_grad = (packed[:tokens, :hidden_units] * slope).astype(BF)
    small[:tokens, :hidden_units] = pre_grad
    small[:tokens, hidden_units:] = (0.5 * pre * (1.0 + tangent)).astype(BF)
    wide_grad = pre_grad.astype(F32)
    plain = jnp.sum(wide_grad * packed[tokens : tokens + 1, :hidden_units], axis=1, keepdims=True)
    moment = jnp.sum(wide_grad * pre, axis=1, keepdims=True)
    share = 1.0 / (2 * chips)
    rows = columns_to_rows([plain * (1.0 / width), moment * (1.0 / width), center * share, scale * share])
    small[tokens:, :128] = rows
    for chip in range(chips):
        other[chip, 2 * tokens :, :] = rows
    side_parts(1 - me, packed[:tokens, hidden_units:].astype(BF), pre_grad, weight_a, weight_b, other)


def own_kernel(core, normed, small, packed, grad_near, grad_far, weight_a, weight_b, own, grad_a, grad_b, keep_a, keep_b, sems):
    me = core[0]
    chips, _, tokens, _ = grad_near.shape
    hidden_units = weight_a.shape[1]
    pre_grad = small[:tokens, :hidden_units]
    act = small[:tokens, hidden_units:]
    for chip in range(chips):
        cols = chip_cols(chip)
        keep_a[cols, :] = dot(normed[:, cols], pre_grad, ((0,), (0,))).astype(BF)
        grad = both_cores(me, grad_near[chip, 1], grad_far[chip, 1])
        keep_b[:, cols] = dot(act, grad, ((0,), (0,))).astype(BF)
    stores = [
        pltpu.make_async_copy(keep_a, grad_a, sems.at[0]),
        pltpu.make_async_copy(keep_b, grad_b, sems.at[1]),
    ]
    for store in stores:
        store.start()
    for chip in range(chips):
        own[chip, 2 * tokens :, :] = small[tokens:, :128]
    side_parts(me, packed[:tokens, hidden_units:].astype(BF), pre_grad, weight_a, weight_b, own)
    for store in stores:
        store.wait()


def pair_kernel(own, received, total):
    body = own.shape[1] - ROWS
    total[0, :body, :] = (own[0, :body, :].astype(F32) + received[0, :body, :].astype(F32)).astype(BF)
    sums = add_parts(own[0, body:, :].astype(F32)) + add_parts(received[0, body:, :].astype(F32))
    total[0, body:, :] = jnp.concatenate([stack_parts(sums[:, :128]), stack_parts(sums[:, 128:])], axis=0)


def chip_total(parts):
    total = parts[0].astype(F32)
    for chip in range(1, parts.shape[0]):
        total += parts[chip].astype(F32)
    return total


def finish_kernel(parts, forward_in, grad_out, fetched, gain, outputs, input_grad):
    tokens = grad_out.shape[0]
    total = chip_total(parts)
    outputs[...] = (forward_in[...].astype(F32) + total[:tokens]).astype(BF)
    scaled = total[tokens : 2 * tokens] * gain[...]
    sums = add_parts(total[2 * tokens :])
    tall = jnp.concatenate([sums, jnp.zeros((124, tokens), F32)], axis=0).T
    plain_mean, moment_mean, center, scale = (tall[:, index : index + 1] for index in range(4))
    hidden = (fetched[...].astype(F32) - center) * scale
    input_grad[...] = (
        grad_out[...].astype(F32) + scale * (scaled - plain_mean - hidden * moment_mean)
    ).astype(BF)


def store_kernel(*refs):
    count = (len(refs) - 1) // 2
    copies = [pltpu.make_async_copy(refs[i], refs[count + i], refs[-1].at[i]) for i in range(count)]
    for copy in copies:
        copy.start()
    for copy in copies:
        copy.wait()


def call(kernel, out_shapes, operands, specs=None, out_specs=None, scratch=(), grid=(), flops=0, nbytes=0):
    return pl.pallas_call(
        kernel,
        out_shape=out_shapes,
        in_specs=specs or vmem(len(operands)),
        out_specs=tuple(out_specs or vmem(len(out_shapes))),
        scratch_shapes=list(scratch),
        grid=grid,
        compiler_params=pltpu.CompilerParams(vmem_limit_bytes=VMEM_LIMIT),
        cost_estimate=pl.CostEstimate(flops=flops, bytes_accessed=nbytes, transcendentals=0),
    )(*operands)


def per_device(inputs, out_grads, parked_store, fetch_slot, norm_gain, weight_in, weight_out):
    forward_in = inputs[0]
    grad_out = out_grads[0]
    weight_a = weight_in[0]
    weight_b = weight_out[0]
    tokens, shard_cols = forward_in.shape
    sections, ranks = lax.axis_size("section"), lax.axis_size("tensor")
    chips = ranks // 2
    width = shard_cols * ranks
    hidden_units = weight_a.shape[1]
    rank = lax.axis_index("tensor")
    core = lax.rem(rank, 2)
    same_core = [[2 * chip + side for chip in range(chips)] for side in range(2)]
    mirror = [(s, sections - 1 - s) for s in range(sections)]
    swap = [(t, t ^ 1) for t in range(ranks)]

    returned = lax.dynamic_index_in_dim(parked_store[0], fetch_slot[0], 0, keepdims=False)
    fetched = lax.ppermute(returned, "section", mirror)
    parked = lax.ppermute(forward_in, "section", mirror)

    def over_chips(blocks):
        return lax.all_to_all(blocks, "tensor", 0, 0, tiled=True, axis_index_groups=same_core)

    def gather(mine):
        near = over_chips(jnp.broadcast_to(mine[None], (chips,) + mine.shape))
        return near, lax.ppermute(near, "tensor", swap)

    shape = jax.ShapeDtypeStruct
    which = core.reshape(1)
    smem = [pl.BlockSpec(memory_space=pltpu.SMEM)]

    index = lax.broadcasted_iota(jnp.int32, (chips, 2, tokens, shard_cols), 1)
    spread = jnp.where(index == 0, forward_in[None, None], grad_out[None, None])
    near = over_chips(spread)
    back_spread = jnp.broadcast_to(fetched[None], (chips,) + fetched.shape)
    near, back_spread = lax.optimization_barrier((near, back_spread))
    far = lax.ppermute(near, "tensor", swap)
    packed = call(
        forward_kernel,
        (shape((tokens + 8, 2 * hidden_units), F32),),
        (which, near, far, norm_gain, weight_a, weight_b),
        specs=smem + vmem(5),
        flops=4 * tokens * width * hidden_units,
        nbytes=4 * 2**20,
    )[0]

    back_near = over_chips(back_spread)
    back_near, packed = lax.optimization_barrier((back_near, packed))
    back_far = lax.ppermute(back_near, "tensor", swap)
    both_parts = shape((chips, 2 * tokens + ROWS, 128), BF)
    normed_shape = shape((tokens, width), BF)
    small_shape = shape((tokens + ROWS, 2 * hidden_units), BF)
    other, normed, small = call(
        backward_kernel,
        (both_parts, normed_shape, small_shape),
        (which, back_near, back_far, packed, norm_gain, weight_a, weight_b),
        specs=smem + vmem(6),
        flops=4 * tokens * width * hidden_units,
        nbytes=6 * 2**20,
    )
    received = lax.ppermute(other, "tensor", swap)
    own, grad_a, grad_b = call(
        own_kernel,
        (both_parts, shape(weight_a.shape, BF), shape(weight_b.shape, BF)),
        (which, normed, small, packed, near, far, weight_a, weight_b),
        specs=smem + vmem(7),
        out_specs=vmem(1) + hbm(2),
        scratch=(
            pltpu.VMEM(weight_a.shape, BF),
            pltpu.VMEM(weight_b.shape, BF),
            pltpu.SemaphoreType.DMA((2,)),
        ),
        flops=6 * tokens * width * hidden_units,
        nbytes=8 * 2**20,
    )

    one_chip = pl.BlockSpec((1, both_parts.shape[1], 128), lambda chip: (chip, 0, 0))
    summed = call(
        pair_kernel, (both_parts,), (own, received), specs=[one_chip] * 2, out_specs=[one_chip], grid=(chips,), nbytes=3 * 2**20
    )[0]
    collected = over_chips(summed)
    kept = lax.dynamic_index_in_dim(back_near, rank // 2, 0, keepdims=False)
    gain_part = lax.dynamic_slice_in_dim(norm_gain, rank * shard_cols, shard_cols, 1)
    piece = shape((tokens, shard_cols), BF)
    outputs, input_grad = call(
        finish_kernel,
        (piece, piece),
        (collected, forward_in, grad_out, kept, gain_part),
        nbytes=2 * 2**20,
    )
    arrivals = lax.ppermute(outputs, "section", [(s, s + 1) for s in range(sections - 1)])
    sent_grads = lax.ppermute(input_grad, "section", [(s + 1, s) for s in range(sections - 1)])

    def store(*values):
        count = len(values)
        return call(
            store_kernel,
            [shape(value.shape, value.dtype) for value in values],
            values,
            out_specs=hbm(count),
            scratch=(pltpu.SemaphoreType.DMA((count,)),),
            nbytes=count * 2**17,
        )

    parked = store(parked)[0]
    arrivals, sent_grads = store(arrivals, sent_grads)
    return (arrivals[None], sent_grads[None], parked[None], grad_a[None], grad_b[None])


def solution(mesh):
    return jax.shard_map(
        per_device,
        mesh=mesh,
        in_specs=(
            P("section", None, "tensor"),
            P("section", None, "tensor"),
            P("section", None, None, "tensor"),
            P("section"),
            P("section", None),
            P("section", None, "tensor"),
            P("section", "tensor", None),
        ),
        out_specs=(
            P("section", None, "tensor"),
            P("section", None, "tensor"),
            P("section", None, "tensor"),
            P("section", None, "tensor"),
            P("section", "tensor", None),
        ),
        check_vma=False,
    )
```

time: 110 us -> 99.3 us (0.903)
  blocking collectives: 28.6 us -> 0 us
  starting transfers between devices: 27.6 us -> 48.4 us
  local copies, waits for them, and re-layouts: 12.3 us -> 3.6 us
  Pallas kernels: 9.17 us -> 13.6 us
  other arithmetic: 0.89 us -> 2.03 us
    all_to_all x1 -> x0, blocking collectives: 28.6 us -> none  [per_device(): lax.all_to_all(spread, 'tensor', 0, 0, tiled=True, axis_index_groups=same...]
    all_to_all x1 -> x3, starting transfers between devices: 4.5 us -> 16.2 us  [over_chips(): lax.all_to_all(blocks, 'tensor', 0, 0, tiled=True, axis_index_groups=same...]
    unnamed x41 -> x16, local copies, waits for them, and re-layouts: 11.9 us -> 1.87 us
    ppermute x1, starting transfers between devices: 1.92 us -> 8.22 us  [per_device(): parked = lax.ppermute(forward_in, 'section', mirror)]
    pallas_call x4 -> x7, Pallas kernels: 9.17 us -> 13.6 us  [call(): pl.pallas_call(kernel, out_shape=out_shapes, in_specs=specs or vmem(len(o...]
    ppermute x1, waiting for transfers between devices: 3.37 us -> 0.01 us  [per_device(): far = lax.ppermute(near, 'tensor', swap)]
    ppermute x1, waiting for transfers between devices: 1.35 us -> 4.19 us  [per_device(): lax.ppermute(input_grad, 'section', [(s + 1, s) for s in range(sections -...]
    ppermute x1, waiting for transfers between devices: 2.55 us -> 0.01 us  [per_device(): received = lax.ppermute(other, 'tensor', swap)]
  transfers between devices with their start and end apart: 7 -> 10, of which waited for: 5 -> 5; matrix products, arithmetic and copies ran while one was open for 0% -> 1% of each run, Pallas kernels for 3% -> 7%
where the time goes in v2:
time: 99.3 us; the launch traced here: 98.6 us
  starting transfers between devices  48.4 us (49%)
  waiting for transfers between devices  29.4 us (30%)
  Pallas kernels  13.6 us (14%)
  local copies, waits for them, and re-layouts  3.6 us (4%)
  other arithmetic  2.03 us (2%)
  between operations  1.61 us (2%)
    all_to_all x3, waiting for transfers between devices, over_chips(): lax.all_to_all(blocks, 'tensor', 0, 0, tiled=True, axis_index_groups=same...  17.1 us
    all_to_all x3, starting transfers between devices, over_chips(): lax.all_to_all(blocks, 'tensor', 0, 0, tiled=True, axis_index_groups=same...  16.2 us
    pallas_call x7, Pallas kernels, call(): pl.pallas_call(kernel, out_shape=out_shapes, in_specs=specs or vmem(len(o...  13.6 us
    ppermute x1, starting transfers between devices, per_device(): fetched = lax.ppermute(returned, 'section', mirror)  12.3 us
    ppermute x1, starting transfers between devices, per_device(): parked = lax.ppermute(forward_in, 'section', mirror)  8.22 us
    ppermute x1, waiting for transfers between devices, per_device(): fetched = lax.ppermute(returned, 'section', mirror)  6.01 us
    ppermute x1, waiting for transfers between devices, per_device(): lax.ppermute(input_grad, 'section', [(s + 1, s) for s in range(sections -...  4.19 us
    ppermute x1, starting transfers between devices, per_device(): lax.ppermute(outputs, 'section', [(s, s + 1) for s in range(sections - 1)])  3.65 us
  transfers between devices with their start and end apart: 10, of which 5 were waited for; matrix products, arithmetic and copies ran while one was open for 1% of the time, Pallas kernels for 7%

profile of v2, /device:TPU:2, one launch (start us, length us, event | category | flops | bytes accessed | tf_op | source)
XLA Modules:
  0.0 98.6 jit_solution(9573760954268897103)
XLA Ops:
  0.6 0.0 copy-start
  0.7 2.0 %broadcast_select_fusion = bf16[8,2,256,128]{3,2,1,0:T(8,128)(2,1)} fusion(pred[2]{0:T(512)(128)(4,1)S(1)} %iota_compare_fusion, bf16[256,128]{1,0:T(8,128)(2,1)} %bitcast.24, bf16[256,128]{1,0:T(8,128)(2,1)} %bitcast.26), kind=kLoop, calls=%fused_computation | loop fusion | flops 524288 | bytes 1179650 | tf_op jit(solution)/shard_map/jit(_where)/select_n | solution.py:254
  2.7 0.0 copy-start.2
  2.7 6.2 %all-to-all-start = ((bf16[8,2,256,128]{3,2,1,0:T(8,128)(2,1)}), bf16[8,2,256,128]{3,2,1,0:T(8,128)(2,1)S(1)}, u32[]{:S(2)}, u32[]{:S(2)}) async-start(bf16[8,2,256,128]{3,2,1,0:T(8,128)(2,1)} %broadcast_select_fusion), calls=%async_computation | async-start | bytes 2097152 | tf_op jit(solution)/shard_map/all_to_all | solution.py:243
  8.8 0.0 copy-start.1
  8.8 0.0 copy-start.7
  9.6 0.0 copy-done
  9.6 12.3 %collective-permute-start = (bf16[256,128]{1,0:T(8,128)(2,1)S(1)}, bf16[256,128]{1,0:T(8,128)(2,1)S(1)}, u32[]{:S(2)}, u32[]{:S(2)}) collective-permute-start(bf16[256,128]{1,0:T(8,128)(2,1)S(1)} %dynamic-slice_bitcast_fusion.1), channel_id=1, source_target_pairs={{0,496},{16,480},{32,464},{48,448},{64,432},{80,416},{96,400},{112... | collective-permute-start | bytes 196616 | tf_op jit(solution)/shard_map/ppermute | solution.py:239
  21.9 6.0 %collective-permute-done = bf16[256,128]{1,0:T(8,128)(2,1)S(1)} collective-permute-done((bf16[256,128]{1,0:T(8,128)(2,1)S(1)}, bf16[256,128]{1,0:T(8,128)(2,1)S(1)}, u32[]{:S(2)}, u32[]{:S(2)}) %collective-permute-start) | collective-permute-done | bytes 65568 | tf_op jit(solution)/shard_map/ppermute | solution.py:239
  27.9 0.0 all-to-all-done.near.grad_near
  27.9 0.9 broadcast_in_dim.45
  28.8 1.9 %collective-permute-start.1 = (bf16[8,2,256,128]{3,2,1,0:T(8,128)(2,1)S(1)}, bf16[8,2,256,128]{3,2,1,0:T(8,128)(2,1)}, u32[]{:S(2)}, u32[]{:S(2)}) collective-permute-start(bf16[8,2,256,128]{3,2,1,0:T(8,128)(2,1)S(1)} %all-to-all-done.near.grad_near), channel_id=1, source_target_pairs={{0,1},{1,0},{2,3},{3,2},{4,5},{5,4},{6,7},{7,6},{8,9},{9,8},{10,11... | collective-permute-start | bytes 3145736 | tf_op jit(solution)/shard_map/ppermute | solution.py:258
  30.7 6.3 %all-to-all-start.1 = ((bf16[8,256,128]{2,1,0:T(8,128)(2,1)}), bf16[8,256,128]{2,1,0:T(8,128)(2,1)}, u32[]{:S(2)}, u32[]{:S(2)}) async-start(bf16[8,256,128]{2,1,0:T(8,128)(2,1)} %broadcast_in_dim.45), calls=%async_computation.1 | async-start | bytes 1048576 | tf_op jit(solution)/shard_map/all_to_all | solution.py:243
  37.0 0.0 collective-permute-done.1.far.grad_far
  37.0 0.0 copy-done.2
  37.0 0.0 copy-done.1
  37.1 0.0 copy-done.7
  37.1 2.7 %shard_map.110.packed = f32[264,512]{1,0:T(8,128)S(1)} custom-call(s32[1]{0:T(128)} %bitcast.core, bf16[8,2,256,128]{3,2,1,0:T(8,128)(2,1)S(1)} %all-to-all-done.near.grad_near, bf16[8,2,256,128]{3,2,1,0:T(8,128)(2,1)} %collective-permute-done.1.far.grad_far, f32[1,2048]{1,0:T(1,128)S(1)} %copy-done.7, bf16[2048,256]{1,0:T(8,128)(2,1)S(1)} %bitcast.18, ...), custom_call_target="tpu_custom_call" | custom-call | flops 536870912 | bytes 4194304 | tf_op jit(solution)/shard_map/pallas_call | solution.py:210
  39.8 0.0 copy-start.3
  39.8 0.8 copy-done.3
  40.6 8.2 %all-to-all-done.1.near = bf16[8,256,128]{2,1,0:T(8,128)(2,1)} async-done(((bf16[8,256,128]{2,1,0:T(8,128)(2,1)}), bf16[8,256,128]{2,1,0:T(8,128)(2,1)}, u32[]{:S(2)}, u32[]{:S(2)}) %all-to-all-start.1) | async-done | bytes 524320 | tf_op jit(solution)/shard_map/all_to_all | solution.py:243
  48.7 1.9 %collective-permute-start.2 = (bf16[8,256,128]{2,1,0:T(8,128)(2,1)}, bf16[8,256,128]{2,1,0:T(8,128)(2,1)S(1)}, u32[]{:S(2)}, u32[]{:S(2)}) collective-permute-start(bf16[8,256,128]{2,1,0:T(8,128)(2,1)} %all-to-all-done.1.near), channel_id=1, source_target_pairs={{0,1},{1,0},{2,3},{3,2},{4,5},{5,4},{6,7},{7,6},{8,9},{9,8},{10,11... | collective-permute-start | bytes 1572872 | tf_op jit(solution)/shard_map/ppermute | solution.py:270
  50.6 2.1 %collective-permute-done.2.far = bf16[8,256,128]{2,1,0:T(8,128)(2,1)S(1)} collective-permute-done((bf16[8,256,128]{2,1,0:T(8,128)(2,1)}, bf16[8,256,128]{2,1,0:T(8,128)(2,1)S(1)}, u32[]{:S(2)}, u32[]{:S(2)}) %collective-permute-start.2) | collective-permute-done | bytes 524320 | tf_op jit(solution)/shard_map/ppermute | solution.py:270
  52.7 0.0 copy-start.4
  52.7 1.0 %copy-done.4 = f32[264,512]{1,0:T(8,128)S(1)} copy-done((f32[264,512]{1,0:T(8,128)S(1)}, f32[264,512]{1,0:T(8,128)}, u32[]{:S(2)}) %copy-start.4) | copy-done | bytes 540696
  53.8 2.9 %shard_map.111 = (bf16[8,544,128]{2,1,0:T(8,128)(2,1)S(1)}, bf16[256,2048]{1,0:T(8,128)(2,1)S(1)}, bf16[288,512]{1,0:T(8,128)(2,1)S(1)}) custom-call(s32[1]{0:T(128)} %bitcast.core, bf16[8,256,128]{2,1,0:T(8,128)(2,1)} %all-to-all-done.1.near, bf16[8,256,128]{2,1,0:T(8,128)(2,1)S(1)} %collective-permute-done.2.far, f32[264,512]{1,0:T(8,128)S(1)} %copy-done.4, ...), custom_call_target="tpu_custom_call" | custom-call | flops 536870912 | bytes 6291456 | tf_op jit(solution)/shard_map/pallas_call | solution.py:210
  56.7 2.0 %collective-permute-start.3 = (bf16[8,544,128]{2,1,0:T(8,128)(2,1)S(1)}, bf16[8,544,128]{2,1,0:T(8,128)(2,1)S(1)}, u32[]{:S(2)}, u32[]{:S(2)}) collective-permute-start(bf16[8,544,128]{2,1,0:T(8,128)(2,1)S(1)} %get-tuple-element.26), channel_id=1, source_target_pairs={{0,1},{1,0},{2,3},{3,2},{4,5},{5,4},{6,7},{7,6},{8,9},{9,8},{10,11... | collective-permute-start | bytes 3342344 | tf_op jit(solution)/shard_map/ppermute | solution.py:282
  58.7 3.4 %shard_map.112 = (bf16[8,544,128]{2,1,0:T(8,128)(2,1)S(1)}, bf16[2048,256]{1,0:T(8,128)(2,1)}, bf16[256,2048]{1,0:T(8,128)(2,1)}) custom-call(s32[1]{0:T(128)} %bitcast.core, bf16[256,2048]{1,0:T(8,128)(2,1)S(1)} %get-tuple-element.23.normed, bf16[288,512]{1,0:T(8,128)(2,1)S(1)} %get-tuple-element.24.small, f32[264,512]{1,0:T(8,128)S(1)} %copy-done.4, ...), custom_call_target="tpu_custom_call" | custom-call | flops 805306368 | bytes 8388608 | tf_op jit(solution)/shard_map/pallas_call | solution.py:210
  62.1 0.0 collective-permute-done.3.received
  62.1 2.9 %shard_map.113 = bf16[8,544,128]{2,1,0:T(8,128)(2,1)} custom-call(bf16[8,544,128]{2,1,0:T(8,128)(2,1)S(1)} %get-tuple-element.25.own, bf16[8,544,128]{2,1,0:T(8,128)(2,1)S(1)} %collective-permute-done.3.received), custom_call_target="tpu_custom_call" | custom-call | bytes 3145728 | tf_op jit(solution)/shard_map/pallas_call | solution.py:210
  65.0 0.0 copy-start.6
  65.0 0.0 copy-start.5
  65.0 3.7 %all-to-all-start.2 = ((bf16[8,544,128]{2,1,0:T(8,128)(2,1)}), bf16[8,544,128]{2,1,0:T(8,128)(2,1)S(1)}, u32[]{:S(2)}, u32[]{:S(2)}) async-start(bf16[8,544,128]{2,1,0:T(8,128)(2,1)} %shard_map.113), calls=%async_computation.2 | async-start | bytes 2228224 | tf_op jit(solution)/shard_map/all_to_all | solution.py:243
  68.7 0.0 copy-done.6
  68.7 8.2 %collective-permute-start.6 = (bf16[256,128]{1,0:T(8,128)(2,1)S(1)}, bf16[256,128]{1,0:T(8,128)(2,1)S(1)}, u32[]{:S(2)}, u32[]{:S(2)}) collective-permute-start(bf16[256,128]{1,0:T(8,128)(2,1)S(1)} %bitcast.27), channel_id=1, source_target_pairs={{0,496},{16,480},{32,464},{48,448},{64,432},{80,416},{96,400},{112... | collective-permute-start | bytes 196616 | tf_op jit(solution)/shard_map/ppermute | solution.py:240
  77.0 0.9 dynamic-slice_bitcast_fusion.fetched
  77.8 8.9 %all-to-all-done.2.parts = bf16[8,544,128]{2,1,0:T(8,128)(2,1)S(1)} async-done(((bf16[8,544,128]{2,1,0:T(8,128)(2,1)}), bf16[8,544,128]{2,1,0:T(8,128)(2,1)S(1)}, u32[]{:S(2)}, u32[]{:S(2)}) %all-to-all-start.2) | async-done | bytes 1114144 | tf_op jit(solution)/shard_map/all_to_all | solution.py:243
  86.7 0.0 copy-done.5
  86.7 0.5 shard_map.114
  87.2 3.6 %collective-permute-start.4 = (bf16[256,128]{1,0:T(8,128)(2,1)S(1)}, bf16[256,128]{1,0:T(8,128)(2,1)S(1)}, u32[]{:S(2)}, u32[]{:S(2)}) collective-permute-start(bf16[256,128]{1,0:T(8,128)(2,1)S(1)} %get-tuple-element.27), channel_id=1, source_target_pairs={{0,16},{16,32},{32,48},{48,64},{64,80},{80,96},{96,112},{112,128},... | collective-permute-start | bytes 196616 | tf_op jit(solution)/shard_map/ppermute | solution.py:312
  90.8 2.2 %collective-permute-start.5 = (bf16[256,128]{1,0:T(8,128)(2,1)S(1)}, bf16[256,128]{1,0:T(8,128)(2,1)S(1)}, u32[]{:S(2)}, u32[]{:S(2)}) collective-permute-start(bf16[256,128]{1,0:T(8,128)(2,1)S(1)} %get-tuple-element.28), channel_id=1, source_target_pairs={{16,0},{32,16},{48,32},{64,48},{80,64},{96,80},{112,96},{128,112},... | collective-permute-start | bytes 196616 | tf_op jit(solution)/shard_map/ppermute | solution.py:313
  93.0 0.0 collective-permute-done.6.refs_0_
  93.1 0.6 shard_map.116
  93.7 0.0 collective-permute-done.4.refs_0_
  93.7 4.2 %collective-permute-done.5.refs_1_ = bf16[256,128]{1,0:T(8,128)(2,1)S(1)} collective-permute-done((bf16[256,128]{1,0:T(8,128)(2,1)S(1)}, bf16[256,128]{1,0:T(8,128)(2,1)S(1)}, u32[]{:S(2)}, u32[]{:S(2)}) %collective-permute-start.5) | collective-permute-done | bytes 65568 | tf_op jit(solution)/shard_map/ppermute | solution.py:313
  97.9 0.7 shard_map.115
  (3 shorter events, 0.0 us)
Async XLA Ops:
  0.6 9.0 %copy-start = (bf16[1,2,256,128]{3,2,1,0:T(8,128)(2,1)S(1)}, bf16[1,2,256,128]{3,2,1,0:T(8,128)(2,1)}, u32[]{:S(2)}) copy-start(bf16[1,2,256,128]{3,2,1,0:T(8,128)(2,1)} %param.9) | copy-start | bytes 393220
  2.7 34.4 %copy-start.2 = (bf16[1,256,2048]{2,1,0:T(8,128)(2,1)S(1)}, bf16[1,256,2048]{2,1,0:T(8,128)(2,1)}, u32[]{:S(2)}) copy-start(bf16[1,256,2048]{2,1,0:T(8,128)(2,1)} %param.13) | copy-start | bytes 3145732
  2.7 25.2 %all-to-all-start = ((bf16[8,2,256,128]{3,2,1,0:T(8,128)(2,1)}), bf16[8,2,256,128]{3,2,1,0:T(8,128)(2,1)S(1)}, u32[]{:S(2)}, u32[]{:S(2)}) async-start(bf16[8,2,256,128]{3,2,1,0:T(8,128)(2,1)} %broadcast_select_fusion), calls=%async_computation | async-start | bytes 2097152 | tf_op jit(solution)/shard_map/all_to_all | solution.py:243
  8.8 28.2 %copy-start.1 = (bf16[1,2048,256]{2,1,0:T(8,128)(2,1)S(1)}, bf16[1,2048,256]{2,1,0:T(8,128)(2,1)}, u32[]{:S(2)}) copy-start(bf16[1,2048,256]{2,1,0:T(8,128)(2,1)} %param.12) | copy-start | bytes 3145732
  8.8 28.2 %copy-start.7 = (f32[1,2048]{1,0:T(1,128)S(1)}, f32[1,2048]{1,0:T(1,128)}, u32[]{:S(2)}) copy-start(f32[1,2048]{1,0:T(1,128)} %gain.3) | copy-start | bytes 24580
  9.6 18.3 %collective-permute-start = (bf16[256,128]{1,0:T(8,128)(2,1)S(1)}, bf16[256,128]{1,0:T(8,128)(2,1)S(1)}, u32[]{:S(2)}, u32[]{:S(2)}) collective-permute-start(bf16[256,128]{1,0:T(8,128)(2,1)S(1)} %dynamic-slice_bitcast_fusion.1), channel_id=1, source_target_pairs={{0,496},{16,480},{32,464},{48,448},{64,432},{80,416},{96,400},{112... | collective-permute-start | bytes 196616 | tf_op jit(solution)/shard_map/ppermute | solution.py:239
  28.8 8.2 %collective-permute-start.1 = (bf16[8,2,256,128]{3,2,1,0:T(8,128)(2,1)S(1)}, bf16[8,2,256,128]{3,2,1,0:T(8,128)(2,1)}, u32[]{:S(2)}, u32[]{:S(2)}) collective-permute-start(bf16[8,2,256,128]{3,2,1,0:T(8,128)(2,1)S(1)} %all-to-all-done.near.grad_near), channel_id=1, source_target_pairs={{0,1},{1,0},{2,3},{3,2},{4,5},{5,4},{6,7},{7,6},{8,9},{9,8},{10,11... | collective-permute-start | bytes 3145736 | tf_op jit(solution)/shard_map/ppermute | solution.py:258
  30.7 18.0 %all-to-all-start.1 = ((bf16[8,256,128]{2,1,0:T(8,128)(2,1)}), bf16[8,256,128]{2,1,0:T(8,128)(2,1)}, u32[]{:S(2)}, u32[]{:S(2)}) async-start(bf16[8,256,128]{2,1,0:T(8,128)(2,1)} %broadcast_in_dim.45), calls=%async_computation.1 | async-start | bytes 1048576 | tf_op jit(solution)/shard_map/all_to_all | solution.py:243
  39.8 0.8 copy-start.3
  48.7 4.0 %collective-permute-start.2 = (bf16[8,256,128]{2,1,0:T(8,128)(2,1)}, bf16[8,256,128]{2,1,0:T(8,128)(2,1)S(1)}, u32[]{:S(2)}, u32[]{:S(2)}) collective-permute-start(bf16[8,256,128]{2,1,0:T(8,128)(2,1)} %all-to-all-done.1.near), channel_id=1, source_target_pairs={{0,1},{1,0},{2,3},{3,2},{4,5},{5,4},{6,7},{7,6},{8,9},{9,8},{10,11... | collective-permute-start | bytes 1572872 | tf_op jit(solution)/shard_map/ppermute | solution.py:270
  52.7 1.0 %copy-start.4 = (f32[264,512]{1,0:T(8,128)S(1)}, f32[264,512]{1,0:T(8,128)}, u32[]{:S(2)}) copy-start(f32[264,512]{1,0:T(8,128)} %copy-done.3) | copy-start | bytes 1622020
  56.7 5.4 %collective-permute-start.3 = (bf16[8,544,128]{2,1,0:T(8,128)(2,1)S(1)}, bf16[8,544,128]{2,1,0:T(8,128)(2,1)S(1)}, u32[]{:S(2)}, u32[]{:S(2)}) collective-permute-start(bf16[8,544,128]{2,1,0:T(8,128)(2,1)S(1)} %get-tuple-element.26), channel_id=1, source_target_pairs={{0,1},{1,0},{2,3},{3,2},{4,5},{5,4},{6,7},{7,6},{8,9},{9,8},{10,11... | collective-permute-start | bytes 3342344 | tf_op jit(solution)/shard_map/ppermute | solution.py:282
  65.0 3.7 %copy-start.6 = (bf16[1,256,128]{2,1,0:T(8,128)(2,1)S(1)}, bf16[1,256,128]{2,1,0:T(8,128)(2,1)}, u32[]{:S(2)}) copy-start(bf16[1,256,128]{2,1,0:T(8,128)(2,1)} %param.7) | copy-start | bytes 196612
  65.0 21.7 %copy-start.5 = (bf16[1,256,128]{2,1,0:T(8,128)(2,1)S(1)}, bf16[1,256,128]{2,1,0:T(8,128)(2,1)}, u32[]{:S(2)}) copy-start(bf16[1,256,128]{2,1,0:T(8,128)(2,1)} %param.8) | copy-start | bytes 196612
  65.0 21.7 %all-to-all-start.2 = ((bf16[8,544,128]{2,1,0:T(8,128)(2,1)}), bf16[8,544,128]{2,1,0:T(8,128)(2,1)S(1)}, u32[]{:S(2)}, u32[]{:S(2)}) async-start(bf16[8,544,128]{2,1,0:T(8,128)(2,1)} %shard_map.113), calls=%async_computation.2 | async-start | bytes 2228224 | tf_op jit(solution)/shard_map/all_to_all | solution.py:243
  68.7 24.3 %collective-permute-start.6 = (bf16[256,128]{1,0:T(8,128)(2,1)S(1)}, bf16[256,128]{1,0:T(8,128)(2,1)S(1)}, u32[]{:S(2)}, u32[]{:S(2)}) collective-permute-start(bf16[256,128]{1,0:T(8,128)(2,1)S(1)} %bitcast.27), channel_id=1, source_target_pairs={{0,496},{16,480},{32,464},{48,448},{64,432},{80,416},{96,400},{112... | collective-permute-start | bytes 196616 | tf_op jit(solution)/shard_map/ppermute | solution.py:240
  87.2 6.5 %collective-permute-start.4 = (bf16[256,128]{1,0:T(8,128)(2,1)S(1)}, bf16[256,128]{1,0:T(8,128)(2,1)S(1)}, u32[]{:S(2)}, u32[]{:S(2)}) collective-permute-start(bf16[256,128]{1,0:T(8,128)(2,1)S(1)} %get-tuple-element.27), channel_id=1, source_target_pairs={{0,16},{16,32},{32,48},{48,64},{64,80},{80,96},{96,112},{112,128},... | collective-permute-start | bytes 196616 | tf_op jit(solution)/shard_map/ppermute | solution.py:312
  90.8 7.1 %collective-permute-start.5 = (bf16[256,128]{1,0:T(8,128)(2,1)S(1)}, bf16[256,128]{1,0:T(8,128)(2,1)S(1)}, u32[]{:S(2)}, u32[]{:S(2)}) collective-permute-start(bf16[256,128]{1,0:T(8,128)(2,1)S(1)} %get-tuple-element.28), channel_id=1, source_target_pairs={{16,0},{32,16},{48,32},{64,48},{80,64},{96,80},{112,96},{128,112},... | collective-permute-start | bytes 196616 | tf_op jit(solution)/shard_map/ppermute | solution.py:313

commit v3 on v2

--- a/solution.py
+++ b/solution.py
@@ -138,42 +138,48 @@
     plain = jnp.sum(wide_grad * packed[tokens : tokens + 1, :hidden_units], axis=1, keepdims=True)
     moment = jnp.sum(wide_grad * pre, axis=1, keepdims=True)
     share = 1.0 / (2 * chips)
-    rows = columns_to_rows([plain * (1.0 / width), moment * (1.0 / width), center * share, scale * share])
+    rows = columns_to_rows([plain * (1.0 / width), moment * (1.0 / width), scale * share, jnp.zeros_like(scale)])
     small[tokens:, :128] = rows
     for chip in range(chips):
         other[chip, 2 * tokens :, :] = rows
     side_parts(1 - me, packed[:tokens, hidden_units:].astype(BF), pre_grad, weight_a, weight_b, other)
 
 
-def own_kernel(core, normed, small, packed, grad_near, grad_far, weight_a, weight_b, own, grad_a, grad_b, keep_a, keep_b, sems):
+def own_kernel(core, small, packed, weight_a, weight_b, own):
+    tokens = small.shape[0] - ROWS
+    hidden_units = weight_a.shape[1]
+    for chip in range(own.shape[0]):
+        own[chip, 2 * tokens :, :] = small[tokens:, :128]
+    act = packed[:tokens, hidden_units:].astype(BF)
+    side_parts(core[0], act, small[:tokens, :hidden_units], weight_a, weight_b, own)
+
+
+def weights_kernel(core, normed, small, grad_near, grad_far, grad_a, grad_b):
     me = core[0]
     chips, _, tokens, _ = grad_near.shape
-    hidden_units = weight_a.shape[1]
+    hidden_units = grad_a.shape[1]
     pre_grad = small[:tokens, :hidden_units]
     act = small[:tokens, hidden_units:]
     for chip in range(chips):
         cols = chip_cols(chip)
-        keep_a[cols, :] = dot(normed[:, cols], pre_grad, ((0,), (0,))).astype(BF)
+        grad_a[cols, :] = dot(normed[:, cols], pre_grad, ((0,), (0,))).astype(BF)
         grad = both_cores(me, grad_near[chip, 1], grad_far[chip, 1])
-        keep_b[:, cols] = dot(act, grad, ((0,), (0,))).astype(BF)
-    stores = [
-        pltpu.make_async_copy(keep_a, grad_a, sems.at[0]),
-        pltpu.make_async_copy(keep_b, grad_b, sems.at[1]),
-    ]
-    for store in stores:
-        store.start()
-    for chip in range(chips):
-        own[chip, 2 * tokens :, :] = small[tokens:, :128]
-    side_parts(me, packed[:tokens, hidden_units:].astype(BF), pre_grad, weight_a, weight_b, own)
-    for store in stores:
-        store.wait()
-
-
-def pair_kernel(own, received, total):
-    body = own.shape[1] - ROWS
-    total[0, :body, :] = (own[0, :body, :].astype(F32) + received[0, :body, :].astype(F32)).astype(BF)
+        grad_b[:, cols] = dot(act, grad, ((0,), (0,))).astype(BF)
+
+
+def pair_kernel(own, received, total, held, sems):
+    chips, rows, _ = own.shape
+    body = rows - ROWS
     sums = add_parts(own[0, body:, :].astype(F32)) + add_parts(received[0, body:, :].astype(F32))
-    total[0, body:, :] = jnp.concatenate([stack_parts(sums[:, :128]), stack_parts(sums[:, 128:])], axis=0)
+    sums = jnp.concatenate([stack_parts(sums[:, :128]), stack_parts(sums[:, 128:])], axis=0)
+    copies = []
+    for chip in range(chips):
+        held[chip, :body, :] = (own[chip, :body, :].astype(F32) + received[chip, :body, :].astype(F32)).astype(BF)
+        held[chip, body:, :] = sums
+        copies.append(pltpu.make_async_copy(held.at[chip], total.at[chip], sems.at[chip]))
+        copies[-1].start()
+    for copy in copies:
+        copy.wait()
 
 
 def chip_total(parts):
@@ -183,18 +189,21 @@
     return total
 
 
-def finish_kernel(parts, forward_in, grad_out, fetched, gain, outputs, input_grad):
+def finish_kernel(odd_ref, parts, forward_in, grad_out, normed, gain, inside, across):
     tokens = grad_out.shape[0]
     total = chip_total(parts)
-    outputs[...] = (forward_in[...].astype(F32) + total[:tokens]).astype(BF)
+    outputs = (forward_in[...].astype(F32) + total[:tokens]).astype(BF)
     scaled = total[tokens : 2 * tokens] * gain[...]
     sums = add_parts(total[2 * tokens :])
     tall = jnp.concatenate([sums, jnp.zeros((124, tokens), F32)], axis=0).T
-    plain_mean, moment_mean, center, scale = (tall[:, index : index + 1] for index in range(4))
-    hidden = (fetched[...].astype(F32) - center) * scale
-    input_grad[...] = (
+    plain_mean, moment_mean, scale = (tall[:, index : index + 1] for index in range(3))
+    hidden = normed[...].astype(F32) / gain[...]
+    input_grad = (
         grad_out[...].astype(F32) + scale * (scaled - plain_mean - hidden * moment_mean)
     ).astype(BF)
+    odd = odd_ref[0] == 1
+    inside[...] = jnp.where(odd, input_grad, outputs)
+    across[...] = jnp.where(odd, outputs, input_grad)
 
 
 def store_kernel(*refs):
@@ -204,6 +213,21 @@
         copy.start()
     for copy in copies:
         copy.wait()
+
+
+def store_pair_kernel(odd_ref, across, inside, arrivals, sent_grads, sems):
+    for odd in range(2):
+
+        @pl.when(odd_ref[0] == odd)
+        def _():
+            copies = [
+                pltpu.make_async_copy(inside, arrivals if odd else sent_grads, sems.at[0]),
+                pltpu.make_async_copy(across, sent_grads if odd else arrivals, sems.at[1]),
+            ]
+            for copy in copies:
+                copy.start()
+            for copy in copies:
+                copy.wait()
 
 
 def call(kernel, out_shapes, operands, specs=None, out_specs=None, scratch=(), grid=(), flops=0, nbytes=0):
@@ -266,7 +290,6 @@
     )[0]
 
     back_near = over_chips(back_spread)
-    back_near, packed = lax.optimization_barrier((back_near, packed))
     back_far = lax.ppermute(back_near, "tensor", swap)
     both_parts = shape((chips, 2 * tokens + ROWS, 128), BF)
     normed_shape = shape((tokens, width), BF)
@@ -280,37 +303,46 @@
         nbytes=6 * 2**20,
     )
     received = lax.ppermute(other, "tensor", swap)
-    own, grad_a, grad_b = call(
+    own = call(
         own_kernel,
-        (both_parts, shape(weight_a.shape, BF), shape(weight_b.shape, BF)),
-        (which, normed, small, packed, near, far, weight_a, weight_b),
-        specs=smem + vmem(7),
-        out_specs=vmem(1) + hbm(2),
-        scratch=(
-            pltpu.VMEM(weight_a.shape, BF),
-            pltpu.VMEM(weight_b.shape, BF),
-            pltpu.SemaphoreType.DMA((2,)),
-        ),
-        flops=6 * tokens * width * hidden_units,
-        nbytes=8 * 2**20,
-    )
-
-    one_chip = pl.BlockSpec((1, both_parts.shape[1], 128), lambda chip: (chip, 0, 0))
+        (both_parts,),
+        (which, small, packed, weight_a, weight_b),
+        specs=smem + vmem(4),
+        flops=2 * tokens * width * hidden_units,
+        nbytes=4 * 2**20,
+    )[0]
+    grad_a, grad_b = call(
+        weights_kernel,
+        (shape(weight_a.shape, BF), shape(weight_b.shape, BF)),
+        (which, normed, small, near, far),
+        specs=smem + vmem(4),
+        flops=4 * tokens * width * hidden_units,
+        nbytes=6 * 2**20,
+    )
+
     summed = call(
-        pair_kernel, (both_parts,), (own, received), specs=[one_chip] * 2, out_specs=[one_chip], grid=(chips,), nbytes=3 * 2**20
+        pair_kernel,
+        (both_parts,),
+        (own, received),
+        out_specs=hbm(1),
+        scratch=(pltpu.VMEM(both_parts.shape, BF), pltpu.SemaphoreType.DMA((chips,))),
+        nbytes=3 * 2**20,
     )[0]
     collected = over_chips(summed)
-    kept = lax.dynamic_index_in_dim(back_near, rank // 2, 0, keepdims=False)
+    collected, grad_a, grad_b = lax.optimization_barrier((collected, grad_a, grad_b))
+    kept = lax.dynamic_slice_in_dim(normed, rank * shard_cols, shard_cols, 1)
     gain_part = lax.dynamic_slice_in_dim(norm_gain, rank * shard_cols, shard_cols, 1)
     piece = shape((tokens, shard_cols), BF)
-    outputs, input_grad = call(
+    section_odd = lax.rem(lax.axis_index("section"), 2).reshape(1)
+    inside, across = call(
         finish_kernel,
         (piece, piece),
-        (collected, forward_in, grad_out, kept, gain_part),
+        (section_odd, collected, forward_in, grad_out, kept, gain_part),
+        specs=smem + vmem(5),
         nbytes=2 * 2**20,
     )
-    arrivals = lax.ppermute(outputs, "section", [(s, s + 1) for s in range(sections - 1)])
-    sent_grads = lax.ppermute(input_grad, "section", [(s + 1, s) for s in range(sections - 1)])
+    inside = lax.ppermute(inside, "section", [(s, s ^ 1) for s in range(sections)])
+    across = lax.ppermute(across, "section", [(s, s + 1 if s % 2 else s - 1) for s in range(1, sections - 1)])
 
     def store(*values):
         count = len(values)
@@ -324,7 +356,15 @@
         )
 
     parked = store(parked)[0]
-    arrivals, sent_grads = store(arrivals, sent_grads)
+    arrivals, sent_grads = call(
+        store_pair_kernel,
+        (piece, piece),
+        (section_odd, across, inside),
+        specs=smem + vmem(2),
+        out_specs=hbm(2),
+        scratch=(pltpu.SemaphoreType.DMA((2,)),),
+        nbytes=2**18,
+    )
     return (arrivals[None], sent_grads[None], parked[None], grad_a[None], grad_b[None])
 
 

time: 99.3 us -> 94.8 us (0.955)
  blocking collectives: 0 us -> 18.3 us
  waiting for transfers between devices: 29.4 us -> 17.4 us
  starting transfers between devices: 48.4 us -> 41.6 us
  local copies, waits for them, and re-layouts: 3.6 us -> 1.12 us
  Pallas kernels: 13.6 us -> 12.1 us
    all_to_all x0 -> x1, blocking collectives: none -> 18.3 us  [over_chips(): lax.all_to_all(blocks, 'tensor', 0, 0, tiled=True, axis_index_groups=same...]
    all_to_all x3 -> x2, waiting for transfers between devices: 17.1 us -> 5.98 us  [over_chips(): lax.all_to_all(blocks, 'tensor', 0, 0, tiled=True, axis_index_groups=same...]
    all_to_all x3 -> x2, starting transfers between devices: 16.2 us -> 9.87 us  [over_chips(): lax.all_to_all(blocks, 'tensor', 0, 0, tiled=True, axis_index_groups=same...]
    ppermute x1, waiting for transfers between devices: 2.09 us -> 0.01 us  [per_device(): back_far = lax.ppermute(back_near, 'tensor', swap)]
    ppermute x1, waiting for transfers between devices: 0.01 us -> 1.87 us  [per_device(): received = lax.ppermute(other, 'tensor', swap)]
    pallas_call x7 -> x8, Pallas kernels: 13.6 us -> 12.1 us  [call(): pl.pallas_call(kernel, out_shape=out_shapes, in_specs=specs or vmem(len(o...]
  transfers between devices with their start and end apart: 10 -> 9, of which waited for: 5 -> 5; matrix products, arithmetic and copies ran while one was open for 1% -> 0% of each run, Pallas kernels for 7% -> 8%
where the time goes in v3:
time: 94.8 us; the launch traced here: 94.2 us
  starting transfers between devices  41.6 us (44%)
  blocking collectives  18.3 us (19%)
  waiting for transfers between devices  17.4 us (18%)
  Pallas kernels  12.1 us (13%)
  other arithmetic  2.03 us (2%)
  between operations  1.67 us (2%)
  local copies, waits for them, and re-layouts  1.12 us (1%)
    all_to_all x1, blocking collectives, over_chips(): lax.all_to_all(blocks, 'tensor', 0, 0, tiled=True, axis_index_groups=same...  18.3 us
    ppermute x1, starting transfers between devices, per_device(): fetched = lax.ppermute(returned, 'section', mirror)  12.3 us
    pallas_call x8, Pallas kernels, call(): pl.pallas_call(kernel, out_shape=out_shapes, in_specs=specs or vmem(len(o...  12.1 us
    all_to_all x2, starting transfers between devices, over_chips(): lax.all_to_all(blocks, 'tensor', 0, 0, tiled=True, axis_index_groups=same...  9.87 us
    ppermute x1, starting transfers between devices, per_device(): parked = lax.ppermute(forward_in, 'section', mirror)  7.63 us
    ppermute x1, waiting for transfers between devices, per_device(): fetched = lax.ppermute(returned, 'section', mirror)  6.01 us
    all_to_all x2, waiting for transfers between devices, over_chips(): lax.all_to_all(blocks, 'tensor', 0, 0, tiled=True, axis_index_groups=same...  5.98 us
    ppermute x1, starting transfers between devices, per_device(): lax.ppermute(across, 'section', [(s, s + 1 if s % 2 else s - 1) for s in...  3.69 us
  transfers between devices with their start and end apart: 9, of which 5 were waited for; matrix products, arithmetic and copies ran while one was open for 0% of the time, Pallas kernels for 8%

profile of v3, /device:TPU:2, one launch (start us, length us, event | category | flops | bytes accessed | tf_op | source)
XLA Modules:
  0.0 94.2 jit_solution(15724665533679567078)
XLA Ops:
  0.6 0.0 copy-start
  0.7 2.0 %broadcast_select_fusion = bf16[8,2,256,128]{3,2,1,0:T(8,128)(2,1)} fusion(pred[2]{0:T(512)(128)(4,1)S(1)} %iota_compare_fusion, bf16[256,128]{1,0:T(8,128)(2,1)} %bitcast.23, bf16[256,128]{1,0:T(8,128)(2,1)} %bitcast.25), kind=kLoop, calls=%fused_computation | loop fusion | flops 524288 | bytes 1179650 | tf_op jit(solution)/shard_map/jit(_where)/select_n | solution.py:278
  2.7 0.0 copy-start.2
  2.7 6.2 %all-to-all-start = ((bf16[8,2,256,128]{3,2,1,0:T(8,128)(2,1)}), bf16[8,2,256,128]{3,2,1,0:T(8,128)(2,1)S(1)}, u32[]{:S(2)}, u32[]{:S(2)}) async-start(bf16[8,2,256,128]{3,2,1,0:T(8,128)(2,1)} %broadcast_select_fusion), calls=%async_computation | async-start | bytes 2097152 | tf_op jit(solution)/shard_map/all_to_all | solution.py:267
  8.8 0.0 copy-start.1
  8.8 0.0 copy-start.9
  9.6 0.0 copy-done
  9.6 12.3 %collective-permute-start = (bf16[256,128]{1,0:T(8,128)(2,1)S(1)}, bf16[256,128]{1,0:T(8,128)(2,1)S(1)}, u32[]{:S(2)}, u32[]{:S(2)}) collective-permute-start(bf16[256,128]{1,0:T(8,128)(2,1)S(1)} %dynamic-slice_bitcast_fusion), channel_id=1, source_target_pairs={{0,496},{16,480},{32,464},{48,448},{64,432},{80,416},{96,400},{112... | collective-permute-start | bytes 196616 | tf_op jit(solution)/shard_map/ppermute | solution.py:263
  21.9 6.0 %collective-permute-done = bf16[256,128]{1,0:T(8,128)(2,1)S(1)} collective-permute-done((bf16[256,128]{1,0:T(8,128)(2,1)S(1)}, bf16[256,128]{1,0:T(8,128)(2,1)S(1)}, u32[]{:S(2)}, u32[]{:S(2)}) %collective-permute-start) | collective-permute-done | bytes 65568 | tf_op jit(solution)/shard_map/ppermute | solution.py:263
  27.9 0.0 all-to-all-done.near.grad_near
  27.9 0.1 broadcast_in_dim.45
  28.0 1.9 %collective-permute-start.2 = (bf16[8,2,256,128]{3,2,1,0:T(8,128)(2,1)S(1)}, bf16[8,2,256,128]{3,2,1,0:T(8,128)(2,1)}, u32[]{:S(2)}, u32[]{:S(2)}) collective-permute-start(bf16[8,2,256,128]{3,2,1,0:T(8,128)(2,1)S(1)} %all-to-all-done.near.grad_near), channel_id=1, source_target_pairs={{0,1},{1,0},{2,3},{3,2},{4,5},{5,4},{6,7},{7,6},{8,9},{9,8},{10,11... | collective-permute-start | bytes 3145736 | tf_op jit(solution)/shard_map/ppermute | solution.py:282
  29.9 18.3 %all_to_all.15.near = bf16[8,256,128]{2,1,0:T(8,128)(2,1)} all-to-all(bf16[8,256,128]{2,1,0:T(8,128)(2,1)S(1)} %broadcast_in_dim.45), channel_id=1, replica_groups={{0,2,4,6,8,10,12,14},{1,3,5,7,9,11,13,15},{16,18,20,22,24,26,28,30},{17..., dimensions={0} | all-to-all | bytes 1048576 | tf_op jit(solution)/shard_map/all_to_all | solution.py:267
  48.2 1.9 %collective-permute-start.1 = (bf16[8,256,128]{2,1,0:T(8,128)(2,1)}, bf16[8,256,128]{2,1,0:T(8,128)(2,1)}, u32[]{:S(2)}, u32[]{:S(2)}) collective-permute-start(bf16[8,256,128]{2,1,0:T(8,128)(2,1)} %all_to_all.15.near), channel_id=1, source_target_pairs={{0,1},{1,0},{2,3},{3,2},{4,5},{5,4},{6,7},{7,6},{8,9},{9,8},{10,11... | collective-permute-start | bytes 1572872 | tf_op jit(solution)/shard_map/ppermute | solution.py:293
  50.1 0.0 collective-permute-done.2.far.grad_far
  50.1 0.0 copy-done.2
  50.1 0.0 copy-done.1
  50.1 0.0 copy-done.9
  50.2 2.5 %shard_map.110.packed = f32[264,512]{1,0:T(8,128)S(1)} custom-call(s32[1]{0:T(128)} %bitcast.1.core, bf16[8,2,256,128]{3,2,1,0:T(8,128)(2,1)S(1)} %all-to-all-done.near.grad_near, bf16[8,2,256,128]{3,2,1,0:T(8,128)(2,1)} %collective-permute-done.2.far.grad_far, f32[1,2048]{1,0:T(1,128)S(1)} %copy-done.9, bf16[2048,256]{1,0:T(8,128)(2,1)S(1)} %bitcast.17, ...), custom_call_target="tpu_custom_call" | custom-call | flops 536870912 | bytes 4194304 | tf_op jit(solution)/shard_map/pallas_call | solution.py:234
  52.7 0.0 collective-permute-done.1.far
  52.7 2.9 %shard_map.111 = (bf16[8,544,128]{2,1,0:T(8,128)(2,1)S(1)}, bf16[256,2048]{1,0:T(8,128)(2,1)S(1)}, bf16[288,512]{1,0:T(8,128)(2,1)S(1)}) custom-call(s32[1]{0:T(128)} %bitcast.1.core, bf16[8,256,128]{2,1,0:T(8,128)(2,1)} %all_to_all.15.near, bf16[8,256,128]{2,1,0:T(8,128)(2,1)} %collective-permute-done.1.far, f32[264,512]{1,0:T(8,128)S(1)} %shard_map.110.packed, ...), custom_call_target="tpu_custom_call" | custom-call | flops 536870912 | bytes 6291456 | tf_op jit(solution)/shard_map/pallas_call | solution.py:234
  55.6 0.0 copy-start.3
  55.6 0.0 copy-start.5
  55.7 2.4 %collective-permute-start.3 = (bf16[8,544,128]{2,1,0:T(8,128)(2,1)S(1)}, bf16[8,544,128]{2,1,0:T(8,128)(2,1)S(1)}, u32[]{:S(2)}, u32[]{:S(2)}) collective-permute-start(bf16[8,544,128]{2,1,0:T(8,128)(2,1)S(1)} %get-tuple-element.22), channel_id=1, source_target_pairs={{0,1},{1,0},{2,3},{3,2},{4,5},{5,4},{6,7},{7,6},{8,9},{9,8},{10,11... | collective-permute-start | bytes 3342344 | tf_op jit(solution)/shard_map/ppermute | solution.py:305
  58.1 0.5 shard_map.112.own
  58.5 0.0 copy-done.3
  58.6 0.0 copy-done.5
  58.6 1.9 %collective-permute-done.3.received = bf16[8,544,128]{2,1,0:T(8,128)(2,1)S(1)} collective-permute-done((bf16[8,544,128]{2,1,0:T(8,128)(2,1)S(1)}, bf16[8,544,128]{2,1,0:T(8,128)(2,1)S(1)}, u32[]{:S(2)}, u32[]{:S(2)}) %collective-permute-start.3) | collective-permute-done | bytes 1114144 | tf_op jit(solution)/shard_map/ppermute | solution.py:305
  60.4 1.1 %shard_map.113 = bf16[8,544,128]{2,1,0:T(8,128)(2,1)} custom-call(bf16[8,544,128]{2,1,0:T(8,128)(2,1)S(1)} %shard_map.112.own, bf16[8,544,128]{2,1,0:T(8,128)(2,1)S(1)} %collective-permute-done.3.received), custom_call_target="tpu_custom_call" | custom-call | bytes 3145728 | tf_op jit(solution)/shard_map/pallas_call | solution.py:234
  61.6 0.0 copy-start.8
  61.6 0.0 copy-start.4
  61.6 3.7 %all-to-all-start.2 = ((bf16[8,544,128]{2,1,0:T(8,128)(2,1)}), bf16[8,544,128]{2,1,0:T(8,128)(2,1)S(1)}, u32[]{:S(2)}, u32[]{:S(2)}) async-start(bf16[8,544,128]{2,1,0:T(8,128)(2,1)} %shard_map.113), calls=%async_computation.2 | async-start | bytes 2228224 | tf_op jit(solution)/shard_map/all_to_all | solution.py:267
  65.3 0.0 copy-done.8
  65.3 7.6 %collective-permute-start.6 = (bf16[256,128]{1,0:T(8,128)(2,1)S(1)}, bf16[256,128]{1,0:T(8,128)(2,1)S(1)}, u32[]{:S(2)}, u32[]{:S(2)}) collective-permute-start(bf16[256,128]{1,0:T(8,128)(2,1)S(1)} %bitcast.26), channel_id=1, source_target_pairs={{0,496},{16,480},{32,464},{48,448},{64,432},{80,416},{96,400},{112... | collective-permute-start | bytes 196616 | tf_op jit(solution)/shard_map/ppermute | solution.py:264
  73.0 0.0 copy-done.4
  73.0 0.0 copy-start.6
  73.0 1.0 %copy-done.6 = bf16[288,512]{1,0:T(8,128)(2,1)S(1)} copy-done((bf16[288,512]{1,0:T(8,128)(2,1)S(1)}, bf16[288,512]{1,0:T(8,128)(2,1)}, u32[]{:S(2)}) %copy-start.6) | copy-done | bytes 294936
  74.0 3.4 %shard_map.114 = (bf16[2048,256]{1,0:T(8,128)(2,1)}, bf16[256,2048]{1,0:T(8,128)(2,1)}) custom-call(s32[1]{0:T(128)} %bitcast.1.core, bf16[256,2048]{1,0:T(8,128)(2,1)S(1)} %copy-done.4, bf16[288,512]{1,0:T(8,128)(2,1)S(1)} %copy-done.6, bf16[8,2,256,128]{3,2,1,0:T(8,128)(2,1)S(1)} %all-to-all-done.near.grad_near, ...), custom_call_target="tpu_custom_call" | custom-call | flops 536870912 | bytes 6291456 | tf_op jit(solution)/shard_map/pallas_call | solution.py:234
  77.4 6.0 %all-to-all-done.2.parts = bf16[8,544,128]{2,1,0:T(8,128)(2,1)S(1)} async-done(((bf16[8,544,128]{2,1,0:T(8,128)(2,1)}), bf16[8,544,128]{2,1,0:T(8,128)(2,1)S(1)}, u32[]{:S(2)}, u32[]{:S(2)}) %all-to-all-start.2) | async-done | bytes 1114144 | tf_op jit(solution)/shard_map/all_to_all | solution.py:267
  83.3 0.0 copy-done.7
  83.3 0.4 shard_map.115
  83.7 3.7 %collective-permute-start.4 = (bf16[256,128]{1,0:T(8,128)(2,1)S(1)}, bf16[256,128]{1,0:T(8,128)(2,1)S(1)}, u32[]{:S(2)}, u32[]{:S(2)}) collective-permute-start(bf16[256,128]{1,0:T(8,128)(2,1)S(1)} %get-tuple-element.27), channel_id=1, source_target_pairs={{16,32},{32,16},{48,64},{64,48},{80,96},{96,80},{112,128},{128,112... | collective-permute-start | bytes 196616 | tf_op jit(solution)/shard_map/ppermute | solution.py:345
  87.4 1.9 %collective-permute-start.5 = (bf16[256,128]{1,0:T(8,128)(2,1)S(1)}, bf16[256,128]{1,0:T(8,128)(2,1)S(1)}, u32[]{:S(2)}, u32[]{:S(2)}) collective-permute-start(bf16[256,128]{1,0:T(8,128)(2,1)S(1)} %get-tuple-element.28), channel_id=1, source_target_pairs={{0,16},{16,0},{32,48},{48,32},{64,80},{80,64},{96,112},{112,96},{1... | collective-permute-start | bytes 196616 | tf_op jit(solution)/shard_map/ppermute | solution.py:344
  89.3 0.0 collective-permute-done.6.refs_0_
  89.3 0.6 shard_map.117
  90.0 0.8 collective-permute-done.4.across
  90.8 2.8 %collective-permute-done.5.inside = bf16[256,128]{1,0:T(8,128)(2,1)S(1)} collective-permute-done((bf16[256,128]{1,0:T(8,128)(2,1)S(1)}, bf16[256,128]{1,0:T(8,128)(2,1)S(1)}, u32[]{:S(2)}, u32[]{:S(2)}) %collective-permute-start.5) | collective-permute-done | bytes 65568 | tf_op jit(solution)/shard_map/ppermute | solution.py:344
  93.6 0.7 shard_map.116
  (5 shorter events, 0.0 us)
Async XLA Ops:
  0.6 9.0 %copy-start = (bf16[1,2,256,128]{3,2,1,0:T(8,128)(2,1)S(1)}, bf16[1,2,256,128]{3,2,1,0:T(8,128)(2,1)}, u32[]{:S(2)}) copy-start(bf16[1,2,256,128]{3,2,1,0:T(8,128)(2,1)} %param.9) | copy-start | bytes 393220
  2.7 47.5 %copy-start.2 = (bf16[1,256,2048]{2,1,0:T(8,128)(2,1)S(1)}, bf16[1,256,2048]{2,1,0:T(8,128)(2,1)}, u32[]{:S(2)}) copy-start(bf16[1,256,2048]{2,1,0:T(8,128)(2,1)} %param.13) | copy-start | bytes 3145732
  2.7 25.2 %all-to-all-start = ((bf16[8,2,256,128]{3,2,1,0:T(8,128)(2,1)}), bf16[8,2,256,128]{3,2,1,0:T(8,128)(2,1)S(1)}, u32[]{:S(2)}, u32[]{:S(2)}) async-start(bf16[8,2,256,128]{3,2,1,0:T(8,128)(2,1)} %broadcast_select_fusion), calls=%async_computation | async-start | bytes 2097152 | tf_op jit(solution)/shard_map/all_to_all | solution.py:267
  8.8 41.3 %copy-start.1 = (bf16[1,2048,256]{2,1,0:T(8,128)(2,1)S(1)}, bf16[1,2048,256]{2,1,0:T(8,128)(2,1)}, u32[]{:S(2)}) copy-start(bf16[1,2048,256]{2,1,0:T(8,128)(2,1)} %param.12) | copy-start | bytes 3145732
  8.8 41.3 %copy-start.9 = (f32[1,2048]{1,0:T(1,128)S(1)}, f32[1,2048]{1,0:T(1,128)}, u32[]{:S(2)}) copy-start(f32[1,2048]{1,0:T(1,128)} %gain.3) | copy-start | bytes 24580
  9.6 18.3 %collective-permute-start = (bf16[256,128]{1,0:T(8,128)(2,1)S(1)}, bf16[256,128]{1,0:T(8,128)(2,1)S(1)}, u32[]{:S(2)}, u32[]{:S(2)}) collective-permute-start(bf16[256,128]{1,0:T(8,128)(2,1)S(1)} %dynamic-slice_bitcast_fusion), channel_id=1, source_target_pairs={{0,496},{16,480},{32,464},{48,448},{64,432},{80,416},{96,400},{112... | collective-permute-start | bytes 196616 | tf_op jit(solution)/shard_map/ppermute | solution.py:263
  28.0 22.1 %collective-permute-start.2 = (bf16[8,2,256,128]{3,2,1,0:T(8,128)(2,1)S(1)}, bf16[8,2,256,128]{3,2,1,0:T(8,128)(2,1)}, u32[]{:S(2)}, u32[]{:S(2)}) collective-permute-start(bf16[8,2,256,128]{3,2,1,0:T(8,128)(2,1)S(1)} %all-to-all-done.near.grad_near), channel_id=1, source_target_pairs={{0,1},{1,0},{2,3},{3,2},{4,5},{5,4},{6,7},{7,6},{8,9},{9,8},{10,11... | collective-permute-start | bytes 3145736 | tf_op jit(solution)/shard_map/ppermute | solution.py:282
  48.2 4.5 %collective-permute-start.1 = (bf16[8,256,128]{2,1,0:T(8,128)(2,1)}, bf16[8,256,128]{2,1,0:T(8,128)(2,1)}, u32[]{:S(2)}, u32[]{:S(2)}) collective-permute-start(bf16[8,256,128]{2,1,0:T(8,128)(2,1)} %all_to_all.15.near), channel_id=1, source_target_pairs={{0,1},{1,0},{2,3},{3,2},{4,5},{5,4},{6,7},{7,6},{8,9},{9,8},{10,11... | collective-permute-start | bytes 1572872 | tf_op jit(solution)/shard_map/ppermute | solution.py:293
  55.6 2.9 %copy-start.3 = (bf16[256,2048]{1,0:T(8,128)(2,1)}, bf16[256,2048]{1,0:T(8,128)(2,1)S(1)}, u32[]{:S(2)}) copy-start(bf16[256,2048]{1,0:T(8,128)(2,1)S(1)} %get-tuple-element.23.normed) | copy-start | bytes 3145732
  55.6 2.9 %copy-start.5 = (bf16[288,512]{1,0:T(8,128)(2,1)}, bf16[288,512]{1,0:T(8,128)(2,1)S(1)}, u32[]{:S(2)}) copy-start(bf16[288,512]{1,0:T(8,128)(2,1)S(1)} %get-tuple-element.21.small) | copy-start | bytes 884740
  55.7 4.8 %collective-permute-start.3 = (bf16[8,544,128]{2,1,0:T(8,128)(2,1)S(1)}, bf16[8,544,128]{2,1,0:T(8,128)(2,1)S(1)}, u32[]{:S(2)}, u32[]{:S(2)}) collective-permute-start(bf16[8,544,128]{2,1,0:T(8,128)(2,1)S(1)} %get-tuple-element.22), channel_id=1, source_target_pairs={{0,1},{1,0},{2,3},{3,2},{4,5},{5,4},{6,7},{7,6},{8,9},{9,8},{10,11... | collective-permute-start | bytes 3342344 | tf_op jit(solution)/shard_map/ppermute | solution.py:305
  61.6 3.7 %copy-start.8 = (bf16[1,256,128]{2,1,0:T(8,128)(2,1)S(1)}, bf16[1,256,128]{2,1,0:T(8,128)(2,1)}, u32[]{:S(2)}) copy-start(bf16[1,256,128]{2,1,0:T(8,128)(2,1)} %param.7) | copy-start | bytes 196612
  61.6 11.4 %copy-start.4 = (bf16[256,2048]{1,0:T(8,128)(2,1)S(1)}, bf16[256,2048]{1,0:T(8,128)(2,1)}, u32[]{:S(2)}) copy-start(bf16[256,2048]{1,0:T(8,128)(2,1)} %copy-done.3) | copy-start | bytes 3145732
  61.6 21.7 %all-to-all-start.2 = ((bf16[8,544,128]{2,1,0:T(8,128)(2,1)}), bf16[8,544,128]{2,1,0:T(8,128)(2,1)S(1)}, u32[]{:S(2)}, u32[]{:S(2)}) async-start(bf16[8,544,128]{2,1,0:T(8,128)(2,1)} %shard_map.113), calls=%async_computation.2 | async-start | bytes 2228224 | tf_op jit(solution)/shard_map/all_to_all | solution.py:267
  65.3 24.0 %collective-permute-start.6 = (bf16[256,128]{1,0:T(8,128)(2,1)S(1)}, bf16[256,128]{1,0:T(8,128)(2,1)S(1)}, u32[]{:S(2)}, u32[]{:S(2)}) collective-permute-start(bf16[256,128]{1,0:T(8,128)(2,1)S(1)} %bitcast.26), channel_id=1, source_target_pairs={{0,496},{16,480},{32,464},{48,448},{64,432},{80,416},{96,400},{112... | collective-permute-start | bytes 196616 | tf_op jit(solution)/shard_map/ppermute | solution.py:264
  73.0 1.0 %copy-start.6 = (bf16[288,512]{1,0:T(8,128)(2,1)S(1)}, bf16[288,512]{1,0:T(8,128)(2,1)}, u32[]{:S(2)}) copy-start(bf16[288,512]{1,0:T(8,128)(2,1)} %copy-done.5) | copy-start | bytes 884740
  74.0 9.4 %copy-start.7 = (bf16[1,256,128]{2,1,0:T(8,128)(2,1)S(1)}, bf16[1,256,128]{2,1,0:T(8,128)(2,1)}, u32[]{:S(2)}) copy-start(bf16[1,256,128]{2,1,0:T(8,128)(2,1)} %param.8) | copy-start | bytes 196612
  83.7 7.1 %collective-permute-start.4 = (bf16[256,128]{1,0:T(8,128)(2,1)S(1)}, bf16[256,128]{1,0:T(8,128)(2,1)S(1)}, u32[]{:S(2)}, u32[]{:S(2)}) collective-permute-start(bf16[256,128]{1,0:T(8,128)(2,1)S(1)} %get-tuple-element.27), channel_id=1, source_target_pairs={{16,32},{32,16},{48,64},{64,48},{80,96},{96,80},{112,128},{128,112... | collective-permute-start | bytes 196616 | tf_op jit(solution)/shard_map/ppermute | solution.py:345
  87.4 6.2 %collective-permute-start.5 = (bf16[256,128]{1,0:T(8,128)(2,1)S(1)}, bf16[256,128]{1,0:T(8,128)(2,1)S(1)}, u32[]{:S(2)}, u32[]{:S(2)}) collective-permute-start(bf16[256,128]{1,0:T(8,128)(2,1)S(1)} %get-tuple-element.28), channel_id=1, source_target_pairs={{0,16},{16,0},{32,48},{48,32},{64,80},{80,64},{96,112},{112,96},{1... | collective-permute-start | bytes 196616 | tf_op jit(solution)/shard_map/ppermute | solution.py:344

commit v4 on v3

v4 whole, which is shorter than its diff:
```python
import functools

import jax
import jax.numpy as jnp
from jax import lax
from jax.experimental import pallas as pl
from jax.experimental.pallas import tpu as pltpu
from jax.sharding import PartitionSpec as P

EPSILON = 1e-05
GELU_ROOT = 0.7978845608028654
GELU_CUBIC = 0.044715

BF = jnp.bfloat16
F32 = jnp.float32
ROWS = 16
VMEM_LIMIT = 16 * 2**20


def hbm(count):
    return [pl.BlockSpec(memory_space=pltpu.HBM)] * count


def vmem(count):
    return [pl.BlockSpec(memory_space=pltpu.VMEM)] * count


def dot(left, right, dims=((1,), (0,))):
    return lax.dot_general(left, right, (dims, ((), ())), preferred_element_type=F32)


def gelu_parts(values):
    inner = GELU_ROOT * (values + GELU_CUBIC * values * values * values)
    return jnp.tanh(inner)


def split_three(values):
    high = values.astype(BF)
    rest = values - high.astype(F32)
    middle = rest.astype(BF)
    return high, middle, (rest - middle.astype(F32)).astype(BF)


def columns_to_rows(columns):
    lane = lax.broadcasted_iota(jnp.int32, (128, 128), 1)
    wide = jnp.zeros((128, 128), F32)
    for index, column in enumerate(columns):
        wide = jnp.where(lane == index, column, wide)
    high, middle, low = (part.astype(F32) for part in split_three(wide.T[:4]))
    return jnp.concatenate([high, middle, low, jnp.zeros_like(high)], axis=0).astype(BF)


def rows_to_columns(rows):
    sums = rows[0:4] + rows[4:8] + rows[8:12]
    tall = jnp.concatenate([sums, jnp.zeros((124, 128), F32)], axis=0).T
    return [tall[:, index : index + 1] for index in range(4)]


def norm_stats(blocks, width):
    total, squares = 0.0, 0.0
    for block in blocks:
        value = block.astype(F32)
        total += value
        squares += value * value
    center = jnp.sum(total, axis=1, keepdims=True) / width
    second = jnp.sum(squares, axis=1, keepdims=True) / width
    return center, lax.rsqrt(second - center * center + EPSILON)


def chip_cols(chip):
    return slice(chip * 256, chip * 256 + 256)


def gelu_slope(values, tangent):
    return 0.5 * (1.0 + tangent) + 0.5 * values * (1.0 - tangent * tangent) * GELU_ROOT * (
        1.0 + 3.0 * GELU_CUBIC * values * values
    )


def block_kernel(
    spent, blocks, back, gain, weight_b, weight_a, *refs
):
    del spent
    *far, parts, middle, held, normed_ref, near_a_ref, far_a_ref, far_b_ref, sems = refs
    ranks = blocks.shape[0]
    chips = ranks // 2
    tokens = back.shape[1]
    width = 128 * ranks
    units = weight_a.shape[1]
    near_load = pltpu.make_async_copy(weight_a, near_a_ref, sems.at[chips])
    loads = []
    for refs, place, axis in ((far[:-2], far_a_ref, 0), (far[-2:], far_b_ref, 1)):
        size = width // len(refs)
        for index, ref in enumerate(refs):
            part = slice(index * size, index * size + size)
            there = place.at[part, :] if axis == 0 else place.at[:, part]
            loads.append(pltpu.make_async_copy(ref, there, sems.at[chips + 1 + len(loads)]))
    near_load.start()
    for load in loads:
        load.start()
    firsts, seconds = (near_a_ref, far_a_ref), (weight_b, far_b_ref)

    def pair(ref, chip, rows):
        return jnp.concatenate([ref[2 * chip, rows, :], ref[2 * chip + 1, rows, :]], axis=1)

    def pass_of(ref, rows):
        center, scale = norm_stats([ref[rank, rows, :] for rank in range(ranks)], width)
        for chip in range(chips):
            cols = chip_cols(chip)
            normed_ref[:, cols] = ((pair(ref, chip, rows).astype(F32) - center) * scale * gain[:, cols]).astype(BF)
        return center, scale

    def put(index, side, value):
        start = (2 * index + side) * units
        middle[:tokens, start : start + units] = value.astype(BF)

    first_rows, second_rows = slice(0, tokens), slice(tokens, 2 * tokens)
    pass_of(blocks, first_rows)
    near_load.wait()
    act_grad = []
    for side in range(2):
        if side:
            for load in loads:
                load.wait()
        pre = dot(normed_ref[...], firsts[side][...])
        put(1, side, 0.5 * pre * (1.0 + gelu_parts(pre)))
        total = jnp.zeros((tokens, units), F32)
        for chip in range(chips):
            total += dot(pair(blocks, chip, second_rows), seconds[side][:, chip_cols(chip)], ((1,), (1,)))
        act_grad.append(total)
    parts_of_gain = [part.astype(F32) for part in split_three(gain[...])]
    gains = jnp.concatenate(parts_of_gain + [jnp.zeros((13, gain.shape[1]), F32)], axis=0).astype(BF)

    center, scale = pass_of(back, first_rows)
    plain, moment = 0.0, 0.0
    for side in range(2):
        pre = dot(normed_ref[...], firsts[side][...])
        tangent = gelu_parts(pre)
        pre_grad = (act_grad[side] * gelu_slope(pre, tangent)).astype(BF)
        put(0, side, pre_grad)
        put(2, side, 0.5 * pre * (1.0 + tangent))
        gained = dot(gains, firsts[side][...])
        wide = pre_grad.astype(F32)
        plain += jnp.sum(wide * (gained[0:1] + gained[1:2] + gained[2:3]), axis=1, keepdims=True)
        moment += jnp.sum(wide * pre, axis=1, keepdims=True)
    share = 1.0 / chips
    rows = columns_to_rows([plain * (1.0 / width), moment * (1.0 / width), center * share, scale * share])
    copies = []
    for chip in range(chips):
        cols = chip_cols(chip)
        branch, term = 0.0, 0.0
        for side in range(2):
            pre_grad = middle[:, side * units : side * units + units]
            act = middle[:, (2 + side) * units : (3 + side) * units]
            branch += dot(act, seconds[side][:, cols])
            term += dot(pre_grad, firsts[side][cols, :], ((1,), (1,)))
        for side in range(2):
            lanes = slice(side * 128, side * 128 + 128)
            held[2 * chip + side, :tokens, :] = branch[:, lanes].astype(BF)
            held[2 * chip + side, tokens : 2 * tokens, :] = term[:, lanes].astype(BF)
            held[2 * chip + side, 2 * tokens :, :] = rows
        both = slice(2 * chip, 2 * chip + 2)
        copies.append(pltpu.make_async_copy(held.at[both], parts.at[both], sems.at[chip]))
        copies[-1].start()
    for copy in copies:
        copy.wait()


def trade_kernel(blocks, back, middle, gain, trade, grads):
    ranks, tokens, _ = back.shape
    width = 128 * ranks
    units = middle.shape[1] // 6
    center, scale = norm_stats([back[rank] for rank in range(ranks)], width)
    for chip in range(ranks // 2):
        cols = chip_cols(chip)
        value = jnp.concatenate([back[2 * chip], back[2 * chip + 1]], axis=1).astype(F32)
        trade[:, cols] = ((value - center) * scale * gain[:, cols]).astype(BF)
        grads[:, cols] = jnp.concatenate([blocks[2 * chip + side, tokens : 2 * tokens, :] for side in range(2)], axis=1)
    trade[:, width : width + units] = middle[:, units : 2 * units]
    trade[:, width + units :] = middle[:, 5 * units :]


def weights_kernel(trade, received, middle, grads, far_grads, grad_a, grad_b, keep_a, keep_b, sems):
    width = grads.shape[1]
    units = grad_a.shape[1]
    pre_grad = jnp.concatenate([middle[:, :units], received[:, width : width + units]], axis=0)
    act = jnp.concatenate([middle[:, 4 * units : 5 * units], received[:, width + units :]], axis=0)
    stores = []
    for chip in range(width // 256):
        cols = chip_cols(chip)
        normed = jnp.concatenate([trade[:, cols], received[:, cols]], axis=0)
        keep_a[cols, :] = dot(normed, pre_grad, ((0,), (0,))).astype(BF)
        grad = jnp.concatenate([grads[:, cols], far_grads[:, cols]], axis=0)
        keep_b[:, cols] = dot(act, grad, ((0,), (0,))).astype(BF)
        stores.append(pltpu.make_async_copy(keep_a.at[cols, :], grad_a.at[cols, :], sems.at[2 * chip]))
        stores.append(pltpu.make_async_copy(keep_b.at[:, cols], grad_b.at[:, cols], sems.at[2 * chip + 1]))
        for store in stores[-2:]:
            store.start()
    for store in stores:
        store.wait()


def finish_kernel(odd_ref, parts, forward_in, grad_out, fetched, gain, inside, across):
    ranks, rows, _ = parts.shape
    tokens = (rows - ROWS) // 2
    odd = odd_ref[0] == 1
    for side in range(2):
        total = parts[side].astype(F32)
        for rank in range(2 + side, ranks, 2):
            total += parts[rank].astype(F32)
        here = slice(side * tokens, side * tokens + tokens)
        outputs = (forward_in[here, :].astype(F32) + total[:tokens]).astype(BF)
        scaled = total[tokens : 2 * tokens] * gain[...]
        plain_mean, moment_mean, center, scale = rows_to_columns(total[2 * tokens :])
        hidden = (fetched[side].astype(F32) - center) * scale
        input_grad = (
            grad_out[here, :].astype(F32) + scale * (scaled - plain_mean - hidden * moment_mean)
        ).astype(BF)
        inside[here, :] = jnp.where(odd, input_grad, outputs)
        across[here, :] = jnp.where(odd, outputs, input_grad)


def store_kernel(*refs):
    count = (len(refs) - 1) // 2
    copies = [pltpu.make_async_copy(refs[i], refs[count + i], refs[-1].at[i]) for i in range(count)]
    for copy in copies:
        copy.start()
    for copy in copies:
        copy.wait()


def store_pair_kernel(odd_ref, across, inside, arrivals, sent_grads, sems):
    for odd in range(2):

        @pl.when(odd_ref[0] == odd)
        def _():
            copies = [
                pltpu.make_async_copy(inside, arrivals if odd else sent_grads, sems.at[0]),
                pltpu.make_async_copy(across, sent_grads if odd else arrivals, sems.at[1]),
            ]
            for copy in copies:
                copy.start()
            for copy in copies:
                copy.wait()


def call(kernel, out_shapes, operands, specs=None, out_specs=None, scratch=(), aliases=None, limit=VMEM_LIMIT, flops=0, nbytes=0):
    return pl.pallas_call(
        kernel,
        out_shape=out_shapes,
        in_specs=specs or vmem(len(operands)),
        out_specs=tuple(out_specs or vmem(len(out_shapes))),
        scratch_shapes=list(scratch),
        input_output_aliases=aliases or {},
        compiler_params=pltpu.CompilerParams(vmem_limit_bytes=limit),
        cost_estimate=pl.CostEstimate(flops=flops, bytes_accessed=nbytes, transcendentals=0),
    )(*operands)


def per_device(inputs, out_grads, parked_store, fetch_slot, norm_gain, weight_in, weight_out):
    forward_in = inputs[0]
    grad_out = out_grads[0]
    weight_a = weight_in[0]
    weight_b = weight_out[0]
    tokens, shard_cols = forward_in.shape
    sections, ranks = lax.axis_size("section"), lax.axis_size("tensor")
    chips = ranks // 2
    width = shard_cols * ranks
    hidden_units = weight_a.shape[1]
    rank = lax.axis_index("tensor")
    half = tokens // 2
    mirror = [(s, sections - 1 - s) for s in range(sections)]
    swap = [(t, t ^ 1) for t in range(ranks)]

    returned = lax.dynamic_index_in_dim(parked_store[0], fetch_slot[0], 0, keepdims=False)
    fetched = lax.ppermute(returned, "section", mirror)
    parked = lax.ppermute(forward_in, "section", mirror)

    shape = jax.ShapeDtypeStruct
    smem = [pl.BlockSpec(memory_space=pltpu.SMEM)]

    def exchange(blocks):
        return lax.all_to_all(blocks, "tensor", 0, 0, tiled=True)

    pieces = (weight_a, weight_b[:, : width // 2], weight_b[:, width // 2 :])
    far = [lax.ppermute(piece, "tensor", swap) for piece in pieces]
    mine = jnp.stack([value.reshape(2, half, shard_cols) for value in (forward_in, grad_out)], axis=1)
    mine = jnp.pad(mine.reshape(2, tokens, shard_cols), ((0, 0), (0, ROWS), (0, 0)))
    spread = jnp.broadcast_to(mine[None], (chips,) + mine.shape).reshape((ranks,) + mine.shape[1:])
    blocks = exchange(spread)
    back_spread = jnp.broadcast_to(fetched.reshape(1, 2, half, shard_cols), (chips, 2, half, shard_cols))
    blocks, back_spread = lax.optimization_barrier((blocks, back_spread.reshape(ranks, half, shard_cols)))

    back = exchange(back_spread)
    parts, middle = call(
        block_kernel,
        (shape(spread.shape, BF), shape((half, 6 * hidden_units), BF)),
        (spread, blocks, back, norm_gain, weight_b, weight_a, *far),
        specs=hbm(1) + vmem(4) + hbm(1 + len(far)),
        out_specs=hbm(1) + vmem(1),
        scratch=(
            pltpu.VMEM(spread.shape, BF),
            pltpu.VMEM((half, width), BF),
            pltpu.VMEM(weight_a.shape, BF),
            pltpu.VMEM(weight_a.shape, BF),
            pltpu.VMEM(weight_b.shape, BF),
            pltpu.SemaphoreType.DMA((chips + 1 + len(far),)),
        ),
        aliases={0: 0},
        flops=10 * tokens * width * hidden_units,
        nbytes=10 * 2**20,
    )

    collected = exchange(parts)
    trade, grads = call(
        trade_kernel,
        (shape((half, width + 2 * hidden_units), BF), shape((half, width), BF)),
        (blocks, back, middle, norm_gain),
        nbytes=4 * 2**20,
    )
    grad_a, grad_b = call(
        weights_kernel,
        (shape(weight_a.shape, BF), shape(weight_b.shape, BF)),
        (trade, lax.ppermute(trade, "tensor", swap), middle, grads, lax.ppermute(grads, "tensor", swap)),
        out_specs=hbm(2),
        scratch=(
            pltpu.VMEM(weight_a.shape, BF),
            pltpu.VMEM(weight_b.shape, BF),
            pltpu.SemaphoreType.DMA((2 * chips,)),
        ),
        flops=4 * tokens * width * hidden_units,
        nbytes=6 * 2**20,
    )
    collected, grad_a, grad_b = lax.optimization_barrier((collected, grad_a, grad_b))
    gain_part = lax.dynamic_slice_in_dim(norm_gain, rank * shard_cols, shard_cols, 1)
    piece = shape((tokens, shard_cols), BF)
    kept = back_spread[:2]

    section_odd = lax.rem(lax.axis_index("section"), 2).reshape(1)
    inside, across = call(
        finish_kernel,
        (piece, piece),
        (section_odd, collected, forward_in, grad_out, kept, gain_part),
        specs=smem + vmem(5),
        nbytes=2 * 2**20,
    )
    inside = lax.ppermute(inside, "section", [(s, s ^ 1) for s in range(sections)])
    across = lax.ppermute(across, "section", [(s, s + 1 if s % 2 else s - 1) for s in range(1, sections - 1)])

    def store(*values):
        count = len(values)
        return call(
            store_kernel,
            [shape(value.shape, value.dtype) for value in values],
            values,
            out_specs=hbm(count),
            scratch=(pltpu.SemaphoreType.DMA((count,)),),
            nbytes=count * 2**17,
        )

    parked = store(parked)[0]
    arrivals, sent_grads = call(
        store_pair_kernel,
        (piece, piece),
        (section_odd, across, inside),
        specs=smem + vmem(2),
        out_specs=hbm(2),
        scratch=(pltpu.SemaphoreType.DMA((2,)),),
        nbytes=2**18,
    )
    return (arrivals[None], sent_grads[None], parked[None], grad_a[None], grad_b[None])


def solution(mesh):
    return jax.shard_map(
        per_device,
        mesh=mesh,
        in_specs=(
            P("section", None, "tensor"),
            P("section", None, "tensor"),
            P("section", None, None, "tensor"),
            P("section"),
            P("section", None),
            P("section", None, "tensor"),
            P("section", "tensor", None),
        ),
        out_specs=(
            P("section", None, "tensor"),
            P("section", None, "tensor"),
            P("section", None, "tensor"),
            P("section", None, "tensor"),
            P("section", "tensor", None),
        ),
        check_vma=False,
    )
```

time: 94.8 us -> 90.3 us (0.953)
  the two profiles are of different devices: /device:TPU:2 before, /device:TPU:98 now
where the time goes in v4:
time: 90.3 us; the launch traced here: 89.6 us
  starting transfers between devices  55.9 us (62%)
  waiting for transfers between devices  16.1 us (18%)
  Pallas kernels  11.1 us (12%)
  local copies, waits for them, and re-layouts  4.01 us (4%)
  between operations  1.54 us (2%)
  other arithmetic  0.92 us (1%)
    all_to_all x3, starting transfers between devices, exchange(): return lax.all_to_all(blocks, 'tensor', 0, 0, tiled=True)  16.3 us
    all_to_all x3, waiting for transfers between devices, exchange(): return lax.all_to_all(blocks, 'tensor', 0, 0, tiled=True)  12.5 us
    ppermute x1, starting transfers between devices, per_device(): fetched = lax.ppermute(returned, 'section', mirror)  12.2 us
    pallas_call x6, Pallas kernels, call(): pl.pallas_call(kernel, out_shape=out_shapes, in_specs=specs or vmem(len(o...  11.1 us
    ppermute x1, starting transfers between devices, per_device(): parked = lax.ppermute(forward_in, 'section', mirror)  8.98 us
    ppermute x3, starting transfers between devices, per_device(): far = [lax.ppermute(piece, 'tensor', swap) for piece in pieces]  6.76 us
    ppermute x1, starting transfers between devices, per_device(): lax.ppermute(across, 'section', [(s, s + 1 if s % 2 else s - 1) for s in...  5.32 us
    ppermute x1, waiting for transfers between devices, per_device(): lax.ppermute(inside, 'section', [(s, s ^ 1) for s in range(sections)])  3.21 us
  transfers between devices with their start and end apart: 12, of which 4 were waited for; matrix products, arithmetic and copies ran while one was open for 3% of the time, Pallas kernels for 6%

profile of v4, /device:TPU:98, one launch (start us, length us, event | category | flops | bytes accessed | tf_op | source)
XLA Modules:
  0.0 89.6 jit_solution(10426657201389652845)
XLA Ops:
  0.6 0.0 copy-start
  0.6 0.9 %pad_maximum_fusion = bf16[2,2,128,128]{3,2,1,0:T(8,128)(2,1)S(1)} fusion(bf16[2,1,128,128]{3,2,1,0:T(8,128)(2,1)} %bitcast.24, bf16[2,1,128,128]{3,2,1,0:T(8,128)(2,1)} %bitcast.26), kind=kLoop, calls=%fused_computation | loop fusion | flops 65536 | bytes 262144 | tf_op jit(solution)/shard_map/stack | solution.py:287
  1.6 1.2 %broadcast_in_dim.28 = bf16[8,2,272,128]{3,2,1,0:T(8,128)(2,1)} broadcast(bf16[2,272,128]{2,1,0:T(8,128)(2,1)S(1)} %pad.4), dimensions={1,2,3} | broadcast | bytes 1253376 | tf_op jit(solution)/shard_map/broadcast_in_dim | solution.py:289
  2.8 0.0 copy-start.1
  2.8 6.3 %all-to-all-start = ((bf16[16,272,128]{2,1,0:T(8,128)(2,1)}), bf16[16,272,128]{2,1,0:T(8,128)(2,1)S(1)}, u32[]{:S(2)}, u32[]{:S(2)}) async-start(bf16[16,272,128]{2,1,0:T(8,128)(2,1)} %bitcast.4.spent), calls=%async_computation | async-start | bytes 2228224 | tf_op jit(solution)/shard_map/all_to_all | solution.py:283
  9.0 2.3 %collective-permute-start.1 = (bf16[2048,256]{1,0:T(8,128)(2,1)}, bf16[2048,256]{1,0:T(8,128)(2,1)}, u32[]{:S(2)}, u32[]{:S(2)}) collective-permute-start(bf16[2048,256]{1,0:T(8,128)(2,1)} %bitcast.10.weight_a), channel_id=1, source_target_pairs={{0,1},{1,0},{2,3},{3,2},{4,5},{5,4},{6,7},{7,6},{8,9},{9,8},{10,11... | collective-permute-start | bytes 3145736 | tf_op jit(solution)/shard_map/ppermute | solution.py:286
  12.0 0.0 copy-done
  12.0 12.2 %collective-permute-start = (bf16[256,128]{1,0:T(8,128)(2,1)S(1)}, bf16[256,128]{1,0:T(8,128)(2,1)S(1)}, u32[]{:S(2)}, u32[]{:S(2)}) collective-permute-start(bf16[256,128]{1,0:T(8,128)(2,1)S(1)} %dynamic-slice_bitcast_fusion), channel_id=1, source_target_pairs={{0,496},{16,480},{32,464},{48,448},{64,432},{80,416},{96,400},{112... | collective-permute-start | bytes 196616 | tf_op jit(solution)/shard_map/ppermute | solution.py:276
  24.3 0.0 copy-done.1
  24.3 1.0 %fusion = (bf16[256,1024]{1,0:T(8,128)(2,1)}, bf16[256,1024]{1,0:T(8,128)(2,1)}) fusion(bf16[256,2048]{1,0:T(8,128)(2,1)S(1)} %bitcast.22), kind=kLoop, calls=%fused_computation.3 | loop fusion | bytes 2097152 | tf_op jit(solution)/shard_map/slice | solution.py:285
  25.3 0.0 copy-start.4
  25.3 2.0 %collective-permute-start.3 = (bf16[256,1024]{1,0:T(8,128)(2,1)}, bf16[256,1024]{1,0:T(8,128)(2,1)}, u32[]{:S(2)}, u32[]{:S(2)}) collective-permute-start(bf16[256,1024]{1,0:T(8,128)(2,1)} %get-tuple-element.35), channel_id=1, source_target_pairs={{0,1},{1,0},{2,3},{3,2},{4,5},{5,4},{6,7},{7,6},{8,9},{9,8},{10,11... | collective-permute-start | bytes 1572872 | tf_op jit(solution)/shard_map/ppermute | solution.py:286
  27.4 2.4 %collective-permute-start.2 = (bf16[256,1024]{1,0:T(8,128)(2,1)}, bf16[256,1024]{1,0:T(8,128)(2,1)}, u32[]{:S(2)}, u32[]{:S(2)}) collective-permute-start(bf16[256,1024]{1,0:T(8,128)(2,1)} %get-tuple-element.36), channel_id=1, source_target_pairs={{0,1},{1,0},{2,3},{3,2},{4,5},{5,4},{6,7},{7,6},{8,9},{9,8},{10,11... | collective-permute-start | bytes 1572872 | tf_op jit(solution)/shard_map/ppermute | solution.py:286
  29.8 0.0 collective-permute-done
  29.8 0.0 all-to-all-done.blocks
  29.8 0.9 %broadcast_in_dim.30 = bf16[8,2,128,128]{3,2,1,0:T(8,128)(2,1)} broadcast(bf16[2,128,128]{2,1,0:T(8,128)(2,1)S(1)} %bitcast.32), dimensions={1,2,3} | broadcast | bytes 589824 | tf_op jit(solution)/shard_map/broadcast_in_dim | solution.py:291
  30.7 6.4 %all-to-all-start.1 = ((bf16[16,128,128]{2,1,0:T(8,128)(2,1)}), bf16[16,128,128]{2,1,0:T(8,128)(2,1)S(1)}, u32[]{:S(2)}, u32[]{:S(2)}) async-start(bf16[16,128,128]{2,1,0:T(8,128)(2,1)} %bitcast.29), calls=%async_computation.1 | async-start | bytes 1048576 | tf_op jit(solution)/shard_map/all_to_all | solution.py:283
  37.1 0.0 collective-permute-done.3.refs_2_
  37.1 0.0 collective-permute-done.2.refs_1_
  37.1 0.0 collective-permute-done.1.refs_0_
  37.1 12.3 %all-to-all-done.1.back = bf16[16,128,128]{2,1,0:T(8,128)(2,1)S(1)} async-done(((bf16[16,128,128]{2,1,0:T(8,128)(2,1)}), bf16[16,128,128]{2,1,0:T(8,128)(2,1)S(1)}, u32[]{:S(2)}, u32[]{:S(2)}) %all-to-all-start.1) | async-done | bytes 524320 | tf_op jit(solution)/shard_map/all_to_all | solution.py:283
  49.5 0.0 copy-done.4
  49.5 5.1 %shard_map.110 = (bf16[16,272,128]{2,1,0:T(8,128)(2,1)}, bf16[128,1536]{1,0:T(8,128)(2,1)S(1)}) custom-call(bf16[16,272,128]{2,1,0:T(8,128)(2,1)} %bitcast.4.spent, bf16[16,272,128]{2,1,0:T(8,128)(2,1)S(1)} %all-to-all-done.blocks, bf16[16,128,128]{2,1,0:T(8,128)(2,1)S(1)} %all-to-all-done.1.back, ...), custom_call_target="tpu_custom_call", output_to_operand_aliasing={{0}: (0, {})} | custom-call | flops 1342177280 | bytes 10485760 | tf_op jit(solution)/shard_map/pallas_call | solution.py:248
  54.6 3.7 %all-to-all-start.2 = ((bf16[16,272,128]{2,1,0:T(8,128)(2,1)}), bf16[16,272,128]{2,1,0:T(8,128)(2,1)S(1)}, u32[]{:S(2)}, u32[]{:S(2)}) async-start(bf16[16,272,128]{2,1,0:T(8,128)(2,1)} %get-tuple-element.22), calls=%async_computation.2 | async-start | bytes 2228224 | tf_op jit(solution)/shard_map/all_to_all | solution.py:283
  58.3 0.0 copy-start.3
  58.3 1.4 %shard_map.111 = (bf16[128,2560]{1,0:T(8,128)(2,1)}, bf16[128,2048]{1,0:T(8,128)(2,1)}) custom-call(bf16[16,272,128]{2,1,0:T(8,128)(2,1)S(1)} %all-to-all-done.blocks, bf16[16,128,128]{2,1,0:T(8,128)(2,1)S(1)} %all-to-all-done.1.back, bf16[128,1536]{1,0:T(8,128)(2,1)S(1)} %get-tuple-element.23.middle, f32[1,2048]{1,0:T(1,128)S(1)} %copy-done.4), custom_call_target="tpu_custom_call" | custom-call | bytes 4194304 | tf_op jit(solution)/shard_map/pallas_call | solution.py:248
  59.7 2.2 %collective-permute-start.4 = (bf16[128,2560]{1,0:T(8,128)(2,1)}, bf16[128,2560]{1,0:T(8,128)(2,1)S(1)}, u32[]{:S(2)}, u32[]{:S(2)}) collective-permute-start(bf16[128,2560]{1,0:T(8,128)(2,1)} %get-tuple-element.24.trade), channel_id=1, source_target_pairs={{0,1},{1,0},{2,3},{3,2},{4,5},{5,4},{6,7},{7,6},{8,9},{9,8},{10,11... | collective-permute-start | bytes 1966088 | tf_op jit(solution)/shard_map/ppermute | solution.py:324
  61.9 2.1 %collective-permute-start.5 = (bf16[128,2048]{1,0:T(8,128)(2,1)}, bf16[128,2048]{1,0:T(8,128)(2,1)S(1)}, u32[]{:S(2)}, u32[]{:S(2)}) collective-permute-start(bf16[128,2048]{1,0:T(8,128)(2,1)} %get-tuple-element.25.grads), channel_id=1, source_target_pairs={{0,1},{1,0},{2,3},{3,2},{4,5},{5,4},{6,7},{7,6},{8,9},{9,8},{10,11... | collective-permute-start | bytes 1572872 | tf_op jit(solution)/shard_map/ppermute | solution.py:324
  64.0 0.0 copy-done.3
  64.0 9.0 %collective-permute-start.8 = (bf16[256,128]{1,0:T(8,128)(2,1)S(1)}, bf16[256,128]{1,0:T(8,128)(2,1)S(1)}, u32[]{:S(2)}, u32[]{:S(2)}) collective-permute-start(bf16[256,128]{1,0:T(8,128)(2,1)S(1)} %bitcast.27), channel_id=1, source_target_pairs={{0,496},{16,480},{32,464},{48,448},{64,432},{80,416},{96,400},{112... | collective-permute-start | bytes 196616 | tf_op jit(solution)/shard_map/ppermute | solution.py:277
  73.1 0.8 slice.11.fetched
  73.9 0.0 copy-start.2
  73.9 0.0 collective-permute-done.5.far_grads
  73.9 0.0 collective-permute-done.4.received
  73.9 3.0 %shard_map.112 = (bf16[2048,256]{1,0:T(8,128)(2,1)}, bf16[256,2048]{1,0:T(8,128)(2,1)}) custom-call(bf16[128,2560]{1,0:T(8,128)(2,1)} %get-tuple-element.24.trade, bf16[128,2560]{1,0:T(8,128)(2,1)S(1)} %collective-permute-done.4.received, bf16[128,1536]{1,0:T(8,128)(2,1)S(1)} %get-tuple-element.23.middle, bf16[128,2048]{1,0:T(8,128)(2,1)} %get-tuple-element.25.grads, ...), custom_call_target="tpu_custom_call" | custom-call | flops 536870912 | bytes 6291456 | tf_op jit(solution)/shard_map/pallas_call | solution.py:248
  76.9 0.1 all-to-all-done.2.parts
  77.0 0.0 copy-done.2
  77.0 0.4 shard_map.113
  77.4 5.3 %collective-permute-start.6 = (bf16[256,128]{1,0:T(8,128)(2,1)S(1)}, bf16[256,128]{1,0:T(8,128)(2,1)S(1)}, u32[]{:S(2)}, u32[]{:S(2)}) collective-permute-start(bf16[256,128]{1,0:T(8,128)(2,1)S(1)} %get-tuple-element.29), channel_id=1, source_target_pairs={{16,32},{32,16},{48,64},{64,48},{80,96},{96,80},{112,128},{128,112... | collective-permute-start | bytes 196616 | tf_op jit(solution)/shard_map/ppermute | solution.py:348
  82.7 1.9 %collective-permute-start.7 = (bf16[256,128]{1,0:T(8,128)(2,1)S(1)}, bf16[256,128]{1,0:T(8,128)(2,1)S(1)}, u32[]{:S(2)}, u32[]{:S(2)}) collective-permute-start(bf16[256,128]{1,0:T(8,128)(2,1)S(1)} %get-tuple-element.30), channel_id=1, source_target_pairs={{0,16},{16,0},{32,48},{48,32},{64,80},{80,64},{96,112},{112,96},{1... | collective-permute-start | bytes 196616 | tf_op jit(solution)/shard_map/ppermute | solution.py:347
  84.7 0.0 collective-permute-done.8.refs_0_
  84.7 0.6 shard_map.115
  85.3 0.4 collective-permute-done.6.across
  85.7 3.2 %collective-permute-done.7.inside = bf16[256,128]{1,0:T(8,128)(2,1)S(1)} collective-permute-done((bf16[256,128]{1,0:T(8,128)(2,1)S(1)}, bf16[256,128]{1,0:T(8,128)(2,1)S(1)}, u32[]{:S(2)}, u32[]{:S(2)}) %collective-permute-start.7) | collective-permute-done | bytes 65568 | tf_op jit(solution)/shard_map/ppermute | solution.py:347
  88.9 0.7 shard_map.114
  (3 shorter events, 0.0 us)
Async XLA Ops:
  0.6 11.4 %copy-start = (bf16[1,2,256,128]{3,2,1,0:T(8,128)(2,1)S(1)}, bf16[1,2,256,128]{3,2,1,0:T(8,128)(2,1)}, u32[]{:S(2)}) copy-start(bf16[1,2,256,128]{3,2,1,0:T(8,128)(2,1)} %param.9) | copy-start | bytes 393220
  2.8 21.5 %copy-start.1 = (bf16[1,256,2048]{2,1,0:T(8,128)(2,1)S(1)}, bf16[1,256,2048]{2,1,0:T(8,128)(2,1)}, u32[]{:S(2)}) copy-start(bf16[1,256,2048]{2,1,0:T(8,128)(2,1)} %param.13) | copy-start | bytes 3145732
  2.8 27.1 %all-to-all-start = ((bf16[16,272,128]{2,1,0:T(8,128)(2,1)}), bf16[16,272,128]{2,1,0:T(8,128)(2,1)S(1)}, u32[]{:S(2)}, u32[]{:S(2)}) async-start(bf16[16,272,128]{2,1,0:T(8,128)(2,1)} %bitcast.4.spent), calls=%async_computation | async-start | bytes 2228224 | tf_op jit(solution)/shard_map/all_to_all | solution.py:283
  9.0 28.1 %collective-permute-start.1 = (bf16[2048,256]{1,0:T(8,128)(2,1)}, bf16[2048,256]{1,0:T(8,128)(2,1)}, u32[]{:S(2)}, u32[]{:S(2)}) collective-permute-start(bf16[2048,256]{1,0:T(8,128)(2,1)} %bitcast.10.weight_a), channel_id=1, source_target_pairs={{0,1},{1,0},{2,3},{3,2},{4,5},{5,4},{6,7},{7,6},{8,9},{9,8},{10,11... | collective-permute-start | bytes 3145736 | tf_op jit(solution)/shard_map/ppermute | solution.py:286
  12.0 17.8 %collective-permute-start = (bf16[256,128]{1,0:T(8,128)(2,1)S(1)}, bf16[256,128]{1,0:T(8,128)(2,1)S(1)}, u32[]{:S(2)}, u32[]{:S(2)}) collective-permute-start(bf16[256,128]{1,0:T(8,128)(2,1)S(1)} %dynamic-slice_bitcast_fusion), channel_id=1, source_target_pairs={{0,496},{16,480},{32,464},{48,448},{64,432},{80,416},{96,400},{112... | collective-permute-start | bytes 196616 | tf_op jit(solution)/shard_map/ppermute | solution.py:276
  25.3 24.1 %copy-start.4 = (f32[1,2048]{1,0:T(1,128)S(1)}, f32[1,2048]{1,0:T(1,128)}, u32[]{:S(2)}) copy-start(f32[1,2048]{1,0:T(1,128)} %gain.3) | copy-start | bytes 24580
  25.3 11.8 %collective-permute-start.3 = (bf16[256,1024]{1,0:T(8,128)(2,1)}, bf16[256,1024]{1,0:T(8,128)(2,1)}, u32[]{:S(2)}, u32[]{:S(2)}) collective-permute-start(bf16[256,1024]{1,0:T(8,128)(2,1)} %get-tuple-element.35), channel_id=1, source_target_pairs={{0,1},{1,0},{2,3},{3,2},{4,5},{5,4},{6,7},{7,6},{8,9},{9,8},{10,11... | collective-permute-start | bytes 1572872 | tf_op jit(solution)/shard_map/ppermute | solution.py:286
  27.4 9.7 %collective-permute-start.2 = (bf16[256,1024]{1,0:T(8,128)(2,1)}, bf16[256,1024]{1,0:T(8,128)(2,1)}, u32[]{:S(2)}, u32[]{:S(2)}) collective-permute-start(bf16[256,1024]{1,0:T(8,128)(2,1)} %get-tuple-element.36), channel_id=1, source_target_pairs={{0,1},{1,0},{2,3},{3,2},{4,5},{5,4},{6,7},{7,6},{8,9},{9,8},{10,11... | collective-permute-start | bytes 1572872 | tf_op jit(solution)/shard_map/ppermute | solution.py:286
  30.7 18.7 %all-to-all-start.1 = ((bf16[16,128,128]{2,1,0:T(8,128)(2,1)}), bf16[16,128,128]{2,1,0:T(8,128)(2,1)S(1)}, u32[]{:S(2)}, u32[]{:S(2)}) async-start(bf16[16,128,128]{2,1,0:T(8,128)(2,1)} %bitcast.29), calls=%async_computation.1 | async-start | bytes 1048576 | tf_op jit(solution)/shard_map/all_to_all | solution.py:283
  54.6 22.5 %all-to-all-start.2 = ((bf16[16,272,128]{2,1,0:T(8,128)(2,1)}), bf16[16,272,128]{2,1,0:T(8,128)(2,1)S(1)}, u32[]{:S(2)}, u32[]{:S(2)}) async-start(bf16[16,272,128]{2,1,0:T(8,128)(2,1)} %get-tuple-element.22), calls=%async_computation.2 | async-start | bytes 2228224 | tf_op jit(solution)/shard_map/all_to_all | solution.py:283
  58.3 5.7 %copy-start.3 = (bf16[1,256,128]{2,1,0:T(8,128)(2,1)S(1)}, bf16[1,256,128]{2,1,0:T(8,128)(2,1)}, u32[]{:S(2)}) copy-start(bf16[1,256,128]{2,1,0:T(8,128)(2,1)} %param.7) | copy-start | bytes 196612
  59.7 14.2 %collective-permute-start.4 = (bf16[128,2560]{1,0:T(8,128)(2,1)}, bf16[128,2560]{1,0:T(8,128)(2,1)S(1)}, u32[]{:S(2)}, u32[]{:S(2)}) collective-permute-start(bf16[128,2560]{1,0:T(8,128)(2,1)} %get-tuple-element.24.trade), channel_id=1, source_target_pairs={{0,1},{1,0},{2,3},{3,2},{4,5},{5,4},{6,7},{7,6},{8,9},{9,8},{10,11... | collective-permute-start | bytes 1966088 | tf_op jit(solution)/shard_map/ppermute | solution.py:324
  61.9 12.0 %collective-permute-start.5 = (bf16[128,2048]{1,0:T(8,128)(2,1)}, bf16[128,2048]{1,0:T(8,128)(2,1)S(1)}, u32[]{:S(2)}, u32[]{:S(2)}) collective-permute-start(bf16[128,2048]{1,0:T(8,128)(2,1)} %get-tuple-element.25.grads), channel_id=1, source_target_pairs={{0,1},{1,0},{2,3},{3,2},{4,5},{5,4},{6,7},{7,6},{8,9},{9,8},{10,11... | collective-permute-start | bytes 1572872 | tf_op jit(solution)/shard_map/ppermute | solution.py:324
  64.0 20.6 %collective-permute-start.8 = (bf16[256,128]{1,0:T(8,128)(2,1)S(1)}, bf16[256,128]{1,0:T(8,128)(2,1)S(1)}, u32[]{:S(2)}, u32[]{:S(2)}) collective-permute-start(bf16[256,128]{1,0:T(8,128)(2,1)S(1)} %bitcast.27), channel_id=1, source_target_pairs={{0,496},{16,480},{32,464},{48,448},{64,432},{80,416},{96,400},{112... | collective-permute-start | bytes 196616 | tf_op jit(solution)/shard_map/ppermute | solution.py:277
  73.9 3.1 %copy-start.2 = (bf16[1,256,128]{2,1,0:T(8,128)(2,1)S(1)}, bf16[1,256,128]{2,1,0:T(8,128)(2,1)}, u32[]{:S(2)}) copy-start(bf16[1,256,128]{2,1,0:T(8,128)(2,1)} %param.8) | copy-start | bytes 196612
  77.4 8.3 %collective-permute-start.6 = (bf16[256,128]{1,0:T(8,128)(2,1)S(1)}, bf16[256,128]{1,0:T(8,128)(2,1)S(1)}, u32[]{:S(2)}, u32[]{:S(2)}) collective-permute-start(bf16[256,128]{1,0:T(8,128)(2,1)S(1)} %get-tuple-element.29), channel_id=1, source_target_pairs={{16,32},{32,16},{48,64},{64,48},{80,96},{96,80},{112,128},{128,112... | collective-permute-start | bytes 196616 | tf_op jit(solution)/shard_map/ppermute | solution.py:348
  82.7 6.2 %collective-permute-start.7 = (bf16[256,128]{1,0:T(8,128)(2,1)S(1)}, bf16[256,128]{1,0:T(8,128)(2,1)S(1)}, u32[]{:S(2)}, u32[]{:S(2)}) collective-permute-start(bf16[256,128]{1,0:T(8,128)(2,1)S(1)} %get-tuple-element.30), channel_id=1, source_target_pairs={{0,16},{16,0},{32,48},{48,32},{64,80},{80,64},{96,112},{112,96},{1... | collective-permute-start | bytes 196616 | tf_op jit(solution)/shard_map/ppermute | solution.py:347

commit v5 on v4

--- a/solution.py
+++ b/solution.py
@@ -87,14 +87,14 @@
     tokens = back.shape[1]
     width = 128 * ranks
     units = weight_a.shape[1]
-    near_load = pltpu.make_async_copy(weight_a, near_a_ref, sems.at[chips])
+    near_load = pltpu.make_async_copy(weight_a, near_a_ref, sems.at[ranks])
     loads = []
     for refs, place, axis in ((far[:-2], far_a_ref, 0), (far[-2:], far_b_ref, 1)):
         size = width // len(refs)
         for index, ref in enumerate(refs):
             part = slice(index * size, index * size + size)
             there = place.at[part, :] if axis == 0 else place.at[:, part]
-            loads.append(pltpu.make_async_copy(ref, there, sems.at[chips + 1 + len(loads)]))
+            loads.append(pltpu.make_async_copy(ref, there, sems.at[ranks + 1 + len(loads)]))
     near_load.start()
     for load in loads:
         load.start()
@@ -145,6 +145,8 @@
         moment += jnp.sum(wide * pre, axis=1, keepdims=True)
     share = 1.0 / chips
     rows = columns_to_rows([plain * (1.0 / width), moment * (1.0 / width), center * share, scale * share])
+    row = lax.broadcasted_iota(jnp.int32, rows.shape, 0)
+    plain_rows = jnp.where(row == 3, share, 0.0).astype(BF)
     copies = []
     for chip in range(chips):
         cols = chip_cols(chip)
@@ -154,14 +156,14 @@
             act = middle[:, (2 + side) * units : (3 + side) * units]
             branch += dot(act, seconds[side][:, cols])
             term += dot(pre_grad, firsts[side][cols, :], ((1,), (1,)))
-        for side in range(2):
-            lanes = slice(side * 128, side * 128 + 128)
-            held[2 * chip + side, :tokens, :] = branch[:, lanes].astype(BF)
-            held[2 * chip + side, tokens : 2 * tokens, :] = term[:, lanes].astype(BF)
-            held[2 * chip + side, 2 * tokens :, :] = rows
-        both = slice(2 * chip, 2 * chip + 2)
-        copies.append(pltpu.make_async_copy(held.at[both], parts.at[both], sems.at[chip]))
-        copies[-1].start()
+        for kind, value, numbers in ((0, term * gain[:, cols], rows), (1, branch, plain_rows)):
+            place = kind * chips + chip
+            for side in range(2):
+                start = side * (tokens + ROWS)
+                held[place, start : start + tokens, :] = value[:, side * 128 : side * 128 + 128].astype(BF)
+                held[place, start + tokens : start + tokens + ROWS, :] = numbers
+            copies.append(pltpu.make_async_copy(held.at[place], parts.at[place], sems.at[place]))
+            copies[-1].start()
     for copy in copies:
         copy.wait()
 
@@ -200,24 +202,31 @@
         store.wait()
 
 
-def finish_kernel(odd_ref, parts, forward_in, grad_out, fetched, gain, inside, across):
-    ranks, rows, _ = parts.shape
-    tokens = (rows - ROWS) // 2
-    odd = odd_ref[0] == 1
+def finish(parts, source, bases, values, result):
+    _, ranks, rows, _ = parts.shape
+    tokens = rows - ROWS
     for side in range(2):
-        total = parts[side].astype(F32)
+        total = parts[source, side].astype(F32)
         for rank in range(2 + side, ranks, 2):
-            total += parts[rank].astype(F32)
-        here = slice(side * tokens, side * tokens + tokens)
-        outputs = (forward_in[here, :].astype(F32) + total[:tokens]).astype(BF)
-        scaled = total[tokens : 2 * tokens] * gain[...]
-        plain_mean, moment_mean, center, scale = rows_to_columns(total[2 * tokens :])
-        hidden = (fetched[side].astype(F32) - center) * scale
-        input_grad = (
-            grad_out[here, :].astype(F32) + scale * (scaled - plain_mean - hidden * moment_mean)
-        ).astype(BF)
-        inside[here, :] = jnp.where(odd, input_grad, outputs)
-        across[here, :] = jnp.where(odd, outputs, input_grad)
+            total += parts[source, rank].astype(F32)
+        plain_mean, moment_mean, center, scale = rows_to_columns(total[tokens:])
+        hidden = (values[side].astype(F32) - center) * scale
+        change = scale * (total[:tokens] - plain_mean - hidden * moment_mean)
+        result[side * tokens : side * tokens + tokens, :] = (bases[side].astype(F32) + change).astype(BF)
+
+
+def across_kernel(odd_ref, parts, forward_in, grad_out, fetched, across):
+    odd = odd_ref[0]
+    tokens = fetched.shape[1]
+    halves = [slice(0, tokens), slice(tokens, 2 * tokens)]
+    bases = [jnp.where(odd == 1, forward_in[here, :], grad_out[here, :]) for here in halves]
+    finish(parts, odd, bases, [fetched[0], fetched[1]], across)
+
+
+def inside_kernel(odd_ref, parts, paired, inside):
+    tokens = inside.shape[0] // 2
+    halves = [slice(0, tokens), slice(tokens, 2 * tokens)]
+    finish(parts, 1 - odd_ref[0], [paired[0, here, :] for here in halves], [paired[1, here, :] for here in halves], inside)
 
 
 def store_kernel(*refs):
@@ -285,13 +294,17 @@
     pieces = (weight_a, weight_b[:, : width // 2], weight_b[:, width // 2 :])
     far = [lax.ppermute(piece, "tensor", swap) for piece in pieces]
     mine = jnp.stack([value.reshape(2, half, shard_cols) for value in (forward_in, grad_out)], axis=1)
-    mine = jnp.pad(mine.reshape(2, tokens, shard_cols), ((0, 0), (0, ROWS), (0, 0)))
+    mine = jnp.pad(mine.reshape(2, tokens, shard_cols), ((0, 0), (0, 2 * ROWS), (0, 0)))
     spread = jnp.broadcast_to(mine[None], (chips,) + mine.shape).reshape((ranks,) + mine.shape[1:])
     blocks = exchange(spread)
     back_spread = jnp.broadcast_to(fetched.reshape(1, 2, half, shard_cols), (chips, 2, half, shard_cols))
     blocks, back_spread = lax.optimization_barrier((blocks, back_spread.reshape(ranks, half, shard_cols)))
 
     back = exchange(back_spread)
+    section_odd = lax.rem(lax.axis_index("section"), 2)
+    sent = jnp.stack([jnp.where(section_odd == 1, grad_out, forward_in), fetched])
+    paired = lax.ppermute(sent, "section", [(s, s ^ 1) for s in range(sections)])
+    back, paired = lax.optimization_barrier((back, paired))
     parts, middle = call(
         block_kernel,
         (shape(spread.shape, BF), shape((half, 6 * hidden_units), BF)),
@@ -304,14 +317,18 @@
             pltpu.VMEM(weight_a.shape, BF),
             pltpu.VMEM(weight_a.shape, BF),
             pltpu.VMEM(weight_b.shape, BF),
-            pltpu.SemaphoreType.DMA((chips + 1 + len(far),)),
+            pltpu.SemaphoreType.DMA((ranks + 1 + len(far),)),
         ),
         aliases={0: 0},
         flops=10 * tokens * width * hidden_units,
         nbytes=10 * 2**20,
     )
 
-    collected = exchange(parts)
+    planes = [[section * ranks + r for section in (first, first + 1) for r in range(ranks)] for first in range(0, sections, 2)]
+    block = (2, ranks, half + ROWS, shard_cols)
+    collected = lax.all_to_all(
+        parts.reshape((2 * ranks,) + block[2:]), ("section", "tensor"), 0, 0, tiled=True, axis_index_groups=planes
+    ).reshape(block)
     trade, grads = call(
         trade_kernel,
         (shape((half, width + 2 * hidden_units), BF), shape((half, width), BF)),
@@ -331,21 +348,18 @@
         flops=4 * tokens * width * hidden_units,
         nbytes=6 * 2**20,
     )
+    piece = shape((tokens, shard_cols), BF)
+    odd_ref = section_odd.reshape(1)
     collected, grad_a, grad_b = lax.optimization_barrier((collected, grad_a, grad_b))
-    gain_part = lax.dynamic_slice_in_dim(norm_gain, rank * shard_cols, shard_cols, 1)
-    piece = shape((tokens, shard_cols), BF)
-    kept = back_spread[:2]
-
-    section_odd = lax.rem(lax.axis_index("section"), 2).reshape(1)
-    inside, across = call(
-        finish_kernel,
-        (piece, piece),
-        (section_odd, collected, forward_in, grad_out, kept, gain_part),
-        specs=smem + vmem(5),
-        nbytes=2 * 2**20,
-    )
-    inside = lax.ppermute(inside, "section", [(s, s ^ 1) for s in range(sections)])
+    across = call(
+        across_kernel,
+        (piece,),
+        (odd_ref, collected, forward_in, grad_out, back_spread[:2]),
+        specs=smem + vmem(4),
+        nbytes=2**20,
+    )[0]
     across = lax.ppermute(across, "section", [(s, s + 1 if s % 2 else s - 1) for s in range(1, sections - 1)])
+    inside = call(inside_kernel, (piece,), (odd_ref, collected, paired), specs=smem + vmem(2), nbytes=2**20)[0]
 
     def store(*values):
         count = len(values)
@@ -362,7 +376,7 @@
     arrivals, sent_grads = call(
         store_pair_kernel,
         (piece, piece),
-        (section_odd, across, inside),
+        (odd_ref, across, inside),
         specs=smem + vmem(2),
         out_specs=hbm(2),
         scratch=(pltpu.SemaphoreType.DMA((2,)),),

time: 90.3 us -> 89.4 us (0.990)
  the two profiles are of different devices: /device:TPU:98 before, /device:TPU:128 now
where the time goes in v5:
time: 89.4 us; the launch traced here: 88.6 us
  starting transfers between devices  54.9 us (61%)
  waiting for transfers between devices  18.1 us (20%)
  Pallas kernels  9.11 us (10%)
  local copies, waits for them, and re-layouts  4.06 us (5%)
  between operations  1.56 us (2%)
  other arithmetic  0.95 us (1%)
    all_to_all x2, starting transfers between devices, exchange(): return lax.all_to_all(blocks, 'tensor', 0, 0, tiled=True)  14.3 us
    ppermute x1, starting transfers between devices, per_device(): fetched = lax.ppermute(returned, 'section', mirror)  10.5 us
    ppermute x1, starting transfers between devices, per_device(): parked = lax.ppermute(forward_in, 'section', mirror)  9.3 us
    pallas_call x7, Pallas kernels, call(): pl.pallas_call(kernel, out_shape=out_shapes, in_specs=specs or vmem(len(o...  9.11 us
    ppermute x1, waiting for transfers between devices, per_device(): lax.ppermute(sent, 'section', [(s, s ^ 1) for s in range(sections)])  7.9 us
    ppermute x3, starting transfers between devices, per_device(): far = [lax.ppermute(piece, 'tensor', swap) for piece in pieces]  6.76 us
    ppermute x1, waiting for transfers between devices, per_device(): lax.ppermute(across, 'section', [(s, s + 1 if s % 2 else s - 1) for s in...  5.26 us
    all_to_all x1, starting transfers between devices, per_device(): lax.all_to_all(parts.reshape((2 * ranks,) + block[2:]), ('section', 'tens...  5.17 us
  transfers between devices with their start and end apart: 12, of which 5 were waited for; matrix products, arithmetic and copies ran while one was open for 3% of the time, Pallas kernels for 4%

profile of v5, /device:TPU:128, one launch (start us, length us, event | category | flops | bytes accessed | tf_op | source)
XLA Modules:
  0.0 88.6 jit_solution(1818649387774575853)
XLA Ops:
  0.6 0.0 copy-start
  0.6 0.9 %pad_maximum_fusion = bf16[2,2,128,128]{3,2,1,0:T(8,128)(2,1)S(1)} fusion(bf16[2,1,128,128]{3,2,1,0:T(8,128)(2,1)} %bitcast.29, bf16[2,1,128,128]{3,2,1,0:T(8,128)(2,1)} %bitcast.31), kind=kLoop, calls=%fused_computation | loop fusion | flops 65536 | bytes 262144 | tf_op jit(solution)/shard_map/stack | solution.py:296
  1.6 1.2 %broadcast_in_dim.28 = bf16[8,2,288,128]{3,2,1,0:T(8,128)(2,1)} broadcast(bf16[2,288,128]{2,1,0:T(8,128)(2,1)S(1)} %pad.4), dimensions={1,2,3} | broadcast | bytes 1327104 | tf_op jit(solution)/shard_map/broadcast_in_dim | solution.py:298
  2.8 0.0 copy-start.1
  2.8 7.2 %all-to-all-start = ((bf16[16,288,128]{2,1,0:T(8,128)(2,1)}), bf16[16,288,128]{2,1,0:T(8,128)(2,1)S(1)}, u32[]{:S(2)}, u32[]{:S(2)}) async-start(bf16[16,288,128]{2,1,0:T(8,128)(2,1)} %bitcast.4.spent), calls=%async_computation | async-start | bytes 2359296 | tf_op jit(solution)/shard_map/all_to_all | solution.py:292
  10.0 2.3 %collective-permute-start.2 = (bf16[2048,256]{1,0:T(8,128)(2,1)}, bf16[2048,256]{1,0:T(8,128)(2,1)}, u32[]{:S(2)}, u32[]{:S(2)}) collective-permute-start(bf16[2048,256]{1,0:T(8,128)(2,1)} %bitcast.11.weight_a), channel_id=1, source_target_pairs={{0,1},{1,0},{2,3},{3,2},{4,5},{5,4},{6,7},{7,6},{8,9},{9,8},{10,11... | collective-permute-start | bytes 3145736 | tf_op jit(solution)/shard_map/ppermute | solution.py:295
  12.9 0.0 copy-done
  13.0 10.5 %collective-permute-start = (bf16[256,128]{1,0:T(8,128)(2,1)S(1)}, bf16[256,128]{1,0:T(8,128)(2,1)S(1)}, u32[]{:S(2)}, u32[]{:S(2)}) collective-permute-start(bf16[256,128]{1,0:T(8,128)(2,1)S(1)} %dynamic-slice_bitcast_fusion), channel_id=1, source_target_pairs={{0,496},{16,480},{32,464},{48,448},{64,432},{80,416},{96,400},{112... | collective-permute-start | bytes 196616 | tf_op jit(solution)/shard_map/ppermute | solution.py:285
  23.5 0.0 copy-done.1
  23.5 1.1 %fusion = (bf16[256,1024]{1,0:T(8,128)(2,1)}, bf16[256,1024]{1,0:T(8,128)(2,1)}) fusion(bf16[256,2048]{1,0:T(8,128)(2,1)S(1)} %bitcast.27), kind=kLoop, calls=%fused_computation.4 | loop fusion | bytes 2097152 | tf_op jit(solution)/shard_map/slice | solution.py:294
  24.5 0.0 copy-start.2
  24.5 0.0 copy-start.3
  24.5 2.0 %collective-permute-start.4 = (bf16[256,1024]{1,0:T(8,128)(2,1)}, bf16[256,1024]{1,0:T(8,128)(2,1)}, u32[]{:S(2)}, u32[]{:S(2)}) collective-permute-start(bf16[256,1024]{1,0:T(8,128)(2,1)} %get-tuple-element.35), channel_id=1, source_target_pairs={{0,1},{1,0},{2,3},{3,2},{4,5},{5,4},{6,7},{7,6},{8,9},{9,8},{10,11... | collective-permute-start | bytes 1572872 | tf_op jit(solution)/shard_map/ppermute | solution.py:295
  26.6 2.4 %collective-permute-start.3 = (bf16[256,1024]{1,0:T(8,128)(2,1)}, bf16[256,1024]{1,0:T(8,128)(2,1)}, u32[]{:S(2)}, u32[]{:S(2)}) collective-permute-start(bf16[256,1024]{1,0:T(8,128)(2,1)} %get-tuple-element.36), channel_id=1, source_target_pairs={{0,1},{1,0},{2,3},{3,2},{4,5},{5,4},{6,7},{7,6},{8,9},{9,8},{10,11... | collective-permute-start | bytes 1572872 | tf_op jit(solution)/shard_map/ppermute | solution.py:295
  29.0 0.0 collective-permute-done
  29.0 0.4 all-to-all-done.blocks
  29.4 0.9 %broadcast_in_dim.30 = bf16[8,2,128,128]{3,2,1,0:T(8,128)(2,1)} broadcast(bf16[2,128,128]{2,1,0:T(8,128)(2,1)S(1)} %bitcast.37), dimensions={1,2,3} | broadcast | bytes 589824 | tf_op jit(solution)/shard_map/broadcast_in_dim | solution.py:300
  30.3 7.2 %all-to-all-start.1 = ((bf16[16,128,128]{2,1,0:T(8,128)(2,1)}), bf16[16,128,128]{2,1,0:T(8,128)(2,1)S(1)}, u32[]{:S(2)}, u32[]{:S(2)}) async-start(bf16[16,128,128]{2,1,0:T(8,128)(2,1)} %bitcast.34), calls=%async_computation.1 | async-start | bytes 1048576 | tf_op jit(solution)/shard_map/all_to_all | solution.py:292
  37.5 0.0 copy-done.2
  37.5 0.0 copy-done.3
  37.6 2.1 %collective-permute-start.1 = (bf16[2,256,128]{2,1,0:T(8,128)(2,1)S(1)}, bf16[2,256,128]{2,1,0:T(8,128)(2,1)S(1)}, u32[]{:S(2)}, u32[]{:S(2)}) collective-permute-start(bf16[2,256,128]{2,1,0:T(8,128)(2,1)S(1)} %pad_maximum_fusion.1), channel_id=1, source_target_pairs={{0,16},{16,0},{32,48},{48,32},{64,80},{80,64},{96,112},{112,96},{1... | collective-permute-start | bytes 393224 | tf_op jit(solution)/shard_map/ppermute | solution.py:306
  39.7 7.9 %collective-permute-done.1.paired = bf16[2,256,128]{2,1,0:T(8,128)(2,1)S(1)} collective-permute-done((bf16[2,256,128]{2,1,0:T(8,128)(2,1)S(1)}, bf16[2,256,128]{2,1,0:T(8,128)(2,1)S(1)}, u32[]{:S(2)}, u32[]{:S(2)}) %collective-permute-start.1) | collective-permute-done | bytes 131104 | tf_op jit(solution)/shard_map/ppermute | solution.py:306
  47.6 2.7 %all-to-all-done.1.back = bf16[16,128,128]{2,1,0:T(8,128)(2,1)S(1)} async-done(((bf16[16,128,128]{2,1,0:T(8,128)(2,1)}), bf16[16,128,128]{2,1,0:T(8,128)(2,1)S(1)}, u32[]{:S(2)}, u32[]{:S(2)}) %all-to-all-start.1) | async-done | bytes 524320 | tf_op jit(solution)/shard_map/all_to_all | solution.py:292
  50.3 0.0 collective-permute-done.4.refs_2_
  50.3 0.0 collective-permute-done.3.refs_1_
  50.4 0.0 collective-permute-done.2.refs_0_
  50.4 0.0 copy-done.6
  50.4 5.1 %shard_map.110 = (bf16[16,288,128]{2,1,0:T(8,128)(2,1)}, bf16[128,1536]{1,0:T(8,128)(2,1)S(1)}) custom-call(bf16[16,288,128]{2,1,0:T(8,128)(2,1)} %bitcast.4.spent, bf16[16,288,128]{2,1,0:T(8,128)(2,1)S(1)} %all-to-all-done.blocks, bf16[16,128,128]{2,1,0:T(8,128)(2,1)S(1)} %all-to-all-done.1.back, ...), custom_call_target="tpu_custom_call", output_to_operand_aliasing={{0}: (0, {})} | custom-call | flops 1342177280 | bytes 10485760 | tf_op jit(solution)/shard_map/pallas_call | solution.py:257
  55.5 0.0 copy-done.4
  55.5 5.2 %all-to-all-start.2 = ((bf16[32,144,128]{2,1,0:T(8,128)(2,1)}), bf16[32,144,128]{2,1,0:T(8,128)(2,1)S(1)}, u32[]{:S(2)}, u32[]{:S(2)}) async-start(bf16[32,144,128]{2,1,0:T(8,128)(2,1)} %bitcast.12), calls=%async_computation.2 | async-start | bytes 2359296 | tf_op jit(solution)/shard_map/all_to_all | solution.py:329
  60.7 0.4 shard_map.111
  61.1 2.2 %collective-permute-start.5 = (bf16[128,2560]{1,0:T(8,128)(2,1)S(1)}, bf16[128,2560]{1,0:T(8,128)(2,1)S(1)}, u32[]{:S(2)}, u32[]{:S(2)}) collective-permute-start(bf16[128,2560]{1,0:T(8,128)(2,1)S(1)} %get-tuple-element.25.trade), channel_id=1, source_target_pairs={{0,1},{1,0},{2,3},{3,2},{4,5},{5,4},{6,7},{7,6},{8,9},{9,8},{10,11... | collective-permute-start | bytes 1966088 | tf_op jit(solution)/shard_map/ppermute | solution.py:341
  63.2 2.1 %collective-permute-start.6 = (bf16[128,2048]{1,0:T(8,128)(2,1)S(1)}, bf16[128,2048]{1,0:T(8,128)(2,1)S(1)}, u32[]{:S(2)}, u32[]{:S(2)}) collective-permute-start(bf16[128,2048]{1,0:T(8,128)(2,1)S(1)} %get-tuple-element.26.grads), channel_id=1, source_target_pairs={{0,1},{1,0},{2,3},{3,2},{4,5},{5,4},{6,7},{7,6},{8,9},{9,8},{10,11... | collective-permute-start | bytes 1572872 | tf_op jit(solution)/shard_map/ppermute | solution.py:341
  65.4 9.3 %collective-permute-start.8 = (bf16[256,128]{1,0:T(8,128)(2,1)S(1)}, bf16[256,128]{1,0:T(8,128)(2,1)S(1)}, u32[]{:S(2)}, u32[]{:S(2)}) collective-permute-start(bf16[256,128]{1,0:T(8,128)(2,1)S(1)} %bitcast.32), channel_id=1, source_target_pairs={{0,496},{16,480},{32,464},{48,448},{64,432},{80,416},{96,400},{112... | collective-permute-start | bytes 196616 | tf_op jit(solution)/shard_map/ppermute | solution.py:286
  74.7 0.8 slice.11.fetched
  75.6 0.0 collective-permute-done.6.far_grads
  75.6 0.0 collective-permute-done.5.received
  75.6 1.7 %shard_map.112 = (bf16[2048,256]{1,0:T(8,128)(2,1)}, bf16[256,2048]{1,0:T(8,128)(2,1)}) custom-call(bf16[128,2560]{1,0:T(8,128)(2,1)S(1)} %get-tuple-element.25.trade, bf16[128,2560]{1,0:T(8,128)(2,1)S(1)} %collective-permute-done.5.received, bf16[128,1536]{1,0:T(8,128)(2,1)S(1)} %get-tuple-element.24.middle, bf16[128,2048]{1,0:T(8,128)(2,1)S(1)} %get-tuple-element.26.grads, ...), custom_call_target="tpu_custom_call" | custom-call | flops 536870912 | bytes 6291456 | tf_op jit(solution)/shard_map/pallas_call | solution.py:257
  77.3 0.0 copy-start.5
  77.3 1.7 %all-to-all-done.2 = bf16[32,144,128]{2,1,0:T(8,128)(2,1)S(1)} async-done(((bf16[32,144,128]{2,1,0:T(8,128)(2,1)}), bf16[32,144,128]{2,1,0:T(8,128)(2,1)S(1)}, u32[]{:S(2)}, u32[]{:S(2)}) %all-to-all-start.2) | async-done | bytes 1179680 | tf_op jit(solution)/shard_map/all_to_all | solution.py:329
  79.0 0.3 shard_map.113
  79.3 2.4 %collective-permute-start.7 = (bf16[256,128]{1,0:T(8,128)(2,1)S(1)}, bf16[256,128]{1,0:T(8,128)(2,1)S(1)}, u32[]{:S(2)}, u32[]{:S(2)}) collective-permute-start(bf16[256,128]{1,0:T(8,128)(2,1)S(1)} %shard_map.113), channel_id=1, source_target_pairs={{16,32},{32,16},{48,64},{64,48},{80,96},{96,80},{112,128},{128,112... | collective-permute-start | bytes 196616 | tf_op jit(solution)/shard_map/ppermute | solution.py:361
  81.7 0.0 collective-permute-done.8.refs_0_
  81.7 0.6 shard_map.116
  82.4 0.0 copy-done.5
  82.4 0.3 shard_map.114.inside
  82.7 5.3 %collective-permute-done.7.across = bf16[256,128]{1,0:T(8,128)(2,1)S(1)} collective-permute-done((bf16[256,128]{1,0:T(8,128)(2,1)S(1)}, bf16[256,128]{1,0:T(8,128)(2,1)S(1)}, u32[]{:S(2)}, u32[]{:S(2)}) %collective-permute-start.7) | collective-permute-done | bytes 65568 | tf_op jit(solution)/shard_map/ppermute | solution.py:361
  88.0 0.7 shard_map.115
  (6 shorter events, 0.1 us)
Async XLA Ops:
  0.6 12.3 %copy-start = (bf16[1,2,256,128]{3,2,1,0:T(8,128)(2,1)S(1)}, bf16[1,2,256,128]{3,2,1,0:T(8,128)(2,1)}, u32[]{:S(2)}) copy-start(bf16[1,2,256,128]{3,2,1,0:T(8,128)(2,1)} %param.9) | copy-start | bytes 393220
  2.8 20.7 %copy-start.1 = (bf16[1,256,2048]{2,1,0:T(8,128)(2,1)S(1)}, bf16[1,256,2048]{2,1,0:T(8,128)(2,1)}, u32[]{:S(2)}) copy-start(bf16[1,256,2048]{2,1,0:T(8,128)(2,1)} %param.13) | copy-start | bytes 3145732
  2.8 26.6 %all-to-all-start = ((bf16[16,288,128]{2,1,0:T(8,128)(2,1)}), bf16[16,288,128]{2,1,0:T(8,128)(2,1)S(1)}, u32[]{:S(2)}, u32[]{:S(2)}) async-start(bf16[16,288,128]{2,1,0:T(8,128)(2,1)} %bitcast.4.spent), calls=%async_computation | async-start | bytes 2359296 | tf_op jit(solution)/shard_map/all_to_all | solution.py:292
  10.0 40.4 %collective-permute-start.2 = (bf16[2048,256]{1,0:T(8,128)(2,1)}, bf16[2048,256]{1,0:T(8,128)(2,1)}, u32[]{:S(2)}, u32[]{:S(2)}) collective-permute-start(bf16[2048,256]{1,0:T(8,128)(2,1)} %bitcast.11.weight_a), channel_id=1, source_target_pairs={{0,1},{1,0},{2,3},{3,2},{4,5},{5,4},{6,7},{7,6},{8,9},{9,8},{10,11... | collective-permute-start | bytes 3145736 | tf_op jit(solution)/shard_map/ppermute | solution.py:295
  13.0 16.0 %collective-permute-start = (bf16[256,128]{1,0:T(8,128)(2,1)S(1)}, bf16[256,128]{1,0:T(8,128)(2,1)S(1)}, u32[]{:S(2)}, u32[]{:S(2)}) collective-permute-start(bf16[256,128]{1,0:T(8,128)(2,1)S(1)} %dynamic-slice_bitcast_fusion), channel_id=1, source_target_pairs={{0,496},{16,480},{32,464},{48,448},{64,432},{80,416},{96,400},{112... | collective-permute-start | bytes 196616 | tf_op jit(solution)/shard_map/ppermute | solution.py:285
  24.5 13.0 %copy-start.2 = (bf16[1,256,128]{2,1,0:T(8,128)(2,1)S(1)}, bf16[1,256,128]{2,1,0:T(8,128)(2,1)}, u32[]{:S(2)}) copy-start(bf16[1,256,128]{2,1,0:T(8,128)(2,1)} %param.8) | copy-start | bytes 196612
  24.5 13.0 %copy-start.3 = (bf16[1,256,128]{2,1,0:T(8,128)(2,1)S(1)}, bf16[1,256,128]{2,1,0:T(8,128)(2,1)}, u32[]{:S(2)}) copy-start(bf16[1,256,128]{2,1,0:T(8,128)(2,1)} %param.7) | copy-start | bytes 196612
  24.5 25.8 %copy-start.6 = (f32[1,2048]{1,0:T(1,128)S(1)}, f32[1,2048]{1,0:T(1,128)}, u32[]{:S(2)}) copy-start(f32[1,2048]{1,0:T(1,128)} %gain.3) | copy-start | bytes 24580
  24.5 25.8 %collective-permute-start.4 = (bf16[256,1024]{1,0:T(8,128)(2,1)}, bf16[256,1024]{1,0:T(8,128)(2,1)}, u32[]{:S(2)}, u32[]{:S(2)}) collective-permute-start(bf16[256,1024]{1,0:T(8,128)(2,1)} %get-tuple-element.35), channel_id=1, source_target_pairs={{0,1},{1,0},{2,3},{3,2},{4,5},{5,4},{6,7},{7,6},{8,9},{9,8},{10,11... | collective-permute-start | bytes 1572872 | tf_op jit(solution)/shard_map/ppermute | solution.py:295
  26.6 23.8 %collective-permute-start.3 = (bf16[256,1024]{1,0:T(8,128)(2,1)}, bf16[256,1024]{1,0:T(8,128)(2,1)}, u32[]{:S(2)}, u32[]{:S(2)}) collective-permute-start(bf16[256,1024]{1,0:T(8,128)(2,1)} %get-tuple-element.36), channel_id=1, source_target_pairs={{0,1},{1,0},{2,3},{3,2},{4,5},{5,4},{6,7},{7,6},{8,9},{9,8},{10,11... | collective-permute-start | bytes 1572872 | tf_op jit(solution)/shard_map/ppermute | solution.py:295
  30.3 20.0 %all-to-all-start.1 = ((bf16[16,128,128]{2,1,0:T(8,128)(2,1)}), bf16[16,128,128]{2,1,0:T(8,128)(2,1)S(1)}, u32[]{:S(2)}, u32[]{:S(2)}) async-start(bf16[16,128,128]{2,1,0:T(8,128)(2,1)} %bitcast.34), calls=%async_computation.1 | async-start | bytes 1048576 | tf_op jit(solution)/shard_map/all_to_all | solution.py:292
  37.6 10.0 %collective-permute-start.1 = (bf16[2,256,128]{2,1,0:T(8,128)(2,1)S(1)}, bf16[2,256,128]{2,1,0:T(8,128)(2,1)S(1)}, u32[]{:S(2)}, u32[]{:S(2)}) collective-permute-start(bf16[2,256,128]{2,1,0:T(8,128)(2,1)S(1)} %pad_maximum_fusion.1), channel_id=1, source_target_pairs={{0,16},{16,0},{32,48},{48,32},{64,80},{80,64},{96,112},{112,96},{1... | collective-permute-start | bytes 393224 | tf_op jit(solution)/shard_map/ppermute | solution.py:306
  47.6 7.9 %copy-start.4 = (bf16[2,256,128]{2,1,0:T(8,128)(2,1)}, bf16[2,256,128]{2,1,0:T(8,128)(2,1)S(1)}, u32[]{:S(2)}) copy-start(bf16[2,256,128]{2,1,0:T(8,128)(2,1)S(1)} %collective-permute-done.1.paired) | copy-start | bytes 393220
  55.5 23.5 %all-to-all-start.2 = ((bf16[32,144,128]{2,1,0:T(8,128)(2,1)}), bf16[32,144,128]{2,1,0:T(8,128)(2,1)S(1)}, u32[]{:S(2)}, u32[]{:S(2)}) async-start(bf16[32,144,128]{2,1,0:T(8,128)(2,1)} %bitcast.12), calls=%async_computation.2 | async-start | bytes 2359296 | tf_op jit(solution)/shard_map/all_to_all | solution.py:329
  61.1 14.5 %collective-permute-start.5 = (bf16[128,2560]{1,0:T(8,128)(2,1)S(1)}, bf16[128,2560]{1,0:T(8,128)(2,1)S(1)}, u32[]{:S(2)}, u32[]{:S(2)}) collective-permute-start(bf16[128,2560]{1,0:T(8,128)(2,1)S(1)} %get-tuple-element.25.trade), channel_id=1, source_target_pairs={{0,1},{1,0},{2,3},{3,2},{4,5},{5,4},{6,7},{7,6},{8,9},{9,8},{10,11... | collective-permute-start | bytes 1966088 | tf_op jit(solution)/shard_map/ppermute | solution.py:341
  63.2 12.3 %collective-permute-start.6 = (bf16[128,2048]{1,0:T(8,128)(2,1)S(1)}, bf16[128,2048]{1,0:T(8,128)(2,1)S(1)}, u32[]{:S(2)}, u32[]{:S(2)}) collective-permute-start(bf16[128,2048]{1,0:T(8,128)(2,1)S(1)} %get-tuple-element.26.grads), channel_id=1, source_target_pairs={{0,1},{1,0},{2,3},{3,2},{4,5},{5,4},{6,7},{7,6},{8,9},{9,8},{10,11... | collective-permute-start | bytes 1572872 | tf_op jit(solution)/shard_map/ppermute | solution.py:341
  65.4 16.3 %collective-permute-start.8 = (bf16[256,128]{1,0:T(8,128)(2,1)S(1)}, bf16[256,128]{1,0:T(8,128)(2,1)S(1)}, u32[]{:S(2)}, u32[]{:S(2)}) collective-permute-start(bf16[256,128]{1,0:T(8,128)(2,1)S(1)} %bitcast.32), channel_id=1, source_target_pairs={{0,496},{16,480},{32,464},{48,448},{64,432},{80,416},{96,400},{112... | collective-permute-start | bytes 196616 | tf_op jit(solution)/shard_map/ppermute | solution.py:286
  77.3 5.1 %copy-start.5 = (bf16[2,256,128]{2,1,0:T(8,128)(2,1)S(1)}, bf16[2,256,128]{2,1,0:T(8,128)(2,1)}, u32[]{:S(2)}) copy-start(bf16[2,256,128]{2,1,0:T(8,128)(2,1)} %copy-done.4) | copy-start | bytes 393220
  79.3 8.6 %collective-permute-start.7 = (bf16[256,128]{1,0:T(8,128)(2,1)S(1)}, bf16[256,128]{1,0:T(8,128)(2,1)S(1)}, u32[]{:S(2)}, u32[]{:S(2)}) collective-permute-start(bf16[256,128]{1,0:T(8,128)(2,1)S(1)} %shard_map.113), channel_id=1, source_target_pairs={{16,32},{32,16},{48,64},{64,48},{80,96},{96,80},{112,128},{128,112... | collective-permute-start | bytes 196616 | tf_op jit(solution)/shard_map/ppermute | solution.py:361

commit v6 on v5

--- a/solution.py
+++ b/solution.py
@@ -13,7 +13,6 @@
 
 BF = jnp.bfloat16
 F32 = jnp.float32
-ROWS = 16
 VMEM_LIMIT = 16 * 2**20
 
 
@@ -39,21 +38,6 @@
     rest = values - high.astype(F32)
     middle = rest.astype(BF)
     return high, middle, (rest - middle.astype(F32)).astype(BF)
-
-
-def columns_to_rows(columns):
-    lane = lax.broadcasted_iota(jnp.int32, (128, 128), 1)
-    wide = jnp.zeros((128, 128), F32)
-    for index, column in enumerate(columns):
-        wide = jnp.where(lane == index, column, wide)
-    high, middle, low = (part.astype(F32) for part in split_three(wide.T[:4]))
-    return jnp.concatenate([high, middle, low, jnp.zeros_like(high)], axis=0).astype(BF)
-
-
-def rows_to_columns(rows):
-    sums = rows[0:4] + rows[4:8] + rows[8:12]
-    tall = jnp.concatenate([sums, jnp.zeros((124, 128), F32)], axis=0).T
-    return [tall[:, index : index + 1] for index in range(4)]
 
 
 def norm_stats(blocks, width):
@@ -78,7 +62,7 @@
 
 
 def block_kernel(
-    spent, blocks, back, gain, weight_b, weight_a, *refs
+    chip_ref, spent, blocks, back, gain, weight_b, weight_a, *refs
 ):
     del spent
     *far, parts, middle, held, normed_ref, near_a_ref, far_a_ref, far_b_ref, sems = refs
@@ -143,10 +127,7 @@
         wide = pre_grad.astype(F32)
         plain += jnp.sum(wide * (gained[0:1] + gained[1:2] + gained[2:3]), axis=1, keepdims=True)
         moment += jnp.sum(wide * pre, axis=1, keepdims=True)
-    share = 1.0 / chips
-    rows = columns_to_rows([plain * (1.0 / width), moment * (1.0 / width), center * share, scale * share])
-    row = lax.broadcasted_iota(jnp.int32, rows.shape, 0)
-    plain_rows = jnp.where(row == 3, share, 0.0).astype(BF)
+    plain_mean, moment_mean = plain * (1.0 / width), moment * (1.0 / width)
     copies = []
     for chip in range(chips):
         cols = chip_cols(chip)
@@ -156,12 +137,15 @@
             act = middle[:, (2 + side) * units : (3 + side) * units]
             branch += dot(act, seconds[side][:, cols])
             term += dot(pre_grad, firsts[side][cols, :], ((1,), (1,)))
-        for kind, value, numbers in ((0, term * gain[:, cols], rows), (1, branch, plain_rows)):
+        hidden = (pair(back, chip, first_rows).astype(F32) - center) * scale
+        term = scale * (term * gain[:, cols] - plain_mean - hidden * moment_mean)
+        mine = chip_ref[0] == chip
+        term += jnp.where(mine, pair(blocks, chip, second_rows).astype(F32), 0.0)
+        branch += jnp.where(mine, pair(blocks, chip, first_rows).astype(F32), 0.0)
+        for kind, value in enumerate((term, branch)):
             place = kind * chips + chip
             for side in range(2):
-                start = side * (tokens + ROWS)
-                held[place, start : start + tokens, :] = value[:, side * 128 : side * 128 + 128].astype(BF)
-                held[place, start + tokens : start + tokens + ROWS, :] = numbers
+                held[place, side * tokens : side * tokens + tokens, :] = value[:, side * 128 : side * 128 + 128].astype(BF)
             copies.append(pltpu.make_async_copy(held.at[place], parts.at[place], sems.at[place]))
             copies[-1].start()
     for copy in copies:
@@ -202,31 +186,13 @@
         store.wait()
 
 
-def finish(parts, source, bases, values, result):
-    _, ranks, rows, _ = parts.shape
-    tokens = rows - ROWS
+def finish_kernel(which, parts, result):
+    _, ranks, tokens, _ = parts.shape
     for side in range(2):
-        total = parts[source, side].astype(F32)
+        total = parts[which[0], side].astype(F32)
         for rank in range(2 + side, ranks, 2):
-            total += parts[source, rank].astype(F32)
-        plain_mean, moment_mean, center, scale = rows_to_columns(total[tokens:])
-        hidden = (values[side].astype(F32) - center) * scale
-        change = scale * (total[:tokens] - plain_mean - hidden * moment_mean)
-        result[side * tokens : side * tokens + tokens, :] = (bases[side].astype(F32) + change).astype(BF)
-
-
-def across_kernel(odd_ref, parts, forward_in, grad_out, fetched, across):
-    odd = odd_ref[0]
-    tokens = fetched.shape[1]
-    halves = [slice(0, tokens), slice(tokens, 2 * tokens)]
-    bases = [jnp.where(odd == 1, forward_in[here, :], grad_out[here, :]) for here in halves]
-    finish(parts, odd, bases, [fetched[0], fetched[1]], across)
-
-
-def inside_kernel(odd_ref, parts, paired, inside):
-    tokens = inside.shape[0] // 2
-    halves = [slice(0, tokens), slice(tokens, 2 * tokens)]
-    finish(parts, 1 - odd_ref[0], [paired[0, here, :] for here in halves], [paired[1, here, :] for here in halves], inside)
+            total += parts[which[0], rank].astype(F32)
+        result[side * tokens : side * tokens + tokens, :] = total.astype(BF)
 
 
 def store_kernel(*refs):
@@ -294,22 +260,18 @@
     pieces = (weight_a, weight_b[:, : width // 2], weight_b[:, width // 2 :])
     far = [lax.ppermute(piece, "tensor", swap) for piece in pieces]
     mine = jnp.stack([value.reshape(2, half, shard_cols) for value in (forward_in, grad_out)], axis=1)
-    mine = jnp.pad(mine.reshape(2, tokens, shard_cols), ((0, 0), (0, 2 * ROWS), (0, 0)))
+    mine = mine.reshape(2, tokens, shard_cols)
     spread = jnp.broadcast_to(mine[None], (chips,) + mine.shape).reshape((ranks,) + mine.shape[1:])
     blocks = exchange(spread)
     back_spread = jnp.broadcast_to(fetched.reshape(1, 2, half, shard_cols), (chips, 2, half, shard_cols))
     blocks, back_spread = lax.optimization_barrier((blocks, back_spread.reshape(ranks, half, shard_cols)))
 
     back = exchange(back_spread)
-    section_odd = lax.rem(lax.axis_index("section"), 2)
-    sent = jnp.stack([jnp.where(section_odd == 1, grad_out, forward_in), fetched])
-    paired = lax.ppermute(sent, "section", [(s, s ^ 1) for s in range(sections)])
-    back, paired = lax.optimization_barrier((back, paired))
     parts, middle = call(
         block_kernel,
         (shape(spread.shape, BF), shape((half, 6 * hidden_units), BF)),
-        (spread, blocks, back, norm_gain, weight_b, weight_a, *far),
-        specs=hbm(1) + vmem(4) + hbm(1 + len(far)),
+        ((rank // 2).reshape(1), spread, blocks, back, norm_gain, weight_b, weight_a, *far),
+        specs=smem + hbm(1) + vmem(4) + hbm(1 + len(far)),
         out_specs=hbm(1) + vmem(1),
         scratch=(
             pltpu.VMEM(spread.shape, BF),
@@ -319,13 +281,13 @@
             pltpu.VMEM(weight_b.shape, BF),
             pltpu.SemaphoreType.DMA((ranks + 1 + len(far),)),
         ),
-        aliases={0: 0},
+        aliases={1: 0},
         flops=10 * tokens * width * hidden_units,
         nbytes=10 * 2**20,
     )
 
     planes = [[section * ranks + r for section in (first, first + 1) for r in range(ranks)] for first in range(0, sections, 2)]
-    block = (2, ranks, half + ROWS, shard_cols)
+    block = (2, ranks, half, shard_cols)
     collected = lax.all_to_all(
         parts.reshape((2 * ranks,) + block[2:]), ("section", "tensor"), 0, 0, tiled=True, axis_index_groups=planes
     ).reshape(block)
@@ -349,17 +311,11 @@
         nbytes=6 * 2**20,
     )
     piece = shape((tokens, shard_cols), BF)
-    odd_ref = section_odd.reshape(1)
+    odd_ref = lax.rem(lax.axis_index("section"), 2).reshape(1)
     collected, grad_a, grad_b = lax.optimization_barrier((collected, grad_a, grad_b))
-    across = call(
-        across_kernel,
-        (piece,),
-        (odd_ref, collected, forward_in, grad_out, back_spread[:2]),
-        specs=smem + vmem(4),
-        nbytes=2**20,
-    )[0]
+    across = call(finish_kernel, (piece,), (odd_ref, collected), specs=smem + vmem(1), nbytes=2**20)[0]
     across = lax.ppermute(across, "section", [(s, s + 1 if s % 2 else s - 1) for s in range(1, sections - 1)])
-    inside = call(inside_kernel, (piece,), (odd_ref, collected, paired), specs=smem + vmem(2), nbytes=2**20)[0]
+    inside = call(finish_kernel, (piece,), (1 - odd_ref, collected), specs=smem + vmem(1), nbytes=2**20)[0]
 
     def store(*values):
         count = len(values)

time: 89.4 us -> 87.6 us (0.980)
  the two profiles are of different devices: /device:TPU:128 before, /device:TPU:102 now
where the time goes in v6:
time: 87.6 us; the launch traced here: 86.9 us
  starting transfers between devices  57.1 us (65%)
  waiting for transfers between devices  11.4 us (13%)
  Pallas kernels  11 us (13%)
  local copies, waits for them, and re-layouts  5.01 us (6%)
  between operations  1.53 us (2%)
  other arithmetic  0.92 us (1%)
    all_to_all x2, starting transfers between devices, exchange(): return lax.all_to_all(blocks, 'tensor', 0, 0, tiled=True)  14.8 us
    ppermute x1, starting transfers between devices, per_device(): fetched = lax.ppermute(returned, 'section', mirror)  11.7 us
    pallas_call x7, Pallas kernels, call(): pl.pallas_call(kernel, out_shape=out_shapes, in_specs=specs or vmem(len(o...  11 us
    all_to_all x2, waiting for transfers between devices, exchange(): return lax.all_to_all(blocks, 'tensor', 0, 0, tiled=True)  8.67 us
    ppermute x1, starting transfers between devices, per_device(): parked = lax.ppermute(forward_in, 'section', mirror)  8.06 us
    all_to_all x1, starting transfers between devices, per_device(): lax.all_to_all(parts.reshape((2 * ranks,) + block[2:]), ('section', 'tens...  7.05 us
    ppermute x3, starting transfers between devices, per_device(): far = [lax.ppermute(piece, 'tensor', swap) for piece in pieces]  6.36 us
    ppermute x1, starting transfers between devices, per_device(): lax.ppermute(across, 'section', [(s, s + 1 if s % 2 else s - 1) for s in...  4.81 us
  transfers between devices with their start and end apart: 11, of which 2 were waited for; matrix products, arithmetic and copies ran while one was open for 2% of the time, Pallas kernels for 6%

profile of v6, /device:TPU:102, one launch (start us, length us, event | category | flops | bytes accessed | tf_op | source)
XLA Modules:
  0.0 86.9 jit_solution(5412110461704166090)
XLA Ops:
  0.6 0.0 copy-start
  0.6 0.9 %pad_maximum_fusion = bf16[2,2,128,128]{3,2,1,0:T(8,128)(2,1)S(1)} fusion(bf16[2,1,128,128]{3,2,1,0:T(8,128)(2,1)} %bitcast.32, bf16[2,1,128,128]{3,2,1,0:T(8,128)(2,1)} %bitcast.33), kind=kLoop, calls=%fused_computation | loop fusion | flops 65536 | bytes 262144 | tf_op jit(solution)/shard_map/stack | solution.py:262
  1.6 1.2 %broadcast_in_dim.30 = bf16[8,2,256,128]{3,2,1,0:T(8,128)(2,1)} broadcast(bf16[2,256,128]{2,1,0:T(8,128)(2,1)S(1)} %bitcast.29), dimensions={1,2,3} | broadcast | bytes 1179648 | tf_op jit(solution)/shard_map/broadcast_in_dim | solution.py:264
  2.8 0.0 copy-start.1
  2.8 7.6 %all-to-all-start = ((bf16[16,256,128]{2,1,0:T(8,128)(2,1)}), bf16[16,256,128]{2,1,0:T(8,128)(2,1)S(1)}, u32[]{:S(2)}, u32[]{:S(2)}) async-start(bf16[16,256,128]{2,1,0:T(8,128)(2,1)} %bitcast.5.spent), calls=%async_computation | async-start | bytes 2097152 | tf_op jit(solution)/shard_map/all_to_all | solution.py:258
  10.4 2.0 %collective-permute-start.1 = (bf16[2048,256]{1,0:T(8,128)(2,1)}, bf16[2048,256]{1,0:T(8,128)(2,1)}, u32[]{:S(2)}, u32[]{:S(2)}) collective-permute-start(bf16[2048,256]{1,0:T(8,128)(2,1)} %bitcast.11.weight_a), channel_id=1, source_target_pairs={{0,1},{1,0},{2,3},{3,2},{4,5},{5,4},{6,7},{7,6},{8,9},{9,8},{10,11... | collective-permute-start | bytes 3145736 | tf_op jit(solution)/shard_map/ppermute | solution.py:261
  13.1 0.0 copy-done
  13.1 11.7 %collective-permute-start = (bf16[256,128]{1,0:T(8,128)(2,1)S(1)}, bf16[256,128]{1,0:T(8,128)(2,1)S(1)}, u32[]{:S(2)}, u32[]{:S(2)}) collective-permute-start(bf16[256,128]{1,0:T(8,128)(2,1)S(1)} %dynamic-slice_bitcast_fusion), channel_id=1, source_target_pairs={{0,496},{16,480},{32,464},{48,448},{64,432},{80,416},{96,400},{112... | collective-permute-start | bytes 196616 | tf_op jit(solution)/shard_map/ppermute | solution.py:251
  24.8 0.0 copy-done.1
  24.8 1.1 %fusion = (bf16[256,1024]{1,0:T(8,128)(2,1)}, bf16[256,1024]{1,0:T(8,128)(2,1)}) fusion(bf16[256,2048]{1,0:T(8,128)(2,1)S(1)} %bitcast.26), kind=kLoop, calls=%fused_computation.2 | loop fusion | bytes 2097152 | tf_op jit(solution)/shard_map/slice | solution.py:260
  25.8 2.0 %collective-permute-start.2 = (bf16[256,1024]{1,0:T(8,128)(2,1)}, bf16[256,1024]{1,0:T(8,128)(2,1)S(1)}, u32[]{:S(2)}, u32[]{:S(2)}) collective-permute-start(bf16[256,1024]{1,0:T(8,128)(2,1)} %get-tuple-element.32), channel_id=1, source_target_pairs={{0,1},{1,0},{2,3},{3,2},{4,5},{5,4},{6,7},{7,6},{8,9},{9,8},{10,11... | collective-permute-start | bytes 1572872 | tf_op jit(solution)/shard_map/ppermute | solution.py:261
  27.8 2.4 %collective-permute-start.3 = (bf16[256,1024]{1,0:T(8,128)(2,1)}, bf16[256,1024]{1,0:T(8,128)(2,1)}, u32[]{:S(2)}, u32[]{:S(2)}) collective-permute-start(bf16[256,1024]{1,0:T(8,128)(2,1)} %get-tuple-element.31), channel_id=1, source_target_pairs={{0,1},{1,0},{2,3},{3,2},{4,5},{5,4},{6,7},{7,6},{8,9},{9,8},{10,11... | collective-permute-start | bytes 1572872 | tf_op jit(solution)/shard_map/ppermute | solution.py:261
  30.1 0.0 collective-permute-done
  30.2 0.0 all-to-all-done.blocks
  30.2 0.9 %broadcast_in_dim.32 = bf16[8,2,128,128]{3,2,1,0:T(8,128)(2,1)} broadcast(bf16[2,128,128]{2,1,0:T(8,128)(2,1)S(1)} %bitcast.30), dimensions={1,2,3} | broadcast | bytes 589824 | tf_op jit(solution)/shard_map/broadcast_in_dim | solution.py:266
  31.1 7.2 %all-to-all-start.1 = ((bf16[16,128,128]{2,1,0:T(8,128)(2,1)}), bf16[16,128,128]{2,1,0:T(8,128)(2,1)S(1)}, u32[]{:S(2)}, u32[]{:S(2)}) async-start(bf16[16,128,128]{2,1,0:T(8,128)(2,1)} %bitcast.28), calls=%async_computation.1 | async-start | bytes 1048576 | tf_op jit(solution)/shard_map/all_to_all | solution.py:258
  38.3 0.0 copy-start.4
  38.3 0.0 collective-permute-done.2.refs_1_
  38.3 0.0 copy-start.2
  38.3 0.8 copy-done.2
  39.1 0.0 collective-permute-done.3.refs_2_
  39.1 0.0 collective-permute-done.1.refs_0_
  39.1 8.7 %all-to-all-done.1.back = bf16[16,128,128]{2,1,0:T(8,128)(2,1)S(1)} async-done(((bf16[16,128,128]{2,1,0:T(8,128)(2,1)}), bf16[16,128,128]{2,1,0:T(8,128)(2,1)S(1)}, u32[]{:S(2)}, u32[]{:S(2)}) %all-to-all-start.1) | async-done | bytes 524320 | tf_op jit(solution)/shard_map/all_to_all | solution.py:258
  47.8 0.0 copy-done.4
  47.8 0.0 copy-start.3
  47.8 1.0 %copy-done.3 = bf16[256,1024]{1,0:T(8,128)(2,1)S(1)} copy-done((bf16[256,1024]{1,0:T(8,128)(2,1)S(1)}, bf16[256,1024]{1,0:T(8,128)(2,1)}, u32[]{:S(2)}) %copy-start.3) | copy-done | bytes 524312
  48.8 5.2 %shard_map.110 = (bf16[16,256,128]{2,1,0:T(8,128)(2,1)}, bf16[128,1536]{1,0:T(8,128)(2,1)S(1)}) custom-call(s32[1]{0:T(128)} %bitcast.1.chip_ref, bf16[16,256,128]{2,1,0:T(8,128)(2,1)} %bitcast.5.spent, bf16[16,256,128]{2,1,0:T(8,128)(2,1)S(1)} %all-to-all-done.blocks, ...), custom_call_target="tpu_custom_call", output_to_operand_aliasing={{0}: (1, {})} | custom-call | flops 1342177280 | bytes 10485760 | tf_op jit(solution)/shard_map/pallas_call | solution.py:223
  54.0 7.1 %all-to-all-start.2 = ((bf16[32,128,128]{2,1,0:T(8,128)(2,1)}), bf16[32,128,128]{2,1,0:T(8,128)(2,1)S(1)}, u32[]{:S(2)}, u32[]{:S(2)}) async-start(bf16[32,128,128]{2,1,0:T(8,128)(2,1)} %bitcast.12), calls=%async_computation.2 | async-start | bytes 2097152 | tf_op jit(solution)/shard_map/all_to_all | solution.py:291
  61.1 0.0 copy-start.5
  61.1 1.4 %shard_map.111 = (bf16[128,2560]{1,0:T(8,128)(2,1)}, bf16[128,2048]{1,0:T(8,128)(2,1)}) custom-call(bf16[16,256,128]{2,1,0:T(8,128)(2,1)S(1)} %all-to-all-done.blocks, bf16[16,128,128]{2,1,0:T(8,128)(2,1)S(1)} %all-to-all-done.1.back, bf16[128,1536]{1,0:T(8,128)(2,1)S(1)} %get-tuple-element.21.middle, f32[1,2048]{1,0:T(1,128)S(1)} %copy-done.4), custom_call_target="tpu_custom_call" | custom-call | bytes 4194304 | tf_op jit(solution)/shard_map/pallas_call | solution.py:223
  62.5 2.0 %collective-permute-start.4 = (bf16[128,2560]{1,0:T(8,128)(2,1)}, bf16[128,2560]{1,0:T(8,128)(2,1)S(1)}, u32[]{:S(2)}, u32[]{:S(2)}) collective-permute-start(bf16[128,2560]{1,0:T(8,128)(2,1)} %get-tuple-element.22.trade), channel_id=1, source_target_pairs={{0,1},{1,0},{2,3},{3,2},{4,5},{5,4},{6,7},{7,6},{8,9},{9,8},{10,11... | collective-permute-start | bytes 1966088 | tf_op jit(solution)/shard_map/ppermute | solution.py:303
  64.5 2.3 %collective-permute-start.5 = (bf16[128,2048]{1,0:T(8,128)(2,1)}, bf16[128,2048]{1,0:T(8,128)(2,1)S(1)}, u32[]{:S(2)}, u32[]{:S(2)}) collective-permute-start(bf16[128,2048]{1,0:T(8,128)(2,1)} %get-tuple-element.23.grads), channel_id=1, source_target_pairs={{0,1},{1,0},{2,3},{3,2},{4,5},{5,4},{6,7},{7,6},{8,9},{9,8},{10,11... | collective-permute-start | bytes 1572872 | tf_op jit(solution)/shard_map/ppermute | solution.py:303
  66.8 0.0 copy-done.5
  66.8 8.1 %collective-permute-start.7 = (bf16[256,128]{1,0:T(8,128)(2,1)S(1)}, bf16[256,128]{1,0:T(8,128)(2,1)S(1)}, u32[]{:S(2)}, u32[]{:S(2)}) collective-permute-start(bf16[256,128]{1,0:T(8,128)(2,1)S(1)} %bitcast.34), channel_id=1, source_target_pairs={{0,496},{16,480},{32,464},{48,448},{64,432},{80,416},{96,400},{112... | collective-permute-start | bytes 196616 | tf_op jit(solution)/shard_map/ppermute | solution.py:252
  74.9 0.0 collective-permute-done.5.far_grads
  74.9 0.0 collective-permute-done.4.received
  74.9 2.9 %shard_map.112 = (bf16[2048,256]{1,0:T(8,128)(2,1)}, bf16[256,2048]{1,0:T(8,128)(2,1)}) custom-call(bf16[128,2560]{1,0:T(8,128)(2,1)} %get-tuple-element.22.trade, bf16[128,2560]{1,0:T(8,128)(2,1)S(1)} %collective-permute-done.4.received, bf16[128,1536]{1,0:T(8,128)(2,1)S(1)} %get-tuple-element.21.middle, bf16[128,2048]{1,0:T(8,128)(2,1)} %get-tuple-element.23.grads, ...), custom_call_target="tpu_custom_call" | custom-call | flops 536870912 | bytes 6291456 | tf_op jit(solution)/shard_map/pallas_call | solution.py:223
  77.9 0.0 all-to-all-done.2
  77.9 0.1 shard_map.113
  77.9 4.8 %collective-permute-start.6 = (bf16[256,128]{1,0:T(8,128)(2,1)S(1)}, bf16[256,128]{1,0:T(8,128)(2,1)S(1)}, u32[]{:S(2)}, u32[]{:S(2)}) collective-permute-start(bf16[256,128]{1,0:T(8,128)(2,1)S(1)} %shard_map.113), channel_id=1, source_target_pairs={{16,32},{32,16},{48,64},{64,48},{80,96},{96,80},{112,128},{128,112... | collective-permute-start | bytes 196616 | tf_op jit(solution)/shard_map/ppermute | solution.py:317
  82.8 0.0 collective-permute-done.7.refs_0_
  82.8 0.6 shard_map.116
  83.4 0.1 shard_map.114.inside
  83.5 2.7 %collective-permute-done.6.across = bf16[256,128]{1,0:T(8,128)(2,1)S(1)} collective-permute-done((bf16[256,128]{1,0:T(8,128)(2,1)S(1)}, bf16[256,128]{1,0:T(8,128)(2,1)S(1)}, u32[]{:S(2)}, u32[]{:S(2)}) %collective-permute-start.6) | collective-permute-done | bytes 65568 | tf_op jit(solution)/shard_map/ppermute | solution.py:317
  86.2 0.7 shard_map.115
  (1 shorter events, 0.0 us)
Async XLA Ops:
  0.6 12.4 %copy-start = (bf16[1,2,256,128]{3,2,1,0:T(8,128)(2,1)S(1)}, bf16[1,2,256,128]{3,2,1,0:T(8,128)(2,1)}, u32[]{:S(2)}) copy-start(bf16[1,2,256,128]{3,2,1,0:T(8,128)(2,1)} %param.9) | copy-start | bytes 393220
  2.8 22.0 %copy-start.1 = (bf16[1,256,2048]{2,1,0:T(8,128)(2,1)S(1)}, bf16[1,256,2048]{2,1,0:T(8,128)(2,1)}, u32[]{:S(2)}) copy-start(bf16[1,256,2048]{2,1,0:T(8,128)(2,1)} %param.13) | copy-start | bytes 3145732
  2.8 27.4 %all-to-all-start = ((bf16[16,256,128]{2,1,0:T(8,128)(2,1)}), bf16[16,256,128]{2,1,0:T(8,128)(2,1)S(1)}, u32[]{:S(2)}, u32[]{:S(2)}) async-start(bf16[16,256,128]{2,1,0:T(8,128)(2,1)} %bitcast.5.spent), calls=%async_computation | async-start | bytes 2097152 | tf_op jit(solution)/shard_map/all_to_all | solution.py:258
  10.4 28.8 %collective-permute-start.1 = (bf16[2048,256]{1,0:T(8,128)(2,1)}, bf16[2048,256]{1,0:T(8,128)(2,1)}, u32[]{:S(2)}, u32[]{:S(2)}) collective-permute-start(bf16[2048,256]{1,0:T(8,128)(2,1)} %bitcast.11.weight_a), channel_id=1, source_target_pairs={{0,1},{1,0},{2,3},{3,2},{4,5},{5,4},{6,7},{7,6},{8,9},{9,8},{10,11... | collective-permute-start | bytes 3145736 | tf_op jit(solution)/shard_map/ppermute | solution.py:261
  13.1 17.1 %collective-permute-start = (bf16[256,128]{1,0:T(8,128)(2,1)S(1)}, bf16[256,128]{1,0:T(8,128)(2,1)S(1)}, u32[]{:S(2)}, u32[]{:S(2)}) collective-permute-start(bf16[256,128]{1,0:T(8,128)(2,1)S(1)} %dynamic-slice_bitcast_fusion), channel_id=1, source_target_pairs={{0,496},{16,480},{32,464},{48,448},{64,432},{80,416},{96,400},{112... | collective-permute-start | bytes 196616 | tf_op jit(solution)/shard_map/ppermute | solution.py:251
  25.8 12.5 %collective-permute-start.2 = (bf16[256,1024]{1,0:T(8,128)(2,1)}, bf16[256,1024]{1,0:T(8,128)(2,1)S(1)}, u32[]{:S(2)}, u32[]{:S(2)}) collective-permute-start(bf16[256,1024]{1,0:T(8,128)(2,1)} %get-tuple-element.32), channel_id=1, source_target_pairs={{0,1},{1,0},{2,3},{3,2},{4,5},{5,4},{6,7},{7,6},{8,9},{9,8},{10,11... | collective-permute-start | bytes 1572872 | tf_op jit(solution)/shard_map/ppermute | solution.py:261
  27.8 11.3 %collective-permute-start.3 = (bf16[256,1024]{1,0:T(8,128)(2,1)}, bf16[256,1024]{1,0:T(8,128)(2,1)}, u32[]{:S(2)}, u32[]{:S(2)}) collective-permute-start(bf16[256,1024]{1,0:T(8,128)(2,1)} %get-tuple-element.31), channel_id=1, source_target_pairs={{0,1},{1,0},{2,3},{3,2},{4,5},{5,4},{6,7},{7,6},{8,9},{9,8},{10,11... | collective-permute-start | bytes 1572872 | tf_op jit(solution)/shard_map/ppermute | solution.py:261
  31.1 16.7 %all-to-all-start.1 = ((bf16[16,128,128]{2,1,0:T(8,128)(2,1)}), bf16[16,128,128]{2,1,0:T(8,128)(2,1)S(1)}, u32[]{:S(2)}, u32[]{:S(2)}) async-start(bf16[16,128,128]{2,1,0:T(8,128)(2,1)} %bitcast.28), calls=%async_computation.1 | async-start | bytes 1048576 | tf_op jit(solution)/shard_map/all_to_all | solution.py:258
  38.3 9.5 %copy-start.4 = (f32[1,2048]{1,0:T(1,128)S(1)}, f32[1,2048]{1,0:T(1,128)}, u32[]{:S(2)}) copy-start(f32[1,2048]{1,0:T(1,128)} %gain.3) | copy-start | bytes 24580
  38.3 0.8 copy-start.2
  47.8 1.0 %copy-start.3 = (bf16[256,1024]{1,0:T(8,128)(2,1)S(1)}, bf16[256,1024]{1,0:T(8,128)(2,1)}, u32[]{:S(2)}) copy-start(bf16[256,1024]{1,0:T(8,128)(2,1)} %copy-done.2) | copy-start | bytes 1572868
  54.0 23.8 %all-to-all-start.2 = ((bf16[32,128,128]{2,1,0:T(8,128)(2,1)}), bf16[32,128,128]{2,1,0:T(8,128)(2,1)S(1)}, u32[]{:S(2)}, u32[]{:S(2)}) async-start(bf16[32,128,128]{2,1,0:T(8,128)(2,1)} %bitcast.12), calls=%async_computation.2 | async-start | bytes 2097152 | tf_op jit(solution)/shard_map/all_to_all | solution.py:291
  61.1 5.7 %copy-start.5 = (bf16[1,256,128]{2,1,0:T(8,128)(2,1)S(1)}, bf16[1,256,128]{2,1,0:T(8,128)(2,1)}, u32[]{:S(2)}) copy-start(bf16[1,256,128]{2,1,0:T(8,128)(2,1)} %param.7) | copy-start | bytes 196612
  62.5 12.4 %collective-permute-start.4 = (bf16[128,2560]{1,0:T(8,128)(2,1)}, bf16[128,2560]{1,0:T(8,128)(2,1)S(1)}, u32[]{:S(2)}, u32[]{:S(2)}) collective-permute-start(bf16[128,2560]{1,0:T(8,128)(2,1)} %get-tuple-element.22.trade), channel_id=1, source_target_pairs={{0,1},{1,0},{2,3},{3,2},{4,5},{5,4},{6,7},{7,6},{8,9},{9,8},{10,11... | collective-permute-start | bytes 1966088 | tf_op jit(solution)/shard_map/ppermute | solution.py:303
  64.5 10.4 %collective-permute-start.5 = (bf16[128,2048]{1,0:T(8,128)(2,1)}, bf16[128,2048]{1,0:T(8,128)(2,1)S(1)}, u32[]{:S(2)}, u32[]{:S(2)}) collective-permute-start(bf16[128,2048]{1,0:T(8,128)(2,1)} %get-tuple-element.23.grads), channel_id=1, source_target_pairs={{0,1},{1,0},{2,3},{3,2},{4,5},{5,4},{6,7},{7,6},{8,9},{9,8},{10,11... | collective-permute-start | bytes 1572872 | tf_op jit(solution)/shard_map/ppermute | solution.py:303
  66.8 15.9 %collective-permute-start.7 = (bf16[256,128]{1,0:T(8,128)(2,1)S(1)}, bf16[256,128]{1,0:T(8,128)(2,1)S(1)}, u32[]{:S(2)}, u32[]{:S(2)}) collective-permute-start(bf16[256,128]{1,0:T(8,128)(2,1)S(1)} %bitcast.34), channel_id=1, source_target_pairs={{0,496},{16,480},{32,464},{48,448},{64,432},{80,416},{96,400},{112... | collective-permute-start | bytes 196616 | tf_op jit(solution)/shard_map/ppermute | solution.py:252
  77.9 8.3 %collective-permute-start.6 = (bf16[256,128]{1,0:T(8,128)(2,1)S(1)}, bf16[256,128]{1,0:T(8,128)(2,1)S(1)}, u32[]{:S(2)}, u32[]{:S(2)}) collective-permute-start(bf16[256,128]{1,0:T(8,128)(2,1)S(1)} %shard_map.113), channel_id=1, source_target_pairs={{16,32},{32,16},{48,64},{64,48},{80,96},{96,80},{112,128},{128,112... | collective-permute-start | bytes 196616 | tf_op jit(solution)/shard_map/ppermute | solution.py:317

commit v7 on v6

--- a/solution.py
+++ b/solution.py
@@ -152,7 +152,7 @@
         copy.wait()
 
 
-def trade_kernel(blocks, back, middle, gain, trade, grads):
+def trade_kernel(back, middle, gain, trade):
     ranks, tokens, _ = back.shape
     width = 128 * ranks
     units = middle.shape[1] // 6
@@ -161,9 +161,14 @@
         cols = chip_cols(chip)
         value = jnp.concatenate([back[2 * chip], back[2 * chip + 1]], axis=1).astype(F32)
         trade[:, cols] = ((value - center) * scale * gain[:, cols]).astype(BF)
-        grads[:, cols] = jnp.concatenate([blocks[2 * chip + side, tokens : 2 * tokens, :] for side in range(2)], axis=1)
     trade[:, width : width + units] = middle[:, units : 2 * units]
     trade[:, width + units :] = middle[:, 5 * units :]
+
+
+def grads_kernel(blocks, grads):
+    ranks, rows, _ = blocks.shape
+    for rank in range(ranks):
+        grads[:, rank * 128 : rank * 128 + 128] = blocks[rank, rows // 2 :, :]
 
 
 def weights_kernel(trade, received, middle, grads, far_grads, grad_a, grad_b, keep_a, keep_b, sems):
@@ -291,12 +296,13 @@
     collected = lax.all_to_all(
         parts.reshape((2 * ranks,) + block[2:]), ("section", "tensor"), 0, 0, tiled=True, axis_index_groups=planes
     ).reshape(block)
-    trade, grads = call(
+    trade = call(
         trade_kernel,
-        (shape((half, width + 2 * hidden_units), BF), shape((half, width), BF)),
-        (blocks, back, middle, norm_gain),
-        nbytes=4 * 2**20,
-    )
+        (shape((half, width + 2 * hidden_units), BF),),
+        (back, middle, norm_gain),
+        nbytes=2 * 2**20,
+    )[0]
+    grads = call(grads_kernel, (shape((half, width), BF),), (blocks,), nbytes=2 * 2**20)[0]
     grad_a, grad_b = call(
         weights_kernel,
         (shape(weight_a.shape, BF), shape(weight_b.shape, BF)),

time: 87.6 us -> 88.6 us (1.011)
  Pallas kernels: 11 us -> 9.98 us
  local copies, waits for them, and re-layouts: 5.01 us -> 5.9 us
    pallas_call x7 -> x8, Pallas kernels: 11 us -> 9.98 us  [call(): pl.pallas_call(kernel, out_shape=out_shapes, in_specs=specs or vmem(len(o...]
    unnamed x12 -> x14, local copies, waits for them, and re-layouts: 1.86 us -> 2.75 us
  transfers between devices with their start and end apart: 11 -> 11, of which waited for: 2 -> 2; matrix products, arithmetic and copies ran while one was open for 2% -> 2% of each run, Pallas kernels for 6% -> 5%
where the time goes in v7:
time: 88.6 us; the launch traced here: 87.8 us
  starting transfers between devices  57.2 us (65%)
  waiting for transfers between devices  12.2 us (14%)
  Pallas kernels  9.98 us (11%)
  local copies, waits for them, and re-layouts  5.9 us (7%)
  between operations  1.57 us (2%)
  other arithmetic  0.92 us (1%)
    all_to_all x2, starting transfers between devices, exchange(): return lax.all_to_all(blocks, 'tensor', 0, 0, tiled=True)  14.8 us
    ppermute x1, starting transfers between devices, per_device(): fetched = lax.ppermute(returned, 'section', mirror)  11.7 us
    pallas_call x8, Pallas kernels, call(): pl.pallas_call(kernel, out_shape=out_shapes, in_specs=specs or vmem(len(o...  9.98 us
    all_to_all x2, waiting for transfers between devices, exchange(): return lax.all_to_all(blocks, 'tensor', 0, 0, tiled=True)  9.45 us
    ppermute x1, starting transfers between devices, per_device(): parked = lax.ppermute(forward_in, 'section', mirror)  8.06 us
    all_to_all x1, starting transfers between devices, per_device(): lax.all_to_all(parts.reshape((2 * ranks,) + block[2:]), ('section', 'tens...  7.04 us
    ppermute x3, starting transfers between devices, per_device(): far = [lax.ppermute(piece, 'tensor', swap) for piece in pieces]  6.36 us
    ppermute x1, starting transfers between devices, per_device(): lax.ppermute(across, 'section', [(s, s + 1 if s % 2 else s - 1) for s in...  4.81 us
  transfers between devices with their start and end apart: 11, of which 2 were waited for; matrix products, arithmetic and copies ran while one was open for 2% of the time, Pallas kernels for 5%

profile of v7, /device:TPU:102, one launch (start us, length us, event | category | flops | bytes accessed | tf_op | source)
XLA Modules:
  0.0 87.8 jit_solution(16518769238000174549)
XLA Ops:
  0.6 0.0 copy-start
  0.6 0.9 %pad_maximum_fusion = bf16[2,2,128,128]{3,2,1,0:T(8,128)(2,1)S(1)} fusion(bf16[2,1,128,128]{3,2,1,0:T(8,128)(2,1)} %bitcast.32, bf16[2,1,128,128]{3,2,1,0:T(8,128)(2,1)} %bitcast.33), kind=kLoop, calls=%fused_computation | loop fusion | flops 65536 | bytes 262144 | tf_op jit(solution)/shard_map/stack | solution.py:267
  1.6 1.2 %broadcast_in_dim.30 = bf16[8,2,256,128]{3,2,1,0:T(8,128)(2,1)} broadcast(bf16[2,256,128]{2,1,0:T(8,128)(2,1)S(1)} %bitcast.29), dimensions={1,2,3} | broadcast | bytes 1179648 | tf_op jit(solution)/shard_map/broadcast_in_dim | solution.py:269
  2.8 0.0 copy-start.1
  2.8 7.6 %all-to-all-start = ((bf16[16,256,128]{2,1,0:T(8,128)(2,1)}), bf16[16,256,128]{2,1,0:T(8,128)(2,1)S(1)}, u32[]{:S(2)}, u32[]{:S(2)}) async-start(bf16[16,256,128]{2,1,0:T(8,128)(2,1)} %bitcast.5.spent), calls=%async_computation | async-start | bytes 2097152 | tf_op jit(solution)/shard_map/all_to_all | solution.py:263
  10.4 2.0 %collective-permute-start.1 = (bf16[2048,256]{1,0:T(8,128)(2,1)}, bf16[2048,256]{1,0:T(8,128)(2,1)}, u32[]{:S(2)}, u32[]{:S(2)}) collective-permute-start(bf16[2048,256]{1,0:T(8,128)(2,1)} %bitcast.11.weight_a), channel_id=1, source_target_pairs={{0,1},{1,0},{2,3},{3,2},{4,5},{5,4},{6,7},{7,6},{8,9},{9,8},{10,11... | collective-permute-start | bytes 3145736 | tf_op jit(solution)/shard_map/ppermute | solution.py:266
  13.1 0.0 copy-done
  13.1 11.7 %collective-permute-start = (bf16[256,128]{1,0:T(8,128)(2,1)S(1)}, bf16[256,128]{1,0:T(8,128)(2,1)S(1)}, u32[]{:S(2)}, u32[]{:S(2)}) collective-permute-start(bf16[256,128]{1,0:T(8,128)(2,1)S(1)} %dynamic-slice_bitcast_fusion), channel_id=1, source_target_pairs={{0,496},{16,480},{32,464},{48,448},{64,432},{80,416},{96,400},{112... | collective-permute-start | bytes 196616 | tf_op jit(solution)/shard_map/ppermute | solution.py:256
  24.8 0.0 copy-done.1
  24.8 1.1 %fusion = (bf16[256,1024]{1,0:T(8,128)(2,1)}, bf16[256,1024]{1,0:T(8,128)(2,1)}) fusion(bf16[256,2048]{1,0:T(8,128)(2,1)S(1)} %bitcast.26), kind=kLoop, calls=%fused_computation.2 | loop fusion | bytes 2097152 | tf_op jit(solution)/shard_map/slice | solution.py:265
  25.8 2.0 %collective-permute-start.2 = (bf16[256,1024]{1,0:T(8,128)(2,1)}, bf16[256,1024]{1,0:T(8,128)(2,1)S(1)}, u32[]{:S(2)}, u32[]{:S(2)}) collective-permute-start(bf16[256,1024]{1,0:T(8,128)(2,1)} %get-tuple-element.28), channel_id=1, source_target_pairs={{0,1},{1,0},{2,3},{3,2},{4,5},{5,4},{6,7},{7,6},{8,9},{9,8},{10,11... | collective-permute-start | bytes 1572872 | tf_op jit(solution)/shard_map/ppermute | solution.py:266
  27.8 2.4 %collective-permute-start.3 = (bf16[256,1024]{1,0:T(8,128)(2,1)}, bf16[256,1024]{1,0:T(8,128)(2,1)}, u32[]{:S(2)}, u32[]{:S(2)}) collective-permute-start(bf16[256,1024]{1,0:T(8,128)(2,1)} %get-tuple-element.27), channel_id=1, source_target_pairs={{0,1},{1,0},{2,3},{3,2},{4,5},{5,4},{6,7},{7,6},{8,9},{9,8},{10,11... | collective-permute-start | bytes 1572872 | tf_op jit(solution)/shard_map/ppermute | solution.py:266
  30.1 0.0 collective-permute-done
  30.2 0.0 all-to-all-done.blocks
  30.2 0.9 %broadcast_in_dim.32 = bf16[8,2,128,128]{3,2,1,0:T(8,128)(2,1)} broadcast(bf16[2,128,128]{2,1,0:T(8,128)(2,1)S(1)} %bitcast.30), dimensions={1,2,3} | broadcast | bytes 589824 | tf_op jit(solution)/shard_map/broadcast_in_dim | solution.py:271
  31.1 7.2 %all-to-all-start.1 = ((bf16[16,128,128]{2,1,0:T(8,128)(2,1)}), bf16[16,128,128]{2,1,0:T(8,128)(2,1)S(1)}, u32[]{:S(2)}, u32[]{:S(2)}) async-start(bf16[16,128,128]{2,1,0:T(8,128)(2,1)} %bitcast.28), calls=%async_computation.1 | async-start | bytes 1048576 | tf_op jit(solution)/shard_map/all_to_all | solution.py:263
  38.3 0.0 copy-start.5
  38.3 0.0 collective-permute-done.2.refs_1_
  38.3 0.0 collective-permute-done.3.refs_2_
  38.3 0.0 collective-permute-done.1.refs_0_
  38.3 9.4 %all-to-all-done.1.back = bf16[16,128,128]{2,1,0:T(8,128)(2,1)S(1)} async-done(((bf16[16,128,128]{2,1,0:T(8,128)(2,1)}), bf16[16,128,128]{2,1,0:T(8,128)(2,1)S(1)}, u32[]{:S(2)}, u32[]{:S(2)}) %all-to-all-start.1) | async-done | bytes 524320 | tf_op jit(solution)/shard_map/all_to_all | solution.py:263
  47.8 0.0 copy-done.5
  47.8 5.3 %shard_map.110 = (bf16[16,256,128]{2,1,0:T(8,128)(2,1)}, bf16[128,1536]{1,0:T(8,128)(2,1)S(1)}) custom-call(s32[1]{0:T(128)} %bitcast.1.chip_ref, bf16[16,256,128]{2,1,0:T(8,128)(2,1)} %bitcast.5.spent, bf16[16,256,128]{2,1,0:T(8,128)(2,1)S(1)} %all-to-all-done.blocks, ...), custom_call_target="tpu_custom_call", output_to_operand_aliasing={{0}: (1, {})} | custom-call | flops 1342177280 | bytes 10485760 | tf_op jit(solution)/shard_map/pallas_call | solution.py:228
  53.1 0.0 copy-start.2
  53.1 0.7 copy-done.2
  53.8 7.0 %all-to-all-start.2 = ((bf16[32,128,128]{2,1,0:T(8,128)(2,1)}), bf16[32,128,128]{2,1,0:T(8,128)(2,1)S(1)}, u32[]{:S(2)}, u32[]{:S(2)}) async-start(bf16[32,128,128]{2,1,0:T(8,128)(2,1)} %bitcast.12), calls=%async_computation.2 | async-start | bytes 2097152 | tf_op jit(solution)/shard_map/all_to_all | solution.py:296
  60.9 0.0 copy-start.3
  60.9 1.0 %copy-done.3 = bf16[128,1536]{1,0:T(8,128)(2,1)S(1)} copy-done((bf16[128,1536]{1,0:T(8,128)(2,1)S(1)}, bf16[128,1536]{1,0:T(8,128)(2,1)}, u32[]{:S(2)}) %copy-start.3) | copy-done | bytes 393240
  61.9 0.3 shard_map.111.trade
  62.2 0.0 copy-start.6
  62.2 2.2 %collective-permute-start.4 = (bf16[128,2560]{1,0:T(8,128)(2,1)S(1)}, bf16[128,2560]{1,0:T(8,128)(2,1)}, u32[]{:S(2)}, u32[]{:S(2)}) collective-permute-start(bf16[128,2560]{1,0:T(8,128)(2,1)S(1)} %shard_map.111.trade), channel_id=1, source_target_pairs={{0,1},{1,0},{2,3},{3,2},{4,5},{5,4},{6,7},{7,6},{8,9},{9,8},{10,11... | collective-permute-start | bytes 1966088 | tf_op jit(solution)/shard_map/ppermute | solution.py:309
  64.4 0.1 shard_map.112.grads
  64.6 2.3 %collective-permute-start.5 = (bf16[128,2048]{1,0:T(8,128)(2,1)S(1)}, bf16[128,2048]{1,0:T(8,128)(2,1)S(1)}, u32[]{:S(2)}, u32[]{:S(2)}) collective-permute-start(bf16[128,2048]{1,0:T(8,128)(2,1)S(1)} %shard_map.112.grads), channel_id=1, source_target_pairs={{0,1},{1,0},{2,3},{3,2},{4,5},{5,4},{6,7},{7,6},{8,9},{9,8},{10,11... | collective-permute-start | bytes 1572872 | tf_op jit(solution)/shard_map/ppermute | solution.py:309
  66.8 0.0 copy-done.6
  66.8 8.1 %collective-permute-start.7 = (bf16[256,128]{1,0:T(8,128)(2,1)S(1)}, bf16[256,128]{1,0:T(8,128)(2,1)S(1)}, u32[]{:S(2)}, u32[]{:S(2)}) collective-permute-start(bf16[256,128]{1,0:T(8,128)(2,1)S(1)} %bitcast.34), channel_id=1, source_target_pairs={{0,496},{16,480},{32,464},{48,448},{64,432},{80,416},{96,400},{112... | collective-permute-start | bytes 196616 | tf_op jit(solution)/shard_map/ppermute | solution.py:257
  74.9 0.0 collective-permute-done.5.far_grads
  74.9 0.0 collective-permute-done.4.received
  74.9 0.0 copy-start.4
  74.9 1.0 %copy-done.4 = bf16[128,1536]{1,0:T(8,128)(2,1)S(1)} copy-done((bf16[128,1536]{1,0:T(8,128)(2,1)S(1)}, bf16[128,1536]{1,0:T(8,128)(2,1)}, u32[]{:S(2)}) %copy-start.4) | copy-done | bytes 393240
  75.9 2.8 %shard_map.113 = (bf16[2048,256]{1,0:T(8,128)(2,1)}, bf16[256,2048]{1,0:T(8,128)(2,1)}) custom-call(bf16[128,2560]{1,0:T(8,128)(2,1)S(1)} %shard_map.111.trade, bf16[128,2560]{1,0:T(8,128)(2,1)} %collective-permute-done.4.received, bf16[128,1536]{1,0:T(8,128)(2,1)S(1)} %copy-done.4, bf16[128,2048]{1,0:T(8,128)(2,1)S(1)} %shard_map.112.grads, ...), custom_call_target="tpu_custom_call" | custom-call | flops 536870912 | bytes 6291456 | tf_op jit(solution)/shard_map/pallas_call | solution.py:228
  78.7 0.0 all-to-all-done.2
  78.7 0.1 shard_map.114
  78.8 4.8 %collective-permute-start.6 = (bf16[256,128]{1,0:T(8,128)(2,1)S(1)}, bf16[256,128]{1,0:T(8,128)(2,1)S(1)}, u32[]{:S(2)}, u32[]{:S(2)}) collective-permute-start(bf16[256,128]{1,0:T(8,128)(2,1)S(1)} %shard_map.114), channel_id=1, source_target_pairs={{16,32},{32,16},{48,64},{64,48},{80,96},{96,80},{112,128},{128,112... | collective-permute-start | bytes 196616 | tf_op jit(solution)/shard_map/ppermute | solution.py:323
  83.6 0.0 collective-permute-done.7.refs_0_
  83.6 0.6 shard_map.117
  84.3 0.1 shard_map.115.inside
  84.4 2.7 %collective-permute-done.6.across = bf16[256,128]{1,0:T(8,128)(2,1)S(1)} collective-permute-done((bf16[256,128]{1,0:T(8,128)(2,1)S(1)}, bf16[256,128]{1,0:T(8,128)(2,1)S(1)}, u32[]{:S(2)}, u32[]{:S(2)}) %collective-permute-start.6) | collective-permute-done | bytes 65568 | tf_op jit(solution)/shard_map/ppermute | solution.py:323
  87.1 0.7 shard_map.116
  (1 shorter events, 0.0 us)
Async XLA Ops:
  0.6 12.4 %copy-start = (bf16[1,2,256,128]{3,2,1,0:T(8,128)(2,1)S(1)}, bf16[1,2,256,128]{3,2,1,0:T(8,128)(2,1)}, u32[]{:S(2)}) copy-start(bf16[1,2,256,128]{3,2,1,0:T(8,128)(2,1)} %param.9) | copy-start | bytes 393220
  2.8 22.0 %copy-start.1 = (bf16[1,256,2048]{2,1,0:T(8,128)(2,1)S(1)}, bf16[1,256,2048]{2,1,0:T(8,128)(2,1)}, u32[]{:S(2)}) copy-start(bf16[1,256,2048]{2,1,0:T(8,128)(2,1)} %param.13) | copy-start | bytes 3145732
  2.8 27.4 %all-to-all-start = ((bf16[16,256,128]{2,1,0:T(8,128)(2,1)}), bf16[16,256,128]{2,1,0:T(8,128)(2,1)S(1)}, u32[]{:S(2)}, u32[]{:S(2)}) async-start(bf16[16,256,128]{2,1,0:T(8,128)(2,1)} %bitcast.5.spent), calls=%async_computation | async-start | bytes 2097152 | tf_op jit(solution)/shard_map/all_to_all | solution.py:263
  10.4 28.0 %collective-permute-start.1 = (bf16[2048,256]{1,0:T(8,128)(2,1)}, bf16[2048,256]{1,0:T(8,128)(2,1)}, u32[]{:S(2)}, u32[]{:S(2)}) collective-permute-start(bf16[2048,256]{1,0:T(8,128)(2,1)} %bitcast.11.weight_a), channel_id=1, source_target_pairs={{0,1},{1,0},{2,3},{3,2},{4,5},{5,4},{6,7},{7,6},{8,9},{9,8},{10,11... | collective-permute-start | bytes 3145736 | tf_op jit(solution)/shard_map/ppermute | solution.py:266
  13.1 17.1 %collective-permute-start = (bf16[256,128]{1,0:T(8,128)(2,1)S(1)}, bf16[256,128]{1,0:T(8,128)(2,1)S(1)}, u32[]{:S(2)}, u32[]{:S(2)}) collective-permute-start(bf16[256,128]{1,0:T(8,128)(2,1)S(1)} %dynamic-slice_bitcast_fusion), channel_id=1, source_target_pairs={{0,496},{16,480},{32,464},{48,448},{64,432},{80,416},{96,400},{112... | collective-permute-start | bytes 196616 | tf_op jit(solution)/shard_map/ppermute | solution.py:256
  25.8 12.5 %collective-permute-start.2 = (bf16[256,1024]{1,0:T(8,128)(2,1)}, bf16[256,1024]{1,0:T(8,128)(2,1)S(1)}, u32[]{:S(2)}, u32[]{:S(2)}) collective-permute-start(bf16[256,1024]{1,0:T(8,128)(2,1)} %get-tuple-element.28), channel_id=1, source_target_pairs={{0,1},{1,0},{2,3},{3,2},{4,5},{5,4},{6,7},{7,6},{8,9},{9,8},{10,11... | collective-permute-start | bytes 1572872 | tf_op jit(solution)/shard_map/ppermute | solution.py:266
  27.8 10.5 %collective-permute-start.3 = (bf16[256,1024]{1,0:T(8,128)(2,1)}, bf16[256,1024]{1,0:T(8,128)(2,1)}, u32[]{:S(2)}, u32[]{:S(2)}) collective-permute-start(bf16[256,1024]{1,0:T(8,128)(2,1)} %get-tuple-element.27), channel_id=1, source_target_pairs={{0,1},{1,0},{2,3},{3,2},{4,5},{5,4},{6,7},{7,6},{8,9},{9,8},{10,11... | collective-permute-start | bytes 1572872 | tf_op jit(solution)/shard_map/ppermute | solution.py:266
  31.1 16.7 %all-to-all-start.1 = ((bf16[16,128,128]{2,1,0:T(8,128)(2,1)}), bf16[16,128,128]{2,1,0:T(8,128)(2,1)S(1)}, u32[]{:S(2)}, u32[]{:S(2)}) async-start(bf16[16,128,128]{2,1,0:T(8,128)(2,1)} %bitcast.28), calls=%async_computation.1 | async-start | bytes 1048576 | tf_op jit(solution)/shard_map/all_to_all | solution.py:263
  38.3 9.5 %copy-start.5 = (f32[1,2048]{1,0:T(1,128)S(1)}, f32[1,2048]{1,0:T(1,128)}, u32[]{:S(2)}) copy-start(f32[1,2048]{1,0:T(1,128)} %gain.3) | copy-start | bytes 24580
  53.1 0.7 copy-start.2
  53.8 24.9 %all-to-all-start.2 = ((bf16[32,128,128]{2,1,0:T(8,128)(2,1)}), bf16[32,128,128]{2,1,0:T(8,128)(2,1)S(1)}, u32[]{:S(2)}, u32[]{:S(2)}) async-start(bf16[32,128,128]{2,1,0:T(8,128)(2,1)} %bitcast.12), calls=%async_computation.2 | async-start | bytes 2097152 | tf_op jit(solution)/shard_map/all_to_all | solution.py:296
  60.9 1.0 %copy-start.3 = (bf16[128,1536]{1,0:T(8,128)(2,1)S(1)}, bf16[128,1536]{1,0:T(8,128)(2,1)}, u32[]{:S(2)}) copy-start(bf16[128,1536]{1,0:T(8,128)(2,1)} %copy-done.2) | copy-start | bytes 1179652
  62.2 4.6 %copy-start.6 = (bf16[1,256,128]{2,1,0:T(8,128)(2,1)S(1)}, bf16[1,256,128]{2,1,0:T(8,128)(2,1)}, u32[]{:S(2)}) copy-start(bf16[1,256,128]{2,1,0:T(8,128)(2,1)} %param.7) | copy-start | bytes 196612
  62.2 12.7 %collective-permute-start.4 = (bf16[128,2560]{1,0:T(8,128)(2,1)S(1)}, bf16[128,2560]{1,0:T(8,128)(2,1)}, u32[]{:S(2)}, u32[]{:S(2)}) collective-permute-start(bf16[128,2560]{1,0:T(8,128)(2,1)S(1)} %shard_map.111.trade), channel_id=1, source_target_pairs={{0,1},{1,0},{2,3},{3,2},{4,5},{5,4},{6,7},{7,6},{8,9},{9,8},{10,11... | collective-permute-start | bytes 1966088 | tf_op jit(solution)/shard_map/ppermute | solution.py:309
  64.6 10.4 %collective-permute-start.5 = (bf16[128,2048]{1,0:T(8,128)(2,1)S(1)}, bf16[128,2048]{1,0:T(8,128)(2,1)S(1)}, u32[]{:S(2)}, u32[]{:S(2)}) collective-permute-start(bf16[128,2048]{1,0:T(8,128)(2,1)S(1)} %shard_map.112.grads), channel_id=1, source_target_pairs={{0,1},{1,0},{2,3},{3,2},{4,5},{5,4},{6,7},{7,6},{8,9},{9,8},{10,11... | collective-permute-start | bytes 1572872 | tf_op jit(solution)/shard_map/ppermute | solution.py:309
  66.8 16.8 %collective-permute-start.7 = (bf16[256,128]{1,0:T(8,128)(2,1)S(1)}, bf16[256,128]{1,0:T(8,128)(2,1)S(1)}, u32[]{:S(2)}, u32[]{:S(2)}) collective-permute-start(bf16[256,128]{1,0:T(8,128)(2,1)S(1)} %bitcast.34), channel_id=1, source_target_pairs={{0,496},{16,480},{32,464},{48,448},{64,432},{80,416},{96,400},{112... | collective-permute-start | bytes 196616 | tf_op jit(solution)/shard_map/ppermute | solution.py:257
  74.9 1.0 %copy-start.4 = (bf16[128,1536]{1,0:T(8,128)(2,1)S(1)}, bf16[128,1536]{1,0:T(8,128)(2,1)}, u32[]{:S(2)}) copy-start(bf16[128,1536]{1,0:T(8,128)(2,1)} %copy-done.2) | copy-start | bytes 1179652
  78.8 8.3 %collective-permute-start.6 = (bf16[256,128]{1,0:T(8,128)(2,1)S(1)}, bf16[256,128]{1,0:T(8,128)(2,1)S(1)}, u32[]{:S(2)}, u32[]{:S(2)}) collective-permute-start(bf16[256,128]{1,0:T(8,128)(2,1)S(1)} %shard_map.114), channel_id=1, source_target_pairs={{16,32},{32,16},{48,64},{64,48},{80,96},{96,80},{112,128},{128,112... | collective-permute-start | bytes 196616 | tf_op jit(solution)/shard_map/ppermute | solution.py:323
